TPU v7x, 32 devices: a whole 2x2x4 slice. The times are simulated.
32 devices in a mesh: dp: 32 (over z, y, x, core).
Axes of the slice: x: 2, y: 2, z: 4, core: 2. Of those that a mesh axis runs over, the one named last changes fastest.
Arguments:
- tokens: bfloat16 [512, 128, 512], P('dp'), may hold values from -6 to 6
- memory: bfloat16 [512, 32, 512], P(None, 'dp'), may hold values from -6 to 6
- target_lengths: int32 [512], P('dp'), may hold values from 16 to 128, as said below
- memory_lengths: int32 [512], P('dp'), may hold values from 16 to 32, as said below
- grad_output: bfloat16 [512, 128, 512], P('dp'), may hold values from -6 to 6
- gain_self: float32 [512], replicated, may hold values from 0.5 to 1.5
- w_qkv: bfloat16 [512, 1536], replicated, may hold values from -0.25 to 0.25
- w_self_out: bfloat16 [512, 512], replicated, may hold values from -1.5 to 1.5
- gain_cross: float32 [512], replicated, may hold values from 0.5 to 1.5
- w_cross_query: bfloat16 [512, 512], replicated, may hold values from -0.25 to 0.25
- w_cross_kv: bfloat16 [512, 1024], replicated, may hold values from -0.25 to 0.25
- w_cross_out: bfloat16 [512, 512], replicated, may hold values from -1.5 to 1.5
- gain_ffn: float32 [512], replicated, may hold values from 0.5 to 1.5
- w_expand: bfloat16 [512, 2048], replicated, may hold values from -0.25 to 0.25
- w_contract: bfloat16 [2048, 512], replicated, may hold values from -0.125 to 0.125
Outputs:
- output: bfloat16 [512, 128, 512], P('dp')
- grad_tokens: bfloat16 [512, 128, 512], P('dp')
- grad_memory: bfloat16 [512, 32, 512], P(None, 'dp')
- grad_gain_self: float32 [512], replicated
- grad_w_qkv: float32 [512, 1536], replicated
- grad_w_self_out: float32 [512, 512], replicated
- grad_gain_cross: float32 [512], replicated
- grad_w_cross_query: float32 [512, 512], replicated
- grad_w_cross_kv: float32 [512, 1024], replicated
- grad_w_cross_out: float32 [512, 512], replicated
- grad_gain_ffn: float32 [512], replicated
- grad_w_expand: float32 [512, 2048], replicated
- grad_w_contract: float32 [2048, 512], replicated
Inputs may be any that keep to these rules, and one draw needn't show every extreme that they name: `target_lengths`: the 16 sequences of one device lie in one length bucket: from c // 2 to c with c = k * 32 for a k of 1 to 4, and one of them has exactly c tokens; some device has c = 128. `memory_lengths`: among the 16 sequences of each device one has exactly 32 memory tokens.
All inputs are finite; a program needn't handle non-finite values.
Results may differ from a plain program's by a relative error of at most 0.017.
Values may be sent and summed in bfloat16 or wider, within the bound.
No kernel may reach another device: no remote copies, remote signals or barrier semaphores. Data moves between devices by JAX's collectives and lax.ppermute only.
A program may use at most 256 MiB of HBM per device.

v0:
```python
from functools import partial

import jax
import jax.numpy as jnp
from jax import lax
from jax.sharding import PartitionSpec as P

HEAD = 64


epsilon = 1e-05
big_negative = -1e30


def product(left_side, right_side):
    return jnp.dot(left_side, right_side, preferred_element_type=jnp.float32)


def inner_rows(left_side, right_side):
    return lax.dot_general(
        left_side, right_side, (((0,), (0,)), ((), ())), preferred_element_type=jnp.float32
    )


def times_transposed(left_side, right_side):
    return lax.dot_general(
        left_side, right_side, (((1,), (1,)), ((), ())), preferred_element_type=jnp.float32
    )


def norm_forward(hidden, gain_vector):
    centred = hidden - jnp.mean(hidden, axis=-1, keepdims=True)
    spread = lax.rsqrt(jnp.mean(centred * centred, axis=-1, keepdims=True) + epsilon)
    normalized = centred * spread
    return (normalized * gain_vector, normalized, spread)


def norm_backward(gradient, gain_vector, normalized, spread):
    scaled = gradient * gain_vector
    gain_grad = jnp.sum(gradient * normalized, axis=0)
    centred_grad = (
        scaled
        - jnp.mean(scaled, axis=-1, keepdims=True)
        - normalized * jnp.mean(scaled * normalized, axis=-1, keepdims=True)
    )
    return (spread * centred_grad, gain_grad)


def split_heads(matrix, seq_count):
    return matrix.reshape(seq_count, -1, matrix.shape[1] // HEAD, HEAD)


def scores_of(queries, keys, allowed):
    factor = queries.shape[-1] ** (-0.5)
    scores = (
        jnp.einsum("sqhe,skhe->shqk", queries, keys, preferred_element_type=jnp.float32) * factor
    )
    return jnp.where(allowed[:, None], scores, big_negative)


def attend(queries, keys, values, allowed):
    scores = scores_of(queries, keys, allowed)
    row_max = jnp.max(scores, axis=-1, keepdims=True)
    exponentials = jnp.exp(scores - row_max)
    row_total = jnp.sum(exponentials, axis=-1, keepdims=True)
    soft_weights = (exponentials / row_total).astype(jnp.bfloat16)
    result = jnp.einsum("shqk,skhe->sqhe", soft_weights, values, preferred_element_type=jnp.float32)
    return (result, row_max + jnp.log(row_total))


def attend_back(grad_result, queries, keys, values, allowed, log_total):
    factor = queries.shape[-1] ** (-0.5)
    soft_weights = jnp.exp(scores_of(queries, keys, allowed) - log_total)
    grad_values = jnp.einsum(
        "shqk,sqhe->skhe",
        soft_weights.astype(jnp.bfloat16),
        grad_result,
        preferred_element_type=jnp.float32,
    )
    grad_weights = jnp.einsum(
        "sqhe,skhe->shqk", grad_result, values, preferred_element_type=jnp.float32
    )
    grad_scores = soft_weights * (
        grad_weights - jnp.sum(soft_weights * grad_weights, axis=-1, keepdims=True)
    )
    grad_scores = grad_scores.astype(jnp.bfloat16)
    grad_queries = (
        jnp.einsum("shqk,skhe->sqhe", grad_scores, keys, preferred_element_type=jnp.float32)
        * factor
    )
    grad_keys = (
        jnp.einsum("shqk,sqhe->skhe", grad_scores, queries, preferred_element_type=jnp.float32)
        * factor
    )
    return (grad_queries, grad_keys, grad_values)


def local(
    tokens,
    memory,
    target_lengths,
    memory_lengths,
    grad_output,
    gain_self,
    w_qkv,
    w_self_out,
    gain_cross,
    w_cross_query,
    w_cross_kv,
    w_cross_out,
    gain_ffn,
    w_expand,
    w_contract,
):
    seq_count, length, model_width = tokens.shape
    row_count = seq_count * length
    position = jnp.arange(length)
    self_allowed = (position[None, :, None] >= position[None, None, :]) & (
        position[None, None, :] < target_lengths[:, None, None]
    )
    residual = tokens.astype(jnp.float32).reshape(row_count, model_width)
    normed, normal_one, spread_one = norm_forward(residual, gain_self)
    act_one = normed.astype(jnp.bfloat16)
    triple = product(act_one, w_qkv).astype(jnp.bfloat16)
    queries = split_heads(triple[:, :model_width], seq_count)
    keys = split_heads(triple[:, model_width : 2 * model_width], seq_count)
    values = split_heads(triple[:, 2 * model_width :], seq_count)
    attended, log_total_one = attend(queries, keys, values, self_allowed)
    attended_low = attended.astype(jnp.bfloat16).reshape(row_count, model_width)
    residual_two = residual + product(attended_low, w_self_out)
    arrived = lax.all_to_all(memory, "dp", split_axis=0, concat_axis=1, tiled=True)
    mem_total = arrived.shape[1]
    arrived_rows = arrived.reshape(seq_count * mem_total, model_width)
    pairs = product(arrived_rows, w_cross_kv).astype(jnp.bfloat16)
    cross_allowed = jnp.arange(mem_total)[None, None, :] < memory_lengths[:, None, None]
    normed, normal_two, spread_two = norm_forward(residual_two, gain_cross)
    act_two = normed.astype(jnp.bfloat16)
    cross_queries = split_heads(product(act_two, w_cross_query).astype(jnp.bfloat16), seq_count)
    cross_keys = split_heads(pairs[:, :model_width], seq_count)
    cross_values = split_heads(pairs[:, model_width:], seq_count)
    cross_out, log_total_two = attend(cross_queries, cross_keys, cross_values, cross_allowed)
    cross_low = cross_out.astype(jnp.bfloat16).reshape(row_count, model_width)
    residual_three = residual_two + product(cross_low, w_cross_out)
    normed, normal_three, spread_three = norm_forward(residual_three, gain_ffn)
    act_three = normed.astype(jnp.bfloat16)
    expanded = product(act_three, w_expand)
    activated = jax.nn.gelu(expanded, approximate=False).astype(jnp.bfloat16)
    output = (
        (residual_three + product(activated, w_contract)).astype(jnp.bfloat16).reshape(tokens.shape)
    )
    in_sequence = (position[None, :] < target_lengths[:, None]).astype(jnp.float32)
    gradient = (grad_output.astype(jnp.float32) * in_sequence[:, :, None]).reshape(
        row_count, model_width
    )
    grad_low = gradient.astype(jnp.bfloat16)
    grad_contract = inner_rows(activated, grad_low)
    grad_activated = times_transposed(grad_low, w_contract)
    unused_value, gelu_pullback = jax.vjp(partial(jax.nn.gelu, approximate=False), expanded)
    grad_expanded = gelu_pullback(grad_activated)[0].astype(jnp.bfloat16)
    grad_expand = inner_rows(act_three, grad_expanded)
    grad_normed, grad_gain_ffn = norm_backward(
        times_transposed(grad_expanded, w_expand), gain_ffn, normal_three, spread_three
    )
    gradient = gradient + grad_normed
    grad_low = gradient.astype(jnp.bfloat16)
    grad_cross_out = inner_rows(cross_low, grad_low)
    grad_heads = split_heads(
        times_transposed(grad_low, w_cross_out).astype(jnp.bfloat16), seq_count
    )
    grad_q, grad_k, grad_v = attend_back(
        grad_heads, cross_queries, cross_keys, cross_values, cross_allowed, log_total_two
    )
    grad_q_low = grad_q.astype(jnp.bfloat16).reshape(row_count, model_width)
    grad_cross_query = inner_rows(act_two, grad_q_low)
    grad_pairs = jnp.concatenate(
        [
            grad_k.astype(jnp.bfloat16).reshape(seq_count * mem_total, model_width),
            grad_v.astype(jnp.bfloat16).reshape(seq_count * mem_total, model_width),
        ],
        axis=1,
    )
    grad_cross_kv = inner_rows(arrived_rows, grad_pairs)
    grad_arrived = (
        times_transposed(grad_pairs, w_cross_kv)
        .astype(jnp.bfloat16)
        .reshape(seq_count, mem_total, model_width)
    )
    grad_memory = lax.all_to_all(grad_arrived, "dp", split_axis=1, concat_axis=0, tiled=True)
    grad_normed, grad_gain_cross = norm_backward(
        times_transposed(grad_q_low, w_cross_query), gain_cross, normal_two, spread_two
    )
    gradient = gradient + grad_normed
    grad_low = gradient.astype(jnp.bfloat16)
    grad_self_out = inner_rows(attended_low, grad_low)
    grad_heads = split_heads(times_transposed(grad_low, w_self_out).astype(jnp.bfloat16), seq_count)
    grad_q, grad_k, grad_v = attend_back(
        grad_heads, queries, keys, values, self_allowed, log_total_one
    )
    grad_triple = jnp.concatenate(
        [
            grad_q.astype(jnp.bfloat16).reshape(row_count, model_width),
            grad_k.astype(jnp.bfloat16).reshape(row_count, model_width),
            grad_v.astype(jnp.bfloat16).reshape(row_count, model_width),
        ],
        axis=1,
    )
    grad_qkv = inner_rows(act_one, grad_triple)
    grad_normed, grad_gain_self = norm_backward(
        times_transposed(grad_triple, w_qkv), gain_self, normal_one, spread_one
    )
    grad_tokens = (gradient + grad_normed).astype(jnp.bfloat16).reshape(tokens.shape)
    (
        grad_gain_self,
        grad_qkv,
        grad_self_out,
        grad_gain_cross,
        grad_cross_query,
        grad_cross_kv,
        grad_cross_out,
        grad_gain_ffn,
        grad_expand,
        grad_contract,
    ) = lax.psum(
        (
            grad_gain_self,
            grad_qkv,
            grad_self_out,
            grad_gain_cross,
            grad_cross_query,
            grad_cross_kv,
            grad_cross_out,
            grad_gain_ffn,
            grad_expand,
            grad_contract,
        ),
        "dp",
    )
    return (
        output,
        grad_tokens,
        grad_memory,
        grad_gain_self,
        grad_qkv,
        grad_self_out,
        grad_gain_cross,
        grad_cross_query,
        grad_cross_kv,
        grad_cross_out,
        grad_gain_ffn,
        grad_expand,
        grad_contract,
    )


def solution(mesh):
    placed = (
        P("dp", None, None),
        P(None, "dp", None),
        P("dp"),
        P("dp"),
        P("dp", None, None),
        P(),
        P(),
        P(),
        P(),
        P(),
        P(),
        P(),
        P(),
        P(),
        P(),
    )
    return jax.shard_map(
        local,
        mesh=mesh,
        in_specs=placed,
        out_specs=(
            P("dp", None, None),
            P("dp", None, None),
            P(None, "dp", None),
            P(),
            P(),
            P(),
            P(),
            P(),
            P(),
            P(),
            P(),
            P(),
            P(),
        ),
        check_vma=False,
    )
```

profile of v0, /device:TPU:0, one launch (start us, length us, event | category | flops | bytes accessed | tf_op | source)
XLA Modules:
  0.0 634.5 jit_solution(2545732525350405096)
XLA Ops:
  11.0 7.4 %all-to-all-start = ((bf16[32,2,4096]{2,1,0:T(2,128)(2,1)}), bf16[32,2,4096]{2,1,0:T(2,128)(2,1)}, u32[]{:S(2)}, u32[]{:S(2)}) async-start(bf16[32,2,4096]{2,1,0:T(2,128)(2,1)} %reshape.303), calls=%async_computation | async-start | bytes 1048576 | tf_op jit(solution)/shard_map/all_to_all | solution.py:131
  32.4 6.1 reshape.299
  43.6 6.1 reshape.298
  54.8 6.1 reshape.297
  60.9 5.2 copy.128
  82.9 6.1 reshape.300
  89.1 5.4 copy.134
  120.3 43.5 %multiply_convert_fusion = (bf16[2048,2048]{1,0:T(8,128)(2,1)}, f32[2048,2048]{1,0:T(8,128)}, f32[2048,2048]{1,0:T(8,128)}) fusion(bf16[512,2048]{1,0:T(8,128)(2,1)S(1)} %copy-done, f32[2048,512]{1,0:T(8,128)S(1)} %get-tuple-element.102, f32[512]{0:T(512)S(1)} %copy-done.62, f32[2048]{0:T(1024)S(1)} %add_rsqrt_fusion, f32[2048]{0:T(1024)S(1)} %broadcast_multiply_fusion.6), kind=kOutput, calls=%fused_computation.3 | convolution fusion | flops 4571791360 | bytes 48252928 | tf_op jit(solution)/shard_map/dot_general | solution.py:16
  163.9 20.5 %add_convert_fusion = bf16[2048,2048]{1,0:T(8,128)(2,1)} fusion(f32[2048,2048]{1,0:T(8,128)} %get-tuple-element.85, f32[2048,2048]{1,0:T(8,128)} %get-tuple-element.103, bf16[2048,512]{1,0:T(8,128)(2,1)} %bitcast_convert_fusion, bf16[2048,512]{1,0:T(8,128)(2,1)} %param.29), kind=kOutput, calls=%fused_computation.2 | convolution fusion | flops 4353687552 | bytes 46137344 | tf_op jit(solution)/shard_map/dot_general | solution.py:26
  184.4 11.6 %fusion.66 = f32[512,2048]{1,0:T(8,128)} fusion(bf16[2048,2048]{1,0:T(8,128)(2,1)} %add_convert_fusion, f32[2048,512]{1,0:T(8,128)} %copy-done.2, f32[512]{0:T(512)S(1)} %copy-done.62, f32[2048]{0:T(1024)S(1)} %add_rsqrt_fusion, f32[2048]{0:T(1024)S(1)} %broadcast_multiply_fusion.6), kind=kOutput, calls=%fused_computation.146 | convolution fusion | flops 4299161600 | bytes 16795648 | tf_op jit(solution)/shard_map/dot_general | solution.py:20
  196.0 5.7 multiply_reduce_fusion.1
  209.3 6.2 reshape.301
  215.4 5.1 copy.139
  245.0 6.1 reshape.302
  256.3 8.5 %convert_bitcast_fusion = bf16[16,128,8,64]{1,3,2,0:T(8,128)(2,1)} fusion(bf16[16,128,8,64]{1,3,2,0:T(8,128)(2,1)} %copy.144, f32[16,8,128,128]{2,3,1,0:T(8,128)} %copy-done.1, f32[16,8,128]{2,1,0:T(8,128)S(1)} %copy-done.44), kind=kOutput, calls=%fused_computation.86 | convolution fusion | flops 273678336 | bytes 12648448 | tf_op jit(solution)/shard_map/shqk,sqhe->skhe/dot_general | solution.py:74
  264.8 5.8 multiply_reduce_fusion
  279.9 10.2 %fusion.76 = f32[2048,512]{1,0:T(8,128)} fusion(bf16[2048,2048]{1,0:T(8,128)(2,1)} %get-tuple-element.84, bf16[2048,512]{1,0:T(8,128)(2,1)S(1)} %copy-done.36), kind=kOutput, calls=%fused_computation.155 | convolution fusion | flops 4294967296 | bytes 14680064 | tf_op jit(solution)/shard_map/dot_general | solution.py:20
  309.1 5.3 fusion.75
  317.6 5.8 all-to-all-start.1
  323.4 11.2 %fusion.23 = (f32[512]{0:T(512)S(1)}, f32[2048]{0:T(1024)S(1)}, f32[2048]{0:T(1024)S(1)}, f32[2048,512]{1,0:T(8,128)}) fusion(bf16[16,128,512]{2,1,0:T(8,128)(2,1)} %param.15, f32[2048]{0:T(1024)S(1)} %copy-done.57, f32[2048]{0:T(1024)S(1)} %copy-done.55, f32[512]{0:T(512)S(1)} %copy-done.61, bf16[2048,1536]{0,1:T(8,128)(2,1)} %copy-done.49, ...), kind=kOutput, calls=%fused_computation.46 | convolution fusion | flops 3230658048 | bytes 14192640 | tf_op jit(solution)/shard_map/dot_general | solution.py:26
  334.6 9.3 %add_convert_fusion.1 = bf16[2048,512]{1,0:T(8,128)(2,1)} fusion(f32[2048,512]{1,0:T(8,128)S(1)} %copy-done.4, bf16[2048,2048]{1,0:T(8,128)(2,1)} %get-tuple-element.84, bf16[2048,512]{1,0:T(8,128)(2,1)S(1)} %copy-done.67), kind=kOutput, calls=%fused_computation.57 | convolution fusion | flops 4297064448 | bytes 16777216 | tf_op jit(solution)/shard_map/dot_general | solution.py:16
  343.8 42.3 %all-reduce = (f32[512]{0:T(512)}, f32[512]{0:T(512)}, f32[512]{0:T(512)}) all-reduce(f32[512]{0:T(512)S(1)} %get-tuple-element.69, f32[512]{0:T(512)S(1)} %get-tuple-element.67, f32[512]{0:T(512)S(1)} %get-tuple-element.65), channel_id=1, replica_groups=mesh['dp'=32] {'dp'}, use_global_device_ids=true, to_apply=%region_19.20 | all-reduce | flops 1536 | bytes 12288 | tf_op jit(solution)/shard_map/psum | solution.py:223
  386.1 6.0 fusion.22
  392.2 218.9 %all-reduce.4.cloned.1.call-done = (f32[512,1536]{1,0:T(8,128)}, f32[512,512]{1,0:T(8,128)}, f32[512,512]{1,0:T(8,128)}, f32[512,1024]{0,1:T(8,128)}, f32[512,51...) async-done(((f32[512,1536]{1,0:T(8,128)}, f32[512,512]{1,0:T(8,128)}, f32[512,512]{1,0:T(8,128)}, f32[512,1024]{0,1:T(8,128)}, f32[512,512]{1,0:T(8,128)}, ...) | async-done | bytes 16777232 | tf_op jit(solution)/shard_map/psum | solution.py:223
  (243 shorter events, 154.5 us)
Async XLA Ops:
  7.2 113.1 %copy-start = (bf16[512,2048]{1,0:T(8,128)(2,1)S(1)}, bf16[512,2048]{1,0:T(8,128)(2,1)}, u32[]{:S(2)}) copy-start(bf16[512,2048]{1,0:T(8,128)(2,1)} %param.28) | copy-start | bytes 6291460
  7.2 15.9 %copy-start.66 = (s32[16]{0:T(128)S(1)}, s32[16]{0:T(128)}, u32[]{:S(2)}) copy-start(s32[16]{0:T(128)} %param.17) | copy-start | bytes 196
  7.2 16.5 %copy-start.60 = (f32[512]{0:T(512)S(1)}, f32[512]{0:T(512)}, u32[]{:S(2)}) copy-start(f32[512]{0:T(512)} %param.20) | copy-start | bytes 6148
  11.0 88.9 %all-to-all-start = ((bf16[32,2,4096]{2,1,0:T(2,128)(2,1)}), bf16[32,2,4096]{2,1,0:T(2,128)(2,1)}, u32[]{:S(2)}, u32[]{:S(2)}) async-start(bf16[32,2,4096]{2,1,0:T(2,128)(2,1)} %reshape.303), calls=%async_computation | async-start | bytes 1048576 | tf_op jit(solution)/shard_map/all_to_all | solution.py:131
  18.4 592.6 %all-reduce.4.cloned.1.call-start = ((), (), s32[]{:S(2)}) async-start(), calls=%async_computation.2 | async-start | bytes 33554432 | tf_op jit(solution)/shard_map/psum | solution.py:223
  18.5 5.3 copy-start.15
  18.5 7.4 %copy-start.68 = (bf16[512,1536]{1,0:T(8,128)(2,1)S(1)}, bf16[512,1536]{1,0:T(8,128)(2,1)}, u32[]{:S(2)}) copy-start(bf16[512,1536]{1,0:T(8,128)(2,1)} %param.21) | copy-start | bytes 4718596
  119.4 44.4 %copy-start.2 = (f32[2048,512]{1,0:T(8,128)}, f32[2048,512]{1,0:T(8,128)S(1)}, u32[]{:S(2)}) copy-start(f32[2048,512]{1,0:T(8,128)S(1)} %get-tuple-element.102) | copy-start | bytes 12582916
  184.4 11.6 %copy-start.3 = (f32[2048,512]{1,0:T(8,128)S(1)}, f32[2048,512]{1,0:T(8,128)}, u32[]{:S(2)}) copy-start(f32[2048,512]{1,0:T(8,128)} %copy-done.2) | copy-start | bytes 12582916
  184.4 11.6 %copy-start.71 = (bf16[2048,2048]{1,0:T(8,128)(2,1)S(1)}, bf16[2048,2048]{1,0:T(8,128)(2,1)}, u32[]{:S(2)}) copy-start(bf16[2048,2048]{1,0:T(8,128)(2,1)} %add_convert_fusion) | copy-start | bytes 25165828
  196.0 5.7 copy-start.12
  256.3 8.5 %copy-start.21 = (bf16[16,128,8,64]{1,3,2,0:T(8,128)(2,1)S(1)}, bf16[16,128,8,64]{1,3,2,0:T(8,128)(2,1)}, u32[]{:S(2)}) copy-start(bf16[16,128,8,64]{1,3,2,0:T(8,128)(2,1)} %copy.144) | copy-start | bytes 6291460
  256.3 8.5 %copy-start.27 = (bf16[16,128,8,64]{1,3,2,0:T(8,128)(2,1)S(1)}, bf16[16,128,8,64]{1,3,2,0:T(8,128)(2,1)}, u32[]{:S(2)}) copy-start(bf16[16,128,8,64]{1,3,2,0:T(8,128)(2,1)} %copy.128) | copy-start | bytes 6291460
  256.3 14.3 %slice-start = ((s8[8388608]{0:T(1024)(128)(4,1)}), s8[4194304]{0:T(1024)(128)(4,1)S(1)}, s32[]{:S(2)}) async-start(s8[8388608]{0:T(1024)(128)(4,1)} %bitcast.163), calls=%async_computation.3 | async-start | bytes 8388608
  264.8 5.9 slice-start.1
  279.9 10.2 %copy-start.35 = (bf16[16,32,8,64]{3,1,2,0:T(8,128)(2,1)S(1)}, bf16[16,32,8,64]{3,1,2,0:T(8,128)(2,1)}, u32[]{:S(2)}) copy-start(bf16[16,32,8,64]{3,1,2,0:T(8,128)(2,1)} %fusion.50) | copy-start | bytes 1572868
  295.1 5.7 copy-start.28
  314.5 8.9 %copy-start.55 = (f32[2048]{0:T(1024)S(1)}, f32[2048]{0:T(1024)}, u32[]{:S(2)}) copy-start(f32[2048]{0:T(1024)} %copy-done.54) | copy-start | bytes 24580
  314.5 8.9 %copy-start.57 = (f32[2048]{0:T(1024)S(1)}, f32[2048]{0:T(1024)}, u32[]{:S(2)}) copy-start(f32[2048]{0:T(1024)} %copy-done.56) | copy-start | bytes 24580
  314.5 8.9 %copy-start.61 = (f32[512]{0:T(512)S(1)}, f32[512]{0:T(512)}, u32[]{:S(2)}) copy-start(f32[512]{0:T(512)} %param.20) | copy-start | bytes 6148
  317.6 74.6 %all-to-all-start.1 = ((bf16[16,32,512]{2,0,1:T(8,128)(2,1)}), bf16[16,32,512]{2,0,1:T(8,128)(2,1)S(1)}, u32[]{:S(2)}, u32[]{:S(2)}) async-start(bf16[16,32,512]{2,0,1:T(8,128)(2,1)} %copy.159), calls=%async_computation.1 | async-start | bytes 1048576 | tf_op jit(solution)/shard_map/all_to_all | solution.py:188
  323.4 11.2 %copy-start.4 = (f32[2048,512]{1,0:T(8,128)S(1)}, f32[2048,512]{1,0:T(8,128)}, u32[]{:S(2)}) copy-start(f32[2048,512]{1,0:T(8,128)} %copy-done.2) | copy-start | bytes 12582916
  323.4 11.2 %copy-start.67 = (bf16[2048,512]{1,0:T(8,128)(2,1)S(1)}, bf16[2048,512]{1,0:T(8,128)(2,1)}, u32[]{:S(2)}) copy-start(bf16[2048,512]{1,0:T(8,128)(2,1)} %param.29) | copy-start | bytes 6291460
  614.7 5.9 copy-start.46
  (53 other events, 151.0 us)
Sparse Core Ops, SparseCore 0:
  314.6 296.3 all-reduce.3
where the time goes:
time: 643 us; the launch traced here: 634 us
  waiting for transfers between devices  219 us (34%)
  matrix products  188 us (29%)
  local copies, waits for them, and re-layouts  125 us (19%)
  blocking collectives  42.3 us (7%)
  other arithmetic  31.3 us (5%)
  between operations  15.3 us (2%)
  starting transfers between devices  13.2 us (2%)
    psum x1, waiting for transfers between devices, local(): lax.psum((grad_gain_self, grad_qkv, grad_self_out, grad_gain_cross, grad_...  219 us
    reshape x14, local copies, waits for them, and re-layouts, split_heads(): return matrix.reshape(seq_count, -1, matrix.shape[1] // HEAD, HEAD)  71 us
    dot_general x7, matrix products, product(): return jnp.dot(left_side, right_side, preferred_element_type=jnp.float32)  63.8 us
    dot_general x7, matrix products, times_transposed(): lax.dot_general(left_side, right_side, (((1,), (1,)), ((), ())), preferre...  47.7 us
    psum x1, blocking collectives, local(): lax.psum((grad_gain_self, grad_qkv, grad_self_out, grad_gain_cross, grad_...  42.3 us
    dot_general x7, matrix products, inner_rows(): lax.dot_general(left_side, right_side, (((0,), (0,)), ((), ())), preferre...  38.1 us
    unnamed x163, local copies, waits for them, and re-layouts  34.5 us
    dot_general x2, matrix products, attend_back(): jnp.einsum('shqk,sqhe->skhe', soft_weights.astype(jnp.bfloat16), grad_res...  13 us
  transfers between devices with their start and end apart: 3, of which 1 were waited for; matrix products, arithmetic and copies ran while one was open for 17% of the time, Pallas kernels for 0%

commit v1 on v0

v1 whole, which is shorter than its diff:
```python
import functools
import jax
import jax.numpy as jnp
from jax import lax
from jax.experimental import pallas as pl
from jax.experimental.pallas import tpu as pltpu
from jax.sharding import PartitionSpec as P

HEAD = 64
PAIR = 128
epsilon = 1e-05
big_negative = -1e30
f32 = jnp.float32
bf16 = jnp.bfloat16
VMEM_LIMIT = 24
HBM = pltpu.HBM
VMEM = pltpu.VMEM


def dot(left, right, left_dim=1, right_dim=0):
    return lax.dot_general(
        left, right, (((left_dim,), (right_dim,)), ((), ())), preferred_element_type=f32
    )


def normalize(hidden):
    centred = hidden - jnp.mean(hidden, axis=-1, keepdims=True)
    spread = lax.rsqrt(jnp.mean(centred * centred, axis=-1, keepdims=True) + epsilon)
    return centred * spread, spread


def norm_backward(gradient, gain, normalized, spread):
    scaled = gradient * gain
    first = jnp.mean(scaled, axis=-1, keepdims=True)
    second = jnp.mean(scaled * normalized, axis=-1, keepdims=True)
    return spread * (scaled - first - normalized * second)


def head_masks(rows):
    lane = lax.broadcasted_iota(jnp.int32, (rows, PAIR), 1)
    first = jnp.where(lane < HEAD, 1.0, 0.0).astype(bf16)
    second = jnp.where(lane >= HEAD, 1.0, 0.0).astype(bf16)
    return first, second


def spread_pair(block, first, second):
    return jnp.concatenate([block * first, block * second], axis=0)


def stack_pair(block):
    half = block.shape[1] // 2
    return jnp.concatenate([block[:, :half], block[:, half:]], axis=0)


def wide_mask(mem_total, width):
    lane = lax.broadcasted_iota(jnp.int32, (mem_total, width), 1)
    parts = [
        jnp.where((lane >= h * HEAD) & (lane < (h + 1) * HEAD), 1.0, 0.0)
        for h in range(width // HEAD)
    ]
    return parts


PARTS = 1
LAG = 1


def stagger(parts):
    waiting = [LAG * n for n in range(len(parts))]
    while parts:
        left = []
        for n, part in enumerate(parts):
            if waiting[n]:
                waiting[n] -= 1
                left.append(n)
            elif next(part, part) is not part:
                left.append(n)
        parts, waiting = [parts[n] for n in left], [waiting[n] for n in left]


def self_forward_kernel(
    seqs, length, width,
    bits, lengths, tokens, gain_self, w_qkv, w_out, gain_cross, w_query,
    act, triple, weights, attended, mid, queries,
):
    step = pl.program_id(0)
    first, second = head_masks(length)
    key_at = lax.broadcasted_iota(jnp.int32, (length, 2 * length), 0)
    query_at = lax.broadcasted_iota(jnp.int32, (length, 2 * length), 1)
    query_at = jnp.where(query_at >= length, query_at - length, query_at)
    causal = key_at <= query_at
    count = seqs // PARTS

    def part(n):
        span = slice(n * count * length, (n + 1) * count * length)
        residual = tokens[span, :].astype(f32)
        normal, _ = normalize(residual)
        low = (normal * gain_self[...]).astype(bf16)
        yield
        both = dot(low, w_qkv[...]).astype(bf16)
        yield
        heads = [(s, p) for s in range(count) for p in range(width // PAIR)]
        scores = []
        for s, p in heads:
            rows = slice(s * length, (s + 1) * length)
            q = both[rows, p * PAIR : (p + 1) * PAIR] * 0.125
            k = both[rows, width + p * PAIR : width + (p + 1) * PAIR]
            scores.append(dot(k, spread_pair(q, first, second), 1, 1))
        yield
        softs = []
        for (s, p), score in zip(heads, scores):
            allowed = causal & (key_at < lengths[step * seqs + n * count + s])
            score = jnp.where(allowed, score, big_negative)
            raised = jnp.exp(score - jnp.max(score, axis=0, keepdims=True))
            softs.append((raised * (1.0 / jnp.sum(raised, axis=0, keepdims=True))).astype(bf16))
        yield
        joined = {}
        for (s, p), soft in zip(heads, softs):
            rows = slice(s * length, (s + 1) * length)
            v = both[rows, 2 * width + p * PAIR : 2 * width + (p + 1) * PAIR]
            joined[s, p] = dot(stack_pair(soft), spread_pair(v, first, second), 0, 0).astype(bf16)
        yield
        out = jnp.concatenate(
            [
                jnp.concatenate([joined[s, p] for p in range(width // PAIR)], axis=1)
                for s in range(count)
            ],
            axis=0,
        )
        residual = residual + dot(out, w_out[...])
        yield
        normal, _ = normalize(residual)
        after = (normal * gain_cross[...]).astype(bf16)
        yield
        found = dot(after, w_query[...]).astype(bf16)
        yield
        act[span, :] = low
        triple[span, :] = both
        attended[span, :] = out
        mid[span, :] = residual.astype(bf16)
        queries[span, :] = found
        for (s, p), soft in zip(heads, softs):
            weights[n * count + s, p] = soft

    stagger([part(n) for n in range(PARTS)])


def cross_forward_kernel(
    seqs, length, width, mem_total,
    bits, lengths, memory_lengths, raw, queries, mid, grad_output, w_kv, w_out, gain_ffn,
    arrived, pairs, weights, cross, late, grad_low, late_near, grad_low_near, act,
):
    step = pl.program_id(0)
    total = raw.shape[0] // mem_total
    at = lax.broadcasted_iota(jnp.int32, (mem_total, raw.shape[0]), 0) * total
    column = lax.broadcasted_iota(jnp.int32, (mem_total, raw.shape[0]), 1)
    own_rows = jnp.concatenate(
        [jnp.where(column == at + (step * seqs + s), 1.0, 0.0).astype(bf16) for s in range(seqs)],
        axis=0,
    )
    own_rows = dot(own_rows, raw[...]).astype(bf16)
    arrived[...] = own_rows
    both = dot(own_rows, w_kv[...]).astype(bf16)
    pairs[...] = both
    mask = jnp.concatenate(wide_mask(mem_total, width), axis=0).astype(bf16)
    heads = width // HEAD
    key_at = lax.broadcasted_iota(jnp.int32, (mem_total, length), 0)
    row_at = lax.broadcasted_iota(jnp.int32, (length, width), 0)

    def spread(s, at):
        return jnp.concatenate([both[s * mem_total : (s + 1) * mem_total, at]] * heads, axis=0) * mask

    scores = []
    for s in range(seqs):
        q = queries[s * length : (s + 1) * length, :] * 0.125
        scores.append(dot(spread(s, slice(0, width)), q, 1, 1).reshape(heads, mem_total, length))
    softs = []
    for s in range(seqs):
        allowed = (key_at < memory_lengths[step * seqs + s])[None]
        score = jnp.where(allowed, scores[s], big_negative)
        raised = jnp.exp(score - jnp.max(score, axis=1, keepdims=True))
        soft = raised * (1.0 / jnp.sum(raised, axis=1, keepdims=True))
        softs.append(soft.reshape(heads * mem_total, length).astype(bf16))
    joined = [dot(softs[s], spread(s, slice(width, 2 * width)), 0, 0).astype(bf16) for s in range(seqs)]
    low = jnp.concatenate(joined, axis=0)
    cross[...] = low
    for s in range(seqs):
        rows = slice(s * length, (s + 1) * length)
        weights[s] = softs[s]
        live = row_at < lengths[step * seqs + s]
        masked = jnp.where(live, grad_output[rows, :].astype(f32), 0.0).astype(bf16)
        grad_low[rows, :] = masked
        grad_low_near[rows, :] = masked
    residual = mid[...].astype(f32) + dot(low, w_out[...])
    late[...] = residual.astype(bf16)
    late_near[...] = residual.astype(bf16)
    normal, _ = normalize(residual)
    act[...] = (normal * gain_ffn[...]).astype(bf16)


def gelu_parts(value):
    half = 0.5 + 0.5 * lax.erf(value * 0.7071067811865476)
    bell = value * jnp.exp2(value * value * (-0.5 * 1.4426950408889634))
    return value * half, half + 0.3989422804014327 * bell


def ffn_kernel(
    row_block,
    bits, act, grad_low, start, w_expand, w_contract,
    result, grad_normed, send, keep,
    activated, grad_expanded, total, change,
):
    step = pl.program_id(0)
    rows = act.shape[0]
    chunk = w_expand.shape[1]

    @pl.when(step == 0)
    def _():
        total[...] = start[...].astype(f32)
        change[...] = jnp.zeros_like(change)

    for b in range(rows // row_block):
        r = slice(b * row_block, (b + 1) * row_block)
        expanded = dot(act[r, :], w_expand[...])
        grad_activated = dot(grad_low[r, :], w_contract[...], 1, 1)
        value, slope = gelu_parts(expanded)
        value = value.astype(bf16)
        slope = (grad_activated * slope).astype(bf16)
        activated[r, :] = value
        grad_expanded[r, :] = slope
        total[r, :] += dot(value, w_contract[...])
        change[r, :] += dot(slope, w_expand[...], 1, 1)

    def fill(grads):
        grads[:chunk, :] = dot(activated[...], grad_low[...], 0, 0).astype(bf16)
        grads[chunk:, :] = dot(act[...], grad_expanded[...], 0, 0).astype(bf16)

    @pl.when(step < pl.num_programs(0) // 2)
    def _():
        fill(send)

    @pl.when(step >= pl.num_programs(0) // 2)
    def _():
        fill(keep)

    @pl.when(step == pl.num_programs(0) - 1)
    def _():
        result[...] = total[...].astype(bf16)
        grad_normed[...] = change[...].astype(bf16)


def give_halves(core, total, send, keep, height):
    half = height // 2
    for n in range(total.shape[0] // height):
        at = pl.ds(pl.multiple_of(n * height + (1 - core) * half, half), half)
        send[n * half : (n + 1) * half, :] = total[at, :].astype(bf16)
        at = pl.ds(pl.multiple_of(n * height + core * half, half), half)
        keep[n * half : (n + 1) * half, :] = total[at, :].astype(bf16)


def cross_backward_kernel(
    seqs, length, width, mem_total,
    bits, grad_normed, late, grad_low, cross, weights, pairs, queries, mid, arrived, attended,
    w_out, w_query, w_kv, gain_ffn, gain_cross,
    gradient, grad_arrived, send, keep,
    total, grad_rows,
):
    step = pl.program_id(0)

    @pl.when(step == 0)
    def _():
        total[...] = jnp.zeros_like(total)

    normal, spread = normalize(late[...].astype(f32))
    change = norm_backward(
        grad_normed[...].astype(f32), gain_ffn[...], normal, spread
    )
    running = grad_low[...].astype(f32) + change
    low = running.astype(bf16)
    total[:width, :] += dot(cross[...], low, 0, 0)
    grad_cross = dot(low, w_out[...], 1, 1).astype(bf16)
    masks = wide_mask(mem_total, width)
    mask = jnp.concatenate(masks, axis=0).astype(bf16)
    heads = width // HEAD

    def widen(s, at):
        return jnp.concatenate([pairs[s * mem_total : (s + 1) * mem_total, at]] * heads, axis=0) * mask

    def narrow(block):
        return sum(block[h * mem_total : (h + 1) * mem_total, :] * masks[h] for h in range(heads))

    softs = [weights[s] for s in range(seqs)]
    grads = [grad_cross[s * length : (s + 1) * length, :] for s in range(seqs)]
    values = [dot(softs[s], grads[s]) for s in range(seqs)]
    changes = [
        dot(widen(s, slice(width, 2 * width)), grads[s], 1, 1).reshape(heads, mem_total, length)
        for s in range(seqs)
    ]
    scores = []
    for s in range(seqs):
        soft = softs[s].astype(f32).reshape(heads, mem_total, length)
        product = soft * changes[s]
        score = product - soft * jnp.sum(product, axis=1, keepdims=True)
        scores.append(score.reshape(heads * mem_total, length).astype(bf16))
    low_q = [
        (dot(scores[s], widen(s, slice(0, width)), 0, 0) * 0.125).astype(bf16) for s in range(seqs)
    ]
    keys = [dot(scores[s], queries[s * length : (s + 1) * length, :]) for s in range(seqs)]
    low_q = jnp.concatenate(low_q, axis=0)
    low_pairs = jnp.concatenate(
        [
            jnp.concatenate(
                [(narrow(keys[s]) * 0.125).astype(bf16), narrow(values[s]).astype(bf16)], axis=1
            )
            for s in range(seqs)
        ],
        axis=0,
    )
    at = pl.ds(pl.multiple_of(step * seqs * mem_total, seqs * mem_total), seqs * mem_total)
    grad_rows[at, :] = dot(low_pairs, w_kv[...], 1, 1).astype(bf16)
    normal, spread = normalize(mid[...].astype(f32))
    act = (normal * gain_cross[...]).astype(bf16)
    total[width : 2 * width, :] += dot(act, low_q, 0, 0)
    total[2 * width : 3 * width, :] += dot(arrived[...], low_pairs[:, :width], 0, 0)
    total[3 * width : 4 * width, :] += dot(arrived[...], low_pairs[:, width:], 0, 0)
    change = norm_backward(
        dot(low_q, w_query[...], 1, 1), gain_cross[...], normal, spread
    )
    running = running + change
    gradient[...] = running.astype(bf16)
    total[4 * width :, :] += dot(attended[...], running.astype(bf16), 0, 0)

    @pl.when(step == pl.num_programs(0) - 1)
    def _():
        give_halves(bits[0], total, send, keep, width)
        rows = grad_rows.shape[0]
        block = min(rows, 512)
        count = rows // mem_total
        for start in range(0, rows, block):
            row = lax.broadcasted_iota(jnp.int32, (block, rows), 0) + start
            column = lax.broadcasted_iota(jnp.int32, (block, rows), 1)
            shift = count.bit_length() - 1
            source = (row & (count - 1)) * mem_total + (row >> shift)
            order = jnp.where(column == source, 1.0, 0.0).astype(bf16)
            grad_arrived[start : start + block, :] = dot(order, grad_rows[...]).astype(bf16)


def self_backward_kernel(
    seqs, length, width,
    bits, gradient, triple, weights, act, w_out,
    grad_triple, send, keep,
    total,
):
    step = pl.program_id(0)

    @pl.when(step == 0)
    def _():
        total[...] = jnp.zeros_like(total)

    low = dot(gradient[...], w_out[...], 1, 1).astype(bf16)
    first, second = head_masks(length)
    heads = [(s, p) for s in range(seqs) for p in range(width // PAIR)]
    for start in range(0, len(heads), GROUP):
        group = []
        for s, p in heads[start : start + GROUP]:
            rows = slice(s * length, (s + 1) * length)
            group.append((s, p, rows, [slice(j * width + p * PAIR, j * width + (p + 1) * PAIR) for j in range(3)]))
        grads = [spread_pair(low[rows, at[0]], first, second) for s, p, rows, at in group]
        softs = [weights[s, p] for s, p, rows, at in group]
        changes = [dot(triple[rows, at[2]], grad, 1, 1) for (s, p, rows, at), grad in zip(group, grads)]
        values = [dot(soft, grad).astype(bf16) for soft, grad in zip(softs, grads)]
        scores = []
        for soft, change in zip(softs, changes):
            soft = soft.astype(f32)
            product = soft * change
            scores.append((product - soft * jnp.sum(product, axis=0, keepdims=True)).astype(bf16))
        keys = [
            dot(score, spread_pair(triple[rows, at[0]] * 0.125, first, second)).astype(bf16)
            for (s, p, rows, at), score in zip(group, scores)
        ]
        queries = [
            (dot(stack_pair(score), spread_pair(triple[rows, at[1]], first, second), 0, 0) * 0.125).astype(bf16)
            for (s, p, rows, at), score in zip(group, scores)
        ]
        for n, (s, p, rows, at) in enumerate(group):
            grad_triple[rows, at[0]] = queries[n]
            grad_triple[rows, at[1]] = keys[n]
            grad_triple[rows, at[2]] = values[n]
    for j in range(3):
        total[j * width : (j + 1) * width, :] += dot(
            act[...], grad_triple[:, j * width : (j + 1) * width], 0, 0
        )

    @pl.when(step == pl.num_programs(0) - 1)
    def _():
        give_halves(bits[0], total, send, keep, width)


def grad_tokens_kernel(bits, gradient, grad_triple, tokens, w_qkv, gain_self, grad_tokens):
    normal, spread = normalize(tokens[...].astype(f32))
    change = norm_backward(dot(grad_triple[...], w_qkv[...], 1, 1), gain_self[...], normal, spread)
    grad_tokens[...] = (gradient[...].astype(f32) + change).astype(bf16)


def row_sums(weight, grad, gain):
    product = weight.astype(f32) * grad
    columns = sum(product[:, n : n + PAIR] for n in range(0, product.shape[1], PAIR))
    return jnp.sum(columns.T, axis=0, keepdims=True) / gain


def pick(core, own, got, fill):
    mine = pl.program_id(0) == core

    @pl.when(mine)
    def _():
        fill(own)

    @pl.when(jnp.logical_not(mine))
    def _():
        fill(got)


def ffn_final_kernel(bits, own, got, w_expand, gain, contract, expand, gain_grad):
    step = pl.program_id(0)
    chunk = expand.shape[1]

    def fill(source):
        contract[...] = source[:chunk, :].astype(f32)
        grad = source[chunk:, :].astype(f32)
        expand[...] = grad
        sums = row_sums(w_expand[...], grad, gain[...])

        @pl.when(step == 0)
        def _():
            gain_grad[...] = sums

        @pl.when(step > 0)
        def _():
            gain_grad[...] += sums

    mine = (step >= pl.num_programs(0) // 2) == (bits[0] == 1)

    @pl.when(mine)
    def _():
        fill(own)

    @pl.when(jnp.logical_not(mine))
    def _():
        fill(got)


def cross_final_kernel(bits, own, got, w_query, gain, cross_out, query, pair, self_out, gain_grad):
    half, width = query.shape

    def fill(source):
        cross_out[...] = source[:half, :].astype(f32)
        grad = source[half : 2 * half, :].astype(f32)
        query[...] = grad
        pair[:, :width] = source[2 * half : 3 * half, :].astype(f32)
        pair[:, width:] = source[3 * half : 4 * half, :].astype(f32)
        self_out[...] = source[4 * half :, :].astype(f32)
        gain_grad[...] = row_sums(w_query[...], grad, gain[...])

    pick(bits[0], own, got, fill)


def self_final_kernel(bits, own, got, w_qkv, gain, qkv, gain_grad):
    half = qkv.shape[0]
    width = own.shape[1]

    def fill(source):
        for j in range(3):
            qkv[:, j * width : (j + 1) * width] = source[j * half : (j + 1) * half, :].astype(f32)
        gain_grad[...] = row_sums(w_qkv[...], qkv[...], gain[...])

    pick(bits[0], own, got, fill)


def call(kernel, grid, bits, ins, outs, scratch=(), flops=0, deps=(), limit=VMEM_LIMIT):
    moved = sum(a.size * a.dtype.itemsize for a, *_ in ins)
    shapes = []
    for shape, dtype, _, *space in outs:
        size = 1
        for n in shape:
            size *= n
        moved += size * jnp.dtype(dtype).itemsize
        shapes.append(space[0](shape, dtype) if space else jax.ShapeDtypeStruct(shape, dtype))
    count = len(ins)
    arrays = [
        pltpu.with_memory_space_constraint(a, space[0]) if space else a for a, _, *space in ins
    ]

    def body(bits_ref, *refs):
        kernel(bits_ref, *refs[:count], *refs[count + len(deps) :])

    return pl.pallas_call(
        body,
        grid_spec=pltpu.PrefetchScalarGridSpec(
            num_scalar_prefetch=1,
            grid=grid,
            in_specs=[spec for _, spec, *_ in ins] + [pl.BlockSpec(memory_space=pl.ANY)] * len(deps),
            out_specs=[spec for _, _, spec, *_ in outs],
            scratch_shapes=list(scratch),
        ),
        out_shape=shapes,
        compiler_params=pltpu.CompilerParams(vmem_limit_bytes=limit * 1024 * 1024),
        cost_estimate=pl.CostEstimate(flops=flops, bytes_accessed=moved, transcendentals=0),
    )(bits, *arrays, *deps)


def by_step(*shape):
    return pl.BlockSpec(shape, lambda i, bits: (i,) + (0,) * (len(shape) - 1))


def whole(*shape):
    return pl.BlockSpec(shape, lambda i, bits: (0,) * len(shape))


def scalars():
    return pl.BlockSpec(memory_space=pltpu.SMEM)


SEQS = 4
GROUP = 16
MOST = 4


def self_forward(bits, tokens, lengths, gain_self, w_qkv, w_out, gain_cross, w_query, length):
    rows, width = tokens.shape
    n = rows // length
    block = SEQS * length
    row = by_step(block, width)
    return call(
        functools.partial(self_forward_kernel, SEQS, length, width),
        (n // SEQS,), bits,
        [
            (lengths, scalars()), (tokens, row, HBM),
            (gain_self, whole(1, width)), (w_qkv, whole(width, 3 * width), HBM),
            (w_out, whole(width, width), HBM), (gain_cross, whole(1, width)),
            (w_query, whole(width, width), HBM),
        ],
        [
            ((rows, width), bf16, row, HBM),
            ((rows, 3 * width), bf16, by_step(block, 3 * width), HBM),
            ((n, width // PAIR, length, 2 * length), bf16, by_step(SEQS, width // PAIR, length, 2 * length), HBM),
            ((rows, width), bf16, row, HBM),
            ((rows, width), bf16, row, HBM),
            ((rows, width), bf16, row, HBM),
        ],
        flops=12 * rows * width * width,
    )


def cross_forward(bits, lengths, memory_lengths, raw, queries, mid, grad_output, w_kv, w_out, gain_ffn, length, mem_total):
    rows, width = queries.shape
    n = rows // length
    block = SEQS * length
    mem = SEQS * mem_total
    heads = width // HEAD
    row = by_step(block, width)
    return call(
        functools.partial(cross_forward_kernel, SEQS, length, width, mem_total),
        (n // SEQS,), bits,
        [
            (lengths, scalars()), (memory_lengths, scalars()),
            (raw, whole(*raw.shape)), (queries, row, HBM),
            (mid, row, HBM), (grad_output, row, HBM),
            (w_kv, whole(width, 2 * width)), (w_out, whole(width, width)),
            (gain_ffn, whole(1, width)),
        ],
        [
            ((n * mem_total, width), bf16, by_step(mem, width), HBM),
            ((n * mem_total, 2 * width), bf16, by_step(mem, 2 * width), HBM),
            ((n, heads * mem_total, length), bf16, by_step(SEQS, heads * mem_total, length), HBM),
            ((rows, width), bf16, row, HBM),
            ((rows, width), bf16, row, HBM),
            ((rows, width), bf16, row, HBM),
            ((rows, width), bf16, row, VMEM),
            ((rows, width), bf16, row, VMEM),
            ((rows, width), bf16, row, VMEM),
        ],
        flops=6 * rows * width * width,
        limit=VMEM_LIMIT if mem_total <= 32 else 2 * VMEM_LIMIT,
    )


def feed_forward(bits, act, grad_low, start, w_expand, w_contract, chunk=512):
    rows, width = act.shape
    hidden = w_expand.shape[1]
    steps = hidden // chunk
    half = steps // 2

    def at(i, bits):
        return lax.rem(i + half * (1 - bits[0]), steps)

    def block(place):
        return pl.BlockSpec((2 * chunk, width), lambda i, bits: (place(i), 0))

    return call(
        functools.partial(ffn_kernel, min(rows, 512)),
        (steps,), bits,
        [
            (act, whole(rows, width)), (grad_low, whole(rows, width)), (start, whole(rows, width)),
            (w_expand, pl.BlockSpec((width, chunk), lambda i, bits: (0, at(i, bits)))),
            (w_contract, pl.BlockSpec((chunk, width), lambda i, bits: (at(i, bits), 0))),
        ],
        [
            ((rows, width), bf16, whole(rows, width), HBM),
            ((rows, width), bf16, whole(rows, width), HBM),
            ((hidden, width), bf16, block(lambda i: jnp.minimum(i, half - 1)), HBM),
            ((hidden, width), bf16, block(lambda i: jnp.maximum(i - half, 0)), HBM),
        ],
        [
            pltpu.VMEM((rows, chunk), bf16),
            pltpu.VMEM((rows, chunk), bf16),
            pltpu.VMEM((rows, width), f32),
            pltpu.VMEM((rows, width), f32),
        ],
        flops=12 * rows * width * hidden,
    )


def cross_backward(bits, grad_normed, late, grad_low, cross, weights, pairs, queries, mid, arrived, attended, w_out, w_query, w_kv, gain_ffn, gain_cross, length, mem_total, deps=()):
    rows, width = queries.shape
    n = rows // length
    block = SEQS * length
    mem = SEQS * mem_total
    heads = width // HEAD
    row = by_step(block, width)
    return call(
        functools.partial(cross_backward_kernel, SEQS, length, width, mem_total),
        (n // SEQS,), bits,
        [
            (grad_normed, row, HBM), (late, row, HBM), (grad_low, row, HBM), (cross, row, HBM),
            (weights, by_step(SEQS, heads * mem_total, length), HBM),
            (pairs, by_step(mem, 2 * width), HBM), (queries, row, HBM), (mid, row, HBM),
            (arrived, by_step(mem, width), HBM), (attended, row, HBM),
            (w_out, whole(width, width), HBM), (w_query, whole(width, width), HBM),
            (w_kv, whole(width, 2 * width), HBM),
            (gain_ffn, whole(1, width)), (gain_cross, whole(1, width)),
        ],
        [
            ((rows, width), bf16, row, HBM),
            ((n * mem_total, width), bf16, whole(n * mem_total, width), HBM),
            ((5 * width // 2, width), bf16, whole(5 * width // 2, width), HBM),
            ((5 * width // 2, width), bf16, whole(5 * width // 2, width), HBM),
        ],
        [
            pltpu.VMEM((5 * width, width), f32),
            pltpu.VMEM((n * mem_total, width), bf16),
        ],
        flops=14 * rows * width * width,
        deps=deps,
        limit=VMEM_LIMIT if mem_total <= 32 else 2 * VMEM_LIMIT,
    )


def self_backward(bits, gradient, triple, weights, act, w_out, length, deps=()):
    rows, width = gradient.shape
    n = rows // length
    block = SEQS * length
    return call(
        functools.partial(self_backward_kernel, SEQS, length, width),
        (n // SEQS,), bits,
        [
            (gradient, by_step(block, width), HBM), (triple, by_step(block, 3 * width), HBM),
            (weights, by_step(SEQS, width // PAIR, length, 2 * length), HBM),
            (act, by_step(block, width), HBM), (w_out, whole(width, width), HBM),
        ],
        [
            ((rows, 3 * width), bf16, by_step(block, 3 * width), HBM),
            ((3 * width // 2, width), bf16, whole(3 * width // 2, width), HBM),
            ((3 * width // 2, width), bf16, whole(3 * width // 2, width), HBM),
        ],
        [pltpu.VMEM((3 * width, width), f32)],
        flops=14 * rows * width * width,
        deps=deps,
    )


def token_gradient(bits, gradient, grad_triple, tokens, w_qkv, gain_self, deps=()):
    rows, width = tokens.shape
    block = 512
    row = by_step(block, width)
    return call(
        grad_tokens_kernel, (rows // block,), bits,
        [
            (gradient, row, HBM), (grad_triple, by_step(block, 3 * width), HBM), (tokens, row, HBM),
            (w_qkv, whole(width, 3 * width), HBM), (gain_self, whole(1, width)),
        ],
        [((rows, width), bf16, row)],
        flops=6 * rows * width * width,
        deps=deps,
    )[0]


def after(arrays, deps):
    if not deps:
        return arrays
    return lax.optimization_barrier((*arrays, *deps))[: len(arrays)]


def added(left, right):
    return (left.astype(f32) + right.astype(f32)).astype(bf16)


def split_sum(mine, keep, got):
    half = keep.shape[0] // 2

    def part(which):
        return added(
            lax.dynamic_slice_in_dim(keep, which * half, half),
            lax.dynamic_slice_in_dim(got, which * half, half),
        )

    return part(1 - mine), part(mine)


def join(mine, own, got):
    return jnp.where(mine == 0, jnp.concatenate([own, got]), jnp.concatenate([got, own]))


def exchange(block, bit, devices):
    return lax.ppermute(block, "dp", [(i, i ^ (1 << bit)) for i in range(devices)])


class Lane:
    def __init__(self, bits, devices, order, send, keep, most):
        halvings, rows = 1, keep.shape[0]
        while halvings < min(most, len(order)) and rows % 32 == 0:
            rows //= 2
            halvings += 1
        self.bits, self.devices = bits, devices
        self.own, self.token = keep, send
        self.got = exchange(send, order[0], devices)
        self.todo = [("split", b) for b in order[1:halvings]]
        self.todo += [("whole", b) for b in order[halvings:]]
        back = order[:halvings][::-1]
        self.todo += [("gather", back[0])] + list(zip(back[:-1], back[1:]))

    def advance(self, deps=()):
        if not self.todo:
            return
        kind, bit = self.todo.pop(0)
        own, got = after((self.own, self.got), deps)
        if kind == "split":
            send, self.own = split_sum(self.bits[bit], own, got)
        elif kind in ("whole", "gather"):
            send = self.own = added(own, got)
        else:
            send = self.own = join(self.bits[kind], own, got)
        self.token = send
        self.got = exchange(send, bit, self.devices)


def ffn_final(bits, own, got, w_expand, gain, deps=(), chunk=512):
    width, hidden = w_expand.shape
    steps = hidden // chunk

    def source(mine):
        def at(i, bits):
            first = (bits[0] == 0) == mine
            return (jnp.where(first, jnp.minimum(i, steps // 2 - 1), jnp.maximum(i - steps // 2, 0)), 0)

        return pl.BlockSpec((2 * chunk, width), at)

    return call(
        ffn_final_kernel, (steps,), bits,
        [
            (own, source(True), HBM), (got, source(False), HBM),
            (w_expand, pl.BlockSpec((width, chunk), lambda i, bits: (0, i))),
            (gain, whole(1, width)),
        ],
        [
            ((hidden, width), f32, by_step(chunk, width)),
            ((width, hidden), f32, pl.BlockSpec((width, chunk), lambda i, bits: (0, i))),
            ((1, width), f32, whole(1, width)),
        ],
        deps=deps,
    )


def cross_final(bits, own, got, w_query, gain, deps=()):
    width = w_query.shape[0]
    half = width // 2
    part = by_step(half, width)
    column = pl.BlockSpec((1, half), lambda i, bits: (0, i))
    return call(
        cross_final_kernel, (2,), bits,
        [
            (own, whole(*own.shape), HBM), (got, whole(*own.shape), HBM), (w_query, part), (gain, column),
        ],
        [
            ((width, width), f32, part), ((width, width), f32, part),
            ((width, 2 * width), f32, by_step(half, 2 * width)), ((width, width), f32, part),
            ((1, width), f32, column),
        ],
        deps=deps,
    )


def self_final(bits, own, got, w_qkv, gain, deps=()):
    width = w_qkv.shape[0]
    half = width // 2
    column = pl.BlockSpec((1, half), lambda i, bits: (0, i))
    return call(
        self_final_kernel, (2,), bits,
        [
            (own, whole(*own.shape), HBM), (got, whole(*own.shape), HBM),
            (w_qkv, by_step(half, 3 * width)), (gain, column),
        ],
        [((width, 3 * width), f32, by_step(half, 3 * width)), ((1, width), f32, column)],
        deps=deps,
    )


def local(
    devices, tokens, memory, target_lengths, memory_lengths, grad_output,
    gain_self, w_qkv, w_self_out, gain_cross, w_cross_query, w_cross_kv, w_cross_out,
    gain_ffn, w_expand, w_contract,
):
    seq_count, length, width = tokens.shape
    rows = seq_count * length
    gain_self, gain_cross, gain_ffn = gain_self[None], gain_cross[None], gain_ffn[None]
    flat_tokens = tokens.reshape(rows, width)
    order = tuple(range(devices.bit_length() - 1))
    turned = order[:1] + order[2:3] + order[1:2] + order[3:]
    me = lax.axis_index("dp")
    mine = [(me >> b) & 1 for b in order]
    bits = jnp.stack(mine).astype(jnp.int32)
    raw = lax.all_to_all(
        memory.reshape(devices, -1, width), "dp", split_axis=0, concat_axis=0, tiled=True
    ).reshape(-1, width)
    mem_total = raw.shape[0] // seq_count
    act_one, triple, self_weights, attended, mid, queries = self_forward(
        bits, flat_tokens, target_lengths, gain_self, w_qkv, w_self_out, gain_cross, w_cross_query, length
    )
    arrived, pairs, cross_weights, cross, late, grad_low, late_near, grad_low_near, act = cross_forward(
        bits, target_lengths, memory_lengths, raw, queries, mid, grad_output.reshape(rows, width),
        w_cross_kv, w_cross_out, gain_ffn, length, mem_total,
    )
    output, grad_normed, send, keep = feed_forward(
        bits, act, grad_low_near, late_near, w_expand, w_contract
    )
    ffn = Lane(mine, devices, order, send, keep, MOST)
    ffn.advance()
    gradient, grad_arrived, send, keep = cross_backward(
        bits, grad_normed, late, grad_low, cross, cross_weights, pairs, queries, mid, arrived,
        attended, w_cross_out, w_cross_query, w_cross_kv, gain_ffn, gain_cross, length, mem_total,
        deps=[ffn.token],
    )
    ffn.advance([send])
    crossed = Lane(mine, devices, order, after((send,), [ffn.token])[0], keep, MOST)
    crossed.advance()
    grad_triple, send, keep = self_backward(
        bits, gradient, triple, self_weights, act_one, w_self_out, length, deps=[ffn.token, crossed.token]
    )
    ffn.advance([send])
    crossed.advance([ffn.token])
    selfs = Lane(mine, devices, turned, after((send,), [crossed.token])[0], keep, MOST)
    selfs.advance()
    grad_memory = lax.all_to_all(
        after((grad_arrived,), [selfs.token])[0].reshape(devices, -1, width),
        "dp", split_axis=0, concat_axis=0, tiled=True,
    ).reshape(memory.shape)
    grad_tokens = token_gradient(
        bits, gradient, grad_triple, flat_tokens, w_qkv, gain_self,
        deps=[ffn.token, crossed.token, selfs.token],
    )
    deps = [grad_tokens, grad_memory]
    while selfs.todo or crossed.todo or ffn.todo:
        for lane in (ffn, crossed, selfs):
            lane.advance(deps)
            deps = [lane.token]
    grad_contract, grad_expand, grad_gain_ffn = ffn_final(bits, ffn.own, ffn.got, w_expand, gain_ffn)
    grad_cross_out, grad_cross_query, grad_cross_kv, grad_self_out, grad_gain_cross = cross_final(
        bits, crossed.own, crossed.got, w_cross_query, gain_cross
    )
    grad_qkv, grad_gain_self = self_final(bits, selfs.own, selfs.got, w_qkv, gain_self)
    return (
        output.reshape(tokens.shape),
        grad_tokens.reshape(tokens.shape),
        grad_memory,
        grad_gain_self[0],
        grad_qkv,
        grad_self_out,
        grad_gain_cross[0],
        grad_cross_query,
        grad_cross_kv,
        grad_cross_out,
        grad_gain_ffn[0],
        grad_expand,
        grad_contract,
    )


def solution(mesh):
    rows, columns, copied = P("dp", None, None), P(None, "dp", None), P()
    return jax.shard_map(
        functools.partial(local, mesh.shape["dp"]),
        mesh=mesh,
        in_specs=(rows, columns, P("dp"), P("dp"), rows) + (copied,) * 10,
        out_specs=(rows, rows, columns) + (copied,) * 10,
        check_vma=False,
    )
```

time: 643 us -> 283 us (0.44); the launches traced: 634 us -> 282 us
  matrix products: 188 us -> 0 us
  waiting for transfers between devices: 219 us -> 79.7 us
  Pallas kernels: 0 us -> 129 us
  local copies, waits for them, and re-layouts: 125 us -> 9.4 us
  blocking collectives: 42.3 us -> 0 us
  starting transfers between devices: 13.2 us -> 39.1 us
  between operations: 15.3 us -> 0.97 us
  other arithmetic: 31.3 us -> 23.9 us
    psum x1 -> x0, waiting for transfers between devices: 219 us -> none  [local(): lax.psum((grad_gain_self, grad_qkv, grad_self_out, grad_gain_cross, grad_...]
    dot_general x33 -> x0, matrix products: 188 us -> none  [the longest x7 63.8 us: product(): return jnp.dot(left_side, right_side, preferred_element_type=jnp.float32)]
    pallas_call x0 -> x9, Pallas kernels: none -> 129 us  [call(): pl.pallas_call(body, grid_spec=pltpu.PrefetchScalarGridSpec(num_scalar_pr...]
    ppermute x0 -> x27, waiting for transfers between devices: none -> 79.7 us  [exchange(): lax.ppermute(block, 'dp', [(i, i ^ 1 << bit) for i in range(devices)])]
    reshape x17 -> x0, local copies, waits for them, and re-layouts: 74.9 us -> none  [the longest x14 71 us: split_heads(): return matrix.reshape(seq_count, -1, matrix.shape[1] // HEAD, HEAD)]
    psum x1 -> x0, blocking collectives: 42.3 us -> none  [local(): lax.psum((grad_gain_self, grad_qkv, grad_self_out, grad_gain_cross, grad_...]
    ppermute x0 -> x27, starting transfers between devices: none -> 25.9 us  [exchange(): lax.ppermute(block, 'dp', [(i, i ^ 1 << bit) for i in range(devices)])]
    unnamed x163 -> x45, local copies, waits for them, and re-layouts: 34.5 us -> 9.31 us
  transfers between devices with their start and end apart: 3 -> 29, of which waited for: 1 -> 16; matrix products, arithmetic and copies ran while one was open for 17% -> 4% of each run, Pallas kernels for 0% -> 27%
where the time goes in v1:
time: 283 us; the launch traced here: 282 us
  Pallas kernels  129 us (46%)
  waiting for transfers between devices  79.7 us (28%)
  starting transfers between devices  39.1 us (14%)
  other arithmetic  23.9 us (8%)
  local copies, waits for them, and re-layouts  9.4 us (3%)
    pallas_call x9, Pallas kernels, call(): pl.pallas_call(body, grid_spec=pltpu.PrefetchScalarGridSpec(num_scalar_pr...  129 us
    ppermute x27, waiting for transfers between devices, exchange(): lax.ppermute(block, 'dp', [(i, i ^ 1 << bit) for i in range(devices)])  79.7 us
    ppermute x27, starting transfers between devices, exchange(): lax.ppermute(block, 'dp', [(i, i ^ 1 << bit) for i in range(devices)])  25.9 us
    convert_element_type x15, other arithmetic, added(): return (left.astype(f32) + right.astype(f32)).astype(bf16)  16.7 us
    unnamed x45, local copies, waits for them, and re-layouts  9.31 us
    all_to_all x1, starting transfers between devices, local(): lax.all_to_all(memory.reshape(devices, -1, width), 'dp', split_axis=0, co...  7.3 us
    select_n x9, other arithmetic, join(): jnp.where(mine == 0, jnp.concatenate([own, got]), jnp.concatenate([got, o...  7.14 us
    all_to_all x1, starting transfers between devices, local(): lax.all_to_all(after((grad_arrived,), [selfs.token])[0].reshape(devices,...  5.87 us
  transfers between devices with their start and end apart: 29, of which 16 were waited for; matrix products, arithmetic and copies ran while one was open for 4% of the time, Pallas kernels for 27%

profile of v1, /device:TPU:0, one launch (start us, length us, event | category | flops | bytes accessed | tf_op | source)
XLA Modules:
  0.0 282.0 jit_solution(17507360368586195283)
XLA Ops:
  0.6 7.3 %all-to-all-start = ((bf16[32,16,512]{2,1,0:T(8,128)(2,1)}), bf16[32,16,512]{2,1,0:T(8,128)(2,1)S(1)}, u32[]{:S(2)}, u32[]{:S(2)}) async-start(bf16[32,16,512]{2,1,0:T(8,128)(2,1)} %bitcast.32), calls=%async_computation | async-start | bytes 1048576 | tf_op jit(solution)/shard_map/all_to_all | solution.py:831
  10.1 15.7 %shard_map.246 = (bf16[2048,512]{1,0:T(8,128)(2,1)}, bf16[2048,1536]{1,0:T(8,128)(2,1)}, bf16[16,4,128,256]{3,2,1,0:T(8,128)(2,1)}, bf16[2048,512]{1,0:T(8,128)(...) custom-call(s32[5]{0:T(128)S(1)} %stack.23.bits_ref, s32[16]{0:T(128)S(1)} %copy-done.11, ...), custom_call_target="tpu_custom_call" | custom-call | flops 6442450944 | bytes 23597120 | tf_op jit(solution)/shard_map/pallas_call | solution.py:496
  27.0 10.7 %shard_map.247 = (bf16[512,512]{1,0:T(8,128)(2,1)}, bf16[512,1024]{1,0:T(8,128)(2,1)}, bf16[16,256,128]{2,1,0:T(8,128)(2,1)}, bf16[2048,512]{1,0:T(8,128)(2,1)},...) custom-call(s32[5]{0:T(128)S(1)} %stack.23.bits_ref, ...), custom_call_target="tpu_custom_call" | custom-call | flops 3221225472 | bytes 23595136 | tf_op jit(solution)/shard_map/pallas_call | solution.py:496
  37.7 35.7 %shard_map.248 = (bf16[2048,512]{1,0:T(8,128)(2,1)}, bf16[2048,512]{1,0:T(8,128)(2,1)}, bf16[2048,512]{1,0:T(8,128)(2,1)}, bf16[2048,512]{1,0:T(8,128)(2,1)}) custom-call(s32[5]{0:T(128)S(1)} %stack.23.bits_ref, bf16[2048,512]{1,0:T(8,128)(2,1)S(1)} %get-tuple-element.96.refs_0_, bf16[2048,512]{1,0:T(8,128)(2,1)S(1)} %get-tuple-element.97.refs_1_, ...), custom_call_target="tpu_custom_call" | custom-call | flops 25769803776 | bytes 18874368 | tf_op jit(solution)/shard_map/pallas_call | solution.py:496
  73.7 4.2 %collective-permute-done = bf16[2048,512]{1,0:T(8,128)(2,1)} collective-permute-done((bf16[2048,512]{1,0:T(8,128)(2,1)}, bf16[2048,512]{1,0:T(8,128)(2,1)}, u32[]{:S(2)}, u32[]{:S(2)}) %collective-permute-start) | collective-permute-done | bytes 2097184 | tf_op jit(solution)/shard_map/ppermute | solution.py:724
  77.9 3.7 %add_convert_fusion = (bf16[1024,512]{1,0:T(8,128)(2,1)}, bf16[1024,512]{1,0:T(8,128)(2,1)S(1)}) fusion(bf16[2048,512]{1,0:T(8,128)(2,1)} %collective-permute-done, s32[]{:T(128)S(6)} %select_n.145, bf16[2048,512]{1,0:T(8,128)(2,1)} %get-tuple-element.108, s32[]{:T(128)S(6)} %select_n.144), kind=kLoop, calls=%fused_computation.1 | loop fusion | flops 4194304 | bytes 6291464 | tf_op jit(solution)/shard_map/convert_element_type | solution.py:704
  83.4 24.7 %shard_map.249 = (bf16[2048,512]{1,0:T(8,128)(2,1)}, bf16[512,512]{1,0:T(8,128)(2,1)}, bf16[1280,512]{1,0:T(8,128)(2,1)}, bf16[1280,512]{1,0:T(8,128)(2,1)}) custom-call(s32[5]{0:T(128)S(1)} %stack.23.bits_ref, bf16[2048,512]{1,0:T(8,128)(2,1)} %get-tuple-element.100.refs_0_, bf16[2048,512]{1,0:T(8,128)(2,1)} %get-tuple-element.101.refs_1_, ...), custom_call_target="tpu_custom_call" | custom-call | flops 7516192768 | bytes 24645632 | tf_op jit(solution)/shard_map/pallas_call | solution.py:496
  116.6 16.6 %shard_map.250 = (bf16[2048,1536]{1,0:T(8,128)(2,1)}, bf16[768,512]{1,0:T(8,128)(2,1)}, bf16[768,512]{1,0:T(8,128)(2,1)}) custom-call(s32[5]{0:T(128)S(1)} %stack.23.bits_ref, bf16[2048,512]{1,0:T(8,128)(2,1)} %get-tuple-element.110.refs_0_, bf16[2048,1536]{1,0:T(8,128)(2,1)} %get-tuple-element.111.refs_1_, ...), custom_call_target="tpu_custom_call" | custom-call | flops 7516192768 | bytes 23068672 | tf_op jit(solution)/shard_map/pallas_call | solution.py:496
  140.0 5.9 %all-to-all-start.1 = ((bf16[32,16,512]{2,1,0:T(8,128)(2,1)}), bf16[32,16,512]{2,1,0:T(8,128)(2,1)}, u32[]{:S(2)}, u32[]{:S(2)}) async-start(bf16[32,16,512]{2,1,0:T(8,128)(2,1)} %bitcast.33), calls=%async_computation.1 | async-start | bytes 1048576 | tf_op jit(solution)/shard_map/all_to_all | solution.py:862
  149.4 10.0 %shard_map.251 = bf16[2048,512]{1,0:T(8,128)(2,1)} custom-call(s32[5]{0:T(128)S(1)} %stack.23.bits_ref, bf16[2048,512]{1,0:T(8,128)(2,1)} %get-tuple-element.110.refs_0_, bf16[2048,1536]{1,0:T(8,128)(2,1)} %get-tuple-element.119.refs_1_, bf16[2048,512]{1,0:T(8,128)(2,1)} %bitcast.30, bf16[512,1536]{1,0:T(8,128)(2,1)} %refs_2_.3, f32[1,512]{1,0:T(1,128)S(1)} %bitcast.21, ...), custom_call_target="tpu_custom_call" | custom-call | flops 3221225472 | bytes 14157824 | tf_op jit(solution)/shard_map/pallas_call | solution.py:496
  159.4 3.0 %collective-permute-done.8 = bf16[256,512]{1,0:T(8,128)(2,1)} collective-permute-done((bf16[256,512]{1,0:T(8,128)(2,1)S(1)}, bf16[256,512]{1,0:T(8,128)(2,1)}, u32[]{:S(2)}, u32[]{:S(2)}) %collective-permute-start.8) | collective-permute-done | bytes 262176 | tf_op jit(solution)/shard_map/ppermute | solution.py:724
  172.1 5.9 %collective-permute-done.11 = bf16[256,512]{1,0:T(8,128)(2,1)} collective-permute-done((bf16[256,512]{1,0:T(8,128)(2,1)S(1)}, bf16[256,512]{1,0:T(8,128)(2,1)}, u32[]{:S(2)}, u32[]{:S(2)}) %collective-permute-start.11) | collective-permute-done | bytes 262176 | tf_op jit(solution)/shard_map/ppermute | solution.py:724
  179.2 3.1 %collective-permute-start.13 = (bf16[160,512]{1,0:T(8,128)(2,1)S(1)}, bf16[160,512]{1,0:T(8,128)(2,1)S(1)}, u32[]{:S(2)}, u32[]{:S(2)}) collective-permute-start(bf16[160,512]{1,0:T(8,128)(2,1)S(1)} %add_convert_fusion.17), channel_id=1, source_target_pairs={{0,16},{1,17},{2,18},{3,19},{4,20},{5,21},{6,22},{7,23},{8,24},{9,... | collective-permute-start | bytes 491528 | tf_op jit(solution)/shard_map/ppermute | solution.py:724
  183.0 7.8 %collective-permute-done.14 = bf16[256,512]{1,0:T(8,128)(2,1)S(1)} collective-permute-done((bf16[256,512]{1,0:T(8,128)(2,1)S(1)}, bf16[256,512]{1,0:T(8,128)(2,1)S(1)}, u32[]{:S(2)}, u32[]{:S(2)}) %collective-permute-start.14) | collective-permute-done | bytes 262176 | tf_op jit(solution)/shard_map/ppermute | solution.py:724
  192.8 4.8 %collective-permute-done.12 = bf16[96,512]{1,0:T(8,128)(2,1)S(1)} collective-permute-done((bf16[96,512]{1,0:T(8,128)(2,1)}, bf16[96,512]{1,0:T(8,128)(2,1)S(1)}, u32[]{:S(2)}, u32[]{:S(2)}) %collective-permute-start.12) | collective-permute-done | bytes 98336 | tf_op jit(solution)/shard_map/ppermute | solution.py:724
  197.6 6.5 %collective-permute-done.17 = bf16[512,512]{1,0:T(8,128)(2,1)} collective-permute-done((bf16[512,512]{1,0:T(8,128)(2,1)S(1)}, bf16[512,512]{1,0:T(8,128)(2,1)}, u32[]{:S(2)}, u32[]{:S(2)}) %collective-permute-start.17) | collective-permute-done | bytes 524320 | tf_op jit(solution)/shard_map/ppermute | solution.py:724
  210.4 4.4 %collective-permute-done.16 = bf16[160,512]{1,0:T(8,128)(2,1)} collective-permute-done((bf16[160,512]{1,0:T(8,128)(2,1)S(1)}, bf16[160,512]{1,0:T(8,128)(2,1)}, u32[]{:S(2)}, u32[]{:S(2)}) %collective-permute-start.16) | collective-permute-done | bytes 163872 | tf_op jit(solution)/shard_map/ppermute | solution.py:724
  217.4 12.6 %collective-permute-done.20 = bf16[1024,512]{1,0:T(8,128)(2,1)S(1)} collective-permute-done((bf16[1024,512]{1,0:T(8,128)(2,1)}, bf16[1024,512]{1,0:T(8,128)(2,1)S(1)}, u32[]{:S(2)}, u32[]{:S(2)}) %collective-permute-start.20) | collective-permute-done | bytes 1048608 | tf_op jit(solution)/shard_map/ppermute | solution.py:724
  234.2 5.2 %collective-permute-done.18 = bf16[96,512]{1,0:T(8,128)(2,1)S(1)} collective-permute-done((bf16[96,512]{1,0:T(8,128)(2,1)S(1)}, bf16[96,512]{1,0:T(8,128)(2,1)S(1)}, u32[]{:S(2)}, u32[]{:S(2)}) %collective-permute-start.18) | collective-permute-done | bytes 98336 | tf_op jit(solution)/shard_map/ppermute | solution.py:724
  239.8 8.6 %collective-permute-done.22 = bf16[640,512]{1,0:T(8,128)(2,1)S(1)} collective-permute-done((bf16[640,512]{1,0:T(8,128)(2,1)S(1)}, bf16[640,512]{1,0:T(8,128)(2,1)S(1)}, u32[]{:S(2)}, u32[]{:S(2)}) %collective-permute-start.22) | collective-permute-done | bytes 655392 | tf_op jit(solution)/shard_map/ppermute | solution.py:724
  252.5 6.1 %collective-permute-done.23 = bf16[384,512]{1,0:T(8,128)(2,1)S(1)} collective-permute-done((bf16[384,512]{1,0:T(8,128)(2,1)S(1)}, bf16[384,512]{1,0:T(8,128)(2,1)S(1)}, u32[]{:S(2)}, u32[]{:S(2)}) %collective-permute-start.23) | collective-permute-done | bytes 393248 | tf_op jit(solution)/shard_map/ppermute | solution.py:724
  262.2 3.9 %shard_map.252 = (f32[512,1536]{1,0:T(8,128)}, f32[1,512]{1,0:T(1,128)}) custom-call(s32[5]{0:T(128)S(1)} %stack.23.bits_ref, bf16[768,512]{1,0:T(8,128)(2,1)} %copy-done.16, bf16[768,512]{1,0:T(8,128)(2,1)} %copy-done.21, bf16[512,1536]{1,0:T(8,128)(2,1)S(1)} %copy-done, f32[1,512]{1,0:T(1,128)S(1)} %bitcast.22), custom_call_target="tpu_custom_call" | custom-call | bytes 6295552 | tf_op jit(solution)/shard_map/pallas_call | solution.py:496
  267.1 4.9 %shard_map.253 = (f32[512,512]{1,0:T(8,128)}, f32[512,512]{1,0:T(8,128)}, f32[512,1024]{1,0:T(8,128)}, f32[512,512]{1,0:T(8,128)}, f32[1,512]{1,0:T(1,128)}) custom-call(s32[5]{0:T(128)S(1)} %stack.23.bits_ref, bf16[1280,512]{1,0:T(8,128)(2,1)} %copy-done.14, bf16[1280,512]{1,0:T(8,128)(2,1)} %copy-done.19, bf16[512,512]{1,0:T(8,128)(2,1)S(1)} %copy-done.2, ...), custom_call_target="tpu_custom_call" | custom-call | bytes 8392704 | tf_op jit(solution)/shard_map/pallas_call | solution.py:496
  273.3 6.8 %shard_map.254 = (f32[2048,512]{1,0:T(8,128)}, f32[512,2048]{1,0:T(8,128)}, f32[1,512]{1,0:T(1,128)}) custom-call(s32[5]{0:T(128)S(1)} %stack.23.bits_ref, bf16[2048,512]{1,0:T(8,128)(2,1)} %copy-done.13, bf16[2048,512]{1,0:T(8,128)(2,1)} %copy-done.17, bf16[512,2048]{1,0:T(8,128)(2,1)S(1)} %copy-done.1, f32[1,512]{1,0:T(1,128)S(1)} %bitcast.28), custom_call_target="tpu_custom_call" | custom-call | bytes 14684160 | tf_op jit(solution)/shard_map/pallas_call | solution.py:496
  (113 shorter events, 62.8 us)
Async XLA Ops:
  0.6 25.1 %all-to-all-start = ((bf16[32,16,512]{2,1,0:T(8,128)(2,1)}), bf16[32,16,512]{2,1,0:T(8,128)(2,1)S(1)}, u32[]{:S(2)}, u32[]{:S(2)}) async-start(bf16[32,16,512]{2,1,0:T(8,128)(2,1)} %bitcast.32), calls=%async_computation | async-start | bytes 1048576 | tf_op jit(solution)/shard_map/all_to_all | solution.py:831
  81.7 26.5 %collective-permute-start.1 = (bf16[1024,512]{1,0:T(8,128)(2,1)S(1)}, bf16[1024,512]{1,0:T(8,128)(2,1)}, u32[]{:S(2)}, u32[]{:S(2)}) collective-permute-start(bf16[1024,512]{1,0:T(8,128)(2,1)S(1)} %get-tuple-element.176.refs_15_), channel_id=1, source_target_pairs={{0,2},{1,3},{2,0},{3,1},{4,6},{5,7},{6,4},{7,5},{8,10},{9,11},{10,... | collective-permute-start | bytes 3145736 | tf_op jit(solution)/shard_map/ppermute | solution.py:724
  110.5 22.7 %collective-permute-start.3 = (bf16[512,512]{1,0:T(8,128)(2,1)S(1)}, bf16[512,512]{1,0:T(8,128)(2,1)S(1)}, u32[]{:S(2)}, u32[]{:S(2)}) collective-permute-start(bf16[512,512]{1,0:T(8,128)(2,1)S(1)} %get-tuple-element.180.refs_5_), channel_id=1, source_target_pairs={{0,4},{1,5},{2,6},{3,7},{4,0},{5,1},{6,2},{7,3},{8,12},{9,13},{10,... | collective-permute-start | bytes 1572872 | tf_op jit(solution)/shard_map/ppermute | solution.py:724
  115.9 18.2 %collective-permute-start.4 = (bf16[640,512]{1,0:T(8,128)(2,1)S(1)}, bf16[640,512]{1,0:T(8,128)(2,1)S(1)}, u32[]{:S(2)}, u32[]{:S(2)}) collective-permute-start(bf16[640,512]{1,0:T(8,128)(2,1)S(1)} %get-tuple-element.178.refs_6_), channel_id=1, source_target_pairs={{0,2},{1,3},{2,0},{3,1},{4,6},{5,7},{6,4},{7,5},{8,10},{9,11},{10,... | collective-permute-start | bytes 1966088 | tf_op jit(solution)/shard_map/ppermute | solution.py:724
  140.0 22.5 %all-to-all-start.1 = ((bf16[32,16,512]{2,1,0:T(8,128)(2,1)}), bf16[32,16,512]{2,1,0:T(8,128)(2,1)}, u32[]{:S(2)}, u32[]{:S(2)}) async-start(bf16[32,16,512]{2,1,0:T(8,128)(2,1)} %bitcast.33), calls=%async_computation.1 | async-start | bytes 1048576 | tf_op jit(solution)/shard_map/all_to_all | solution.py:862
  145.8 16.6 %collective-permute-start.8 = (bf16[256,512]{1,0:T(8,128)(2,1)S(1)}, bf16[256,512]{1,0:T(8,128)(2,1)}, u32[]{:S(2)}, u32[]{:S(2)}) collective-permute-start(bf16[256,512]{1,0:T(8,128)(2,1)S(1)} %get-tuple-element.186.refs_5_), channel_id=1, source_target_pairs={{0,8},{1,9},{2,10},{3,11},{4,12},{5,13},{6,14},{7,15},{8,0},{9,1},... | collective-permute-start | bytes 786440 | tf_op jit(solution)/shard_map/ppermute | solution.py:724
  147.4 18.7 %collective-permute-start.7 = (bf16[320,512]{1,0:T(8,128)(2,1)S(1)}, bf16[320,512]{1,0:T(8,128)(2,1)}, u32[]{:S(2)}, u32[]{:S(2)}) collective-permute-start(bf16[320,512]{1,0:T(8,128)(2,1)S(1)} %get-tuple-element.184.refs_6_), channel_id=1, source_target_pairs={{0,4},{1,5},{2,6},{3,7},{4,0},{5,1},{6,2},{7,3},{8,12},{9,13},{10,... | collective-permute-start | bytes 983048 | tf_op jit(solution)/shard_map/ppermute | solution.py:724
  148.8 21.0 %collective-permute-start.6 = (bf16[384,512]{1,0:T(8,128)(2,1)S(1)}, bf16[384,512]{1,0:T(8,128)(2,1)}, u32[]{:S(2)}, u32[]{:S(2)}) collective-permute-start(bf16[384,512]{1,0:T(8,128)(2,1)S(1)} %get-tuple-element.182.refs_7_), channel_id=1, source_target_pairs={{0,4},{1,5},{2,6},{3,7},{4,0},{5,1},{6,2},{7,3},{8,12},{9,13},{10,... | collective-permute-start | bytes 1179656 | tf_op jit(solution)/shard_map/ppermute | solution.py:724
  163.6 14.4 %collective-permute-start.11 = (bf16[256,512]{1,0:T(8,128)(2,1)S(1)}, bf16[256,512]{1,0:T(8,128)(2,1)}, u32[]{:S(2)}, u32[]{:S(2)}) collective-permute-start(bf16[256,512]{1,0:T(8,128)(2,1)S(1)} %add_convert_fusion.11), channel_id=1, source_target_pairs={{0,16},{1,17},{2,18},{3,19},{4,20},{5,21},{6,22},{7,23},{8,24},{9,... | collective-permute-start | bytes 786440 | tf_op jit(solution)/shard_map/ppermute | solution.py:724
  167.3 11.8 %collective-permute-start.10 = (bf16[160,512]{1,0:T(8,128)(2,1)S(1)}, bf16[160,512]{1,0:T(8,128)(2,1)S(1)}, u32[]{:S(2)}, u32[]{:S(2)}) collective-permute-start(bf16[160,512]{1,0:T(8,128)(2,1)S(1)} %get-tuple-element.190), channel_id=1, source_target_pairs={{0,8},{1,9},{2,10},{3,11},{4,12},{5,13},{6,14},{7,15},{8,0},{9,1},... | collective-permute-start | bytes 491528 | tf_op jit(solution)/shard_map/ppermute | solution.py:724
  171.0 11.3 %collective-permute-start.9 = (bf16[192,512]{1,0:T(8,128)(2,1)S(1)}, bf16[192,512]{1,0:T(8,128)(2,1)S(1)}, u32[]{:S(2)}, u32[]{:S(2)}) collective-permute-start(bf16[192,512]{1,0:T(8,128)(2,1)S(1)} %get-tuple-element.187), channel_id=1, source_target_pairs={{0,2},{1,3},{2,0},{3,1},{4,6},{5,7},{6,4},{7,5},{8,10},{9,11},{10,... | collective-permute-start | bytes 589832 | tf_op jit(solution)/shard_map/ppermute | solution.py:724
  179.0 11.7 %collective-permute-start.14 = (bf16[256,512]{1,0:T(8,128)(2,1)S(1)}, bf16[256,512]{1,0:T(8,128)(2,1)S(1)}, u32[]{:S(2)}, u32[]{:S(2)}) collective-permute-start(bf16[256,512]{1,0:T(8,128)(2,1)S(1)} %add_convert_fusion.10), channel_id=1, source_target_pairs={{0,8},{1,9},{2,10},{3,11},{4,12},{5,13},{6,14},{7,15},{8,0},{9,1},... | collective-permute-start | bytes 786440 | tf_op jit(solution)/shard_map/ppermute | solution.py:724
  179.2 13.6 %collective-permute-start.13 = (bf16[160,512]{1,0:T(8,128)(2,1)S(1)}, bf16[160,512]{1,0:T(8,128)(2,1)S(1)}, u32[]{:S(2)}, u32[]{:S(2)}) collective-permute-start(bf16[160,512]{1,0:T(8,128)(2,1)S(1)} %add_convert_fusion.17), channel_id=1, source_target_pairs={{0,16},{1,17},{2,18},{3,19},{4,20},{5,21},{6,22},{7,23},{8,24},{9,... | collective-permute-start | bytes 491528 | tf_op jit(solution)/shard_map/ppermute | solution.py:724
  191.0 13.1 %collective-permute-start.17 = (bf16[512,512]{1,0:T(8,128)(2,1)S(1)}, bf16[512,512]{1,0:T(8,128)(2,1)}, u32[]{:S(2)}, u32[]{:S(2)}) collective-permute-start(bf16[512,512]{1,0:T(8,128)(2,1)S(1)} %maximum_select_fusion.5), channel_id=1, source_target_pairs={{0,4},{1,5},{2,6},{3,7},{4,0},{5,1},{6,2},{7,3},{8,12},{9,13},{10,... | collective-permute-start | bytes 1572872 | tf_op jit(solution)/shard_map/ppermute | solution.py:724
  206.6 23.5 %collective-permute-start.20 = (bf16[1024,512]{1,0:T(8,128)(2,1)}, bf16[1024,512]{1,0:T(8,128)(2,1)S(1)}, u32[]{:S(2)}, u32[]{:S(2)}) collective-permute-start(bf16[1024,512]{1,0:T(8,128)(2,1)} %maximum_select_fusion.2), channel_id=1, source_target_pairs={{0,2},{1,3},{2,0},{3,1},{4,6},{5,7},{6,4},{7,5},{8,10},{9,11},{10,... | collective-permute-start | bytes 3145736 | tf_op jit(solution)/shard_map/ppermute | solution.py:724
  208.3 6.5 %collective-permute-start.16 = (bf16[160,512]{1,0:T(8,128)(2,1)S(1)}, bf16[160,512]{1,0:T(8,128)(2,1)}, u32[]{:S(2)}, u32[]{:S(2)}) collective-permute-start(bf16[160,512]{1,0:T(8,128)(2,1)S(1)} %add_convert_fusion.16), channel_id=1, source_target_pairs={{0,8},{1,9},{2,10},{3,11},{4,12},{5,13},{6,14},{7,15},{8,0},{9,1},... | collective-permute-start | bytes 491528 | tf_op jit(solution)/shard_map/ppermute | solution.py:724
  208.3 9.1 %collective-permute-start.15 = (bf16[96,512]{1,0:T(8,128)(2,1)S(1)}, bf16[96,512]{1,0:T(8,128)(2,1)S(1)}, u32[]{:S(2)}, u32[]{:S(2)}) collective-permute-start(bf16[96,512]{1,0:T(8,128)(2,1)S(1)} %add_convert_fusion.21), channel_id=1, source_target_pairs={{0,16},{1,17},{2,18},{3,19},{4,20},{5,21},{6,22},{7,23},{8,24},{9,... | collective-permute-start | bytes 294920 | tf_op jit(solution)/shard_map/ppermute | solution.py:724
  215.9 16.3 %collective-permute-start.19 = (bf16[320,512]{1,0:T(8,128)(2,1)S(1)}, bf16[320,512]{1,0:T(8,128)(2,1)S(1)}, u32[]{:S(2)}, u32[]{:S(2)}) collective-permute-start(bf16[320,512]{1,0:T(8,128)(2,1)S(1)} %maximum_select_fusion.7), channel_id=1, source_target_pairs={{0,4},{1,5},{2,6},{3,7},{4,0},{5,1},{6,2},{7,3},{8,12},{9,13},{10,... | collective-permute-start | bytes 983048 | tf_op jit(solution)/shard_map/ppermute | solution.py:724
  232.4 16.1 %collective-permute-start.22 = (bf16[640,512]{1,0:T(8,128)(2,1)S(1)}, bf16[640,512]{1,0:T(8,128)(2,1)S(1)}, u32[]{:S(2)}, u32[]{:S(2)}) collective-permute-start(bf16[640,512]{1,0:T(8,128)(2,1)S(1)} %maximum_select_fusion.4), channel_id=1, source_target_pairs={{0,2},{1,3},{2,0},{3,1},{4,6},{5,7},{6,4},{7,5},{8,10},{9,11},{10,... | collective-permute-start | bytes 1966088 | tf_op jit(solution)/shard_map/ppermute | solution.py:724
  234.2 37.8 %collective-permute-start.26 = (bf16[2048,512]{1,0:T(8,128)(2,1)S(1)}, bf16[2048,512]{1,0:T(8,128)(2,1)S(1)}, u32[]{:S(2)}, u32[]{:S(2)}) collective-permute-start(bf16[2048,512]{1,0:T(8,128)(2,1)S(1)} %maximum_select_fusion.refs_0_), channel_id=1, source_target_pairs={{0,1},{1,0},{2,3},{3,2},{4,5},{5,4},{6,7},{7,6},{8,9},{9,8},{10,11... | collective-permute-start | bytes 6291464 | tf_op jit(solution)/shard_map/ppermute | solution.py:724
  234.2 5.2 %collective-permute-start.18 = (bf16[96,512]{1,0:T(8,128)(2,1)S(1)}, bf16[96,512]{1,0:T(8,128)(2,1)S(1)}, u32[]{:S(2)}, u32[]{:S(2)}) collective-permute-start(bf16[96,512]{1,0:T(8,128)(2,1)S(1)} %add_convert_fusion.20), channel_id=1, source_target_pairs={{0,8},{1,9},{2,10},{3,11},{4,12},{5,13},{6,14},{7,15},{8,0},{9,1},... | collective-permute-start | bytes 294920 | tf_op jit(solution)/shard_map/ppermute | solution.py:724
  239.4 11.2 %collective-permute-start.21 = (bf16[192,512]{1,0:T(8,128)(2,1)S(1)}, bf16[192,512]{1,0:T(8,128)(2,1)S(1)}, u32[]{:S(2)}, u32[]{:S(2)}) collective-permute-start(bf16[192,512]{1,0:T(8,128)(2,1)S(1)} %maximum_select_fusion.8), channel_id=1, source_target_pairs={{0,2},{1,3},{2,0},{3,1},{4,6},{5,7},{6,4},{7,5},{8,10},{9,11},{10,... | collective-permute-start | bytes 589832 | tf_op jit(solution)/shard_map/ppermute | solution.py:724
  250.7 7.8 %collective-permute-start.23 = (bf16[384,512]{1,0:T(8,128)(2,1)S(1)}, bf16[384,512]{1,0:T(8,128)(2,1)S(1)}, u32[]{:S(2)}, u32[]{:S(2)}) collective-permute-start(bf16[384,512]{1,0:T(8,128)(2,1)S(1)} %maximum_select_fusion.6), channel_id=1, source_target_pairs={{0,4},{1,5},{2,6},{3,7},{4,0},{5,1},{6,2},{7,3},{8,12},{9,13},{10,... | collective-permute-start | bytes 1179656 | tf_op jit(solution)/shard_map/ppermute | solution.py:724
  252.5 13.6 %collective-permute-start.25 = (bf16[1280,512]{1,0:T(8,128)(2,1)S(1)}, bf16[1280,512]{1,0:T(8,128)(2,1)S(1)}, u32[]{:S(2)}, u32[]{:S(2)}) collective-permute-start(bf16[1280,512]{1,0:T(8,128)(2,1)S(1)} %maximum_select_fusion.1.refs_0_), channel_id=1, source_target_pairs={{0,1},{1,0},{2,3},{3,2},{4,5},{5,4},{6,7},{7,6},{8,9},{9,8},{10,11... | collective-permute-start | bytes 3932168 | tf_op jit(solution)/shard_map/ppermute | solution.py:724
  (27 other events, 230.1 us)

commit v2 on v1

--- a/solution.py
+++ b/solution.py
@@ -204,6 +204,14 @@
     return value * half, half + 0.3989422804014327 * bell
 
 
+def place(bits, n, turned=None):
+    first, second = bits[1], bits[2]
+    if turned is not None:
+        first, second = jnp.where(turned, second, first), jnp.where(turned, first, second)
+    mine = first * 4 + second * 2 + bits[3]
+    return jnp.bitwise_xor(mine, 7 - n)
+
+
 def ffn_kernel(
     row_block,
     bits, act, grad_low, start, w_expand, w_contract,
@@ -232,8 +240,12 @@
         change[r, :] += dot(slope, w_expand[...], 1, 1)
 
     def fill(grads):
-        grads[:chunk, :] = dot(activated[...], grad_low[...], 0, 0).astype(bf16)
-        grads[chunk:, :] = dot(act[...], grad_expanded[...], 0, 0).astype(bf16)
+        found = [dot(activated[...], grad_low[...], 0, 0), dot(act[...], grad_expanded[...], 0, 0)]
+        size = chunk // 4
+        turned = lax.rem(step, pl.num_programs(0) // 2) == 1
+        for n in range(8):
+            at = pl.ds(pl.multiple_of(place(bits, n, turned) * size, size), size)
+            grads[at, :] = found[n // 4][n % 4 * size : (n % 4 + 1) * size, :].astype(bf16)
 
     @pl.when(step < pl.num_programs(0) // 2)
     def _():
@@ -249,13 +261,22 @@
         grad_normed[...] = change[...].astype(bf16)
 
 
-def give_halves(core, total, send, keep, height):
-    half = height // 2
-    for n in range(total.shape[0] // height):
-        at = pl.ds(pl.multiple_of(n * height + (1 - core) * half, half), half)
-        send[n * half : (n + 1) * half, :] = total[at, :].astype(bf16)
-        at = pl.ds(pl.multiple_of(n * height + core * half, half), half)
-        keep[n * half : (n + 1) * half, :] = total[at, :].astype(bf16)
+def add_halves(total, n, value):
+    half = value.shape[0] // 2
+    rows = total.shape[0] // 2
+    total[n * half : (n + 1) * half, :] += value[:half]
+    total[rows + n * half : rows + (n + 1) * half, :] += value[half:]
+
+
+def give_halves(bits, total, send, keep, turned):
+    rows = send.shape[0]
+    size = rows // 8
+    for n in range(8):
+        to = pl.ds(pl.multiple_of(place(bits, n, turned) * size, size), size)
+        at = pl.ds(pl.multiple_of((1 - bits[0]) * rows + n * size, size), size)
+        send[to, :] = total[at, :].astype(bf16)
+        at = pl.ds(pl.multiple_of(bits[0] * rows + n * size, size), size)
+        keep[to, :] = total[at, :].astype(bf16)
 
 
 def cross_backward_kernel(
@@ -277,7 +298,7 @@
     )
     running = grad_low[...].astype(f32) + change
     low = running.astype(bf16)
-    total[:width, :] += dot(cross[...], low, 0, 0)
+    add_halves(total, 0, dot(cross[...], low, 0, 0))
     grad_cross = dot(low, w_out[...], 1, 1).astype(bf16)
     masks = wide_mask(mem_total, width)
     mask = jnp.concatenate(masks, axis=0).astype(bf16)
@@ -320,19 +341,19 @@
     grad_rows[at, :] = dot(low_pairs, w_kv[...], 1, 1).astype(bf16)
     normal, spread = normalize(mid[...].astype(f32))
     act = (normal * gain_cross[...]).astype(bf16)
-    total[width : 2 * width, :] += dot(act, low_q, 0, 0)
-    total[2 * width : 3 * width, :] += dot(arrived[...], low_pairs[:, :width], 0, 0)
-    total[3 * width : 4 * width, :] += dot(arrived[...], low_pairs[:, width:], 0, 0)
+    add_halves(total, 1, dot(act, low_q, 0, 0))
+    add_halves(total, 2, dot(arrived[...], low_pairs[:, :width], 0, 0))
+    add_halves(total, 3, dot(arrived[...], low_pairs[:, width:], 0, 0))
     change = norm_backward(
         dot(low_q, w_query[...], 1, 1), gain_cross[...], normal, spread
     )
     running = running + change
     gradient[...] = running.astype(bf16)
-    total[4 * width :, :] += dot(attended[...], running.astype(bf16), 0, 0)
+    add_halves(total, 4, dot(attended[...], running.astype(bf16), 0, 0))
 
     @pl.when(step == pl.num_programs(0) - 1)
     def _():
-        give_halves(bits[0], total, send, keep, width)
+        give_halves(bits, total, send, keep, TURNED[0])
         rows = grad_rows.shape[0]
         block = min(rows, 512)
         count = rows // mem_total
@@ -387,13 +408,11 @@
             grad_triple[rows, at[1]] = keys[n]
             grad_triple[rows, at[2]] = values[n]
     for j in range(3):
-        total[j * width : (j + 1) * width, :] += dot(
-            act[...], grad_triple[:, j * width : (j + 1) * width], 0, 0
-        )
+        add_halves(total, j, dot(act[...], grad_triple[:, j * width : (j + 1) * width], 0, 0))
 
     @pl.when(step == pl.num_programs(0) - 1)
     def _():
-        give_halves(bits[0], total, send, keep, width)
+        give_halves(bits, total, send, keep, TURNED[1])
 
 
 def grad_tokens_kernel(bits, gradient, grad_triple, tokens, w_qkv, gain_self, grad_tokens):
@@ -408,8 +427,13 @@
     return jnp.sum(columns.T, axis=0, keepdims=True) / gain
 
 
-def pick(core, own, got, fill):
-    mine = pl.program_id(0) == core
+def in_order(bits, mine, own, got, ordered, turned):
+    size = ordered.shape[0] // 8
+
+    def fill(source):
+        for n in range(8):
+            at = pl.ds(pl.multiple_of(place(bits, n, turned) * size, size), size)
+            ordered[n * size : (n + 1) * size, :] = source[at, :]
 
     @pl.when(mine)
     def _():
@@ -420,60 +444,44 @@
         fill(got)
 
 
-def ffn_final_kernel(bits, own, got, w_expand, gain, contract, expand, gain_grad):
+def ffn_final_kernel(bits, own, got, w_expand, gain, contract, expand, gain_grad, ordered):
     step = pl.program_id(0)
     chunk = expand.shape[1]
-
-    def fill(source):
-        contract[...] = source[:chunk, :].astype(f32)
-        grad = source[chunk:, :].astype(f32)
-        expand[...] = grad
-        sums = row_sums(w_expand[...], grad, gain[...])
-
-        @pl.when(step == 0)
-        def _():
-            gain_grad[...] = sums
-
-        @pl.when(step > 0)
-        def _():
-            gain_grad[...] += sums
-
-    mine = (step >= pl.num_programs(0) // 2) == (bits[0] == 1)
-
-    @pl.when(mine)
-    def _():
-        fill(own)
-
-    @pl.when(jnp.logical_not(mine))
-    def _():
-        fill(got)
-
-
-def cross_final_kernel(bits, own, got, w_query, gain, cross_out, query, pair, self_out, gain_grad):
+    half = pl.num_programs(0) // 2
+    in_order(bits, (step >= half) == (bits[0] == 1), own, got, ordered, lax.rem(step, half) == 1)
+    contract[...] = ordered[:chunk, :].astype(f32)
+    grad = ordered[chunk:, :].astype(f32)
+    expand[...] = grad
+    sums = row_sums(w_expand[...], grad, gain[...])
+
+    @pl.when(step == 0)
+    def _():
+        gain_grad[...] = sums
+
+    @pl.when(step > 0)
+    def _():
+        gain_grad[...] += sums
+
+
+def cross_final_kernel(bits, own, got, w_query, gain, cross_out, query, pair, self_out, gain_grad, ordered):
     half, width = query.shape
-
-    def fill(source):
-        cross_out[...] = source[:half, :].astype(f32)
-        grad = source[half : 2 * half, :].astype(f32)
-        query[...] = grad
-        pair[:, :width] = source[2 * half : 3 * half, :].astype(f32)
-        pair[:, width:] = source[3 * half : 4 * half, :].astype(f32)
-        self_out[...] = source[4 * half :, :].astype(f32)
-        gain_grad[...] = row_sums(w_query[...], grad, gain[...])
-
-    pick(bits[0], own, got, fill)
-
-
-def self_final_kernel(bits, own, got, w_qkv, gain, qkv, gain_grad):
+    in_order(bits, pl.program_id(0) == bits[0], own, got, ordered, TURNED[0])
+    cross_out[...] = ordered[:half, :].astype(f32)
+    grad = ordered[half : 2 * half, :].astype(f32)
+    query[...] = grad
+    pair[:, :width] = ordered[2 * half : 3 * half, :].astype(f32)
+    pair[:, width:] = ordered[3 * half : 4 * half, :].astype(f32)
+    self_out[...] = ordered[4 * half :, :].astype(f32)
+    gain_grad[...] = row_sums(w_query[...], grad, gain[...])
+
+
+def self_final_kernel(bits, own, got, w_qkv, gain, qkv, gain_grad, ordered):
     half = qkv.shape[0]
     width = own.shape[1]
-
-    def fill(source):
-        for j in range(3):
-            qkv[:, j * width : (j + 1) * width] = source[j * half : (j + 1) * half, :].astype(f32)
-        gain_grad[...] = row_sums(w_qkv[...], qkv[...], gain[...])
-
-    pick(bits[0], own, got, fill)
+    in_order(bits, pl.program_id(0) == bits[0], own, got, ordered, TURNED[1])
+    for j in range(3):
+        qkv[:, j * width : (j + 1) * width] = ordered[j * half : (j + 1) * half, :].astype(f32)
+    gain_grad[...] = row_sums(w_qkv[...], qkv[...], gain[...])
 
 
 def call(kernel, grid, bits, ins, outs, scratch=(), flops=0, deps=(), limit=VMEM_LIMIT):
@@ -522,7 +530,42 @@
 
 SEQS = 4
 GROUP = 16
-MOST = 4
+TURNED = (True, None)
+PLAN = (
+    "do ffn",
+    "cross",
+    "do ffn",
+    "start cross",
+    "do cross",
+    "memory",
+    "self",
+    "do ffn",
+    "do cross",
+    "start self",
+    "do self",
+    "do ffn",
+    "do cross",
+    "tokens",
+    "do ffn",
+    "do self",
+    "do cross",
+    "do ffn",
+    "do self",
+    "do cross",
+    "do ffn",
+    "do self",
+    "do cross",
+    "do self",
+    "do self",
+    "do ffn",
+    "do cross",
+    "do self",
+    "end ffn",
+    "do self",
+    "do cross",
+    "end self",
+    "end cross",
+)
 
 
 def self_forward(bits, tokens, lengths, gain_self, w_qkv, w_out, gain_cross, w_query, length):
@@ -548,6 +591,7 @@
             ((rows, width), bf16, row, HBM),
         ],
         flops=12 * rows * width * width,
+        limit=36,
     )
 
 
@@ -617,6 +661,7 @@
             pltpu.VMEM((rows, width), f32),
         ],
         flops=12 * rows * width * hidden,
+        limit=32,
     )
 
 
@@ -651,7 +696,7 @@
         ],
         flops=14 * rows * width * width,
         deps=deps,
-        limit=VMEM_LIMIT if mem_total <= 32 else 2 * VMEM_LIMIT,
+        limit=40 if mem_total <= 32 else 56,
     )
 
 
@@ -674,6 +719,7 @@
         ],
         [pltpu.VMEM((3 * width, width), f32)],
         flops=14 * rows * width * width,
+        limit=40,
         deps=deps,
     )
 
@@ -704,53 +750,60 @@
     return (left.astype(f32) + right.astype(f32)).astype(bf16)
 
 
-def split_sum(mine, keep, got):
-    half = keep.shape[0] // 2
-
-    def part(which):
-        return added(
-            lax.dynamic_slice_in_dim(keep, which * half, half),
-            lax.dynamic_slice_in_dim(got, which * half, half),
-        )
-
-    return part(1 - mine), part(mine)
-
-
-def join(mine, own, got):
-    return jnp.where(mine == 0, jnp.concatenate([own, got]), jnp.concatenate([got, own]))
-
-
 def exchange(block, bit, devices):
     return lax.ppermute(block, "dp", [(i, i ^ (1 << bit)) for i in range(devices)])
 
 
 class Lane:
-    def __init__(self, bits, devices, order, send, keep, most):
-        halvings, rows = 1, keep.shape[0]
-        while halvings < min(most, len(order)) and rows % 32 == 0:
-            rows //= 2
-            halvings += 1
-        self.bits, self.devices = bits, devices
-        self.own, self.token = keep, send
-        self.got = exchange(send, order[0], devices)
-        self.todo = [("split", b) for b in order[1:halvings]]
-        self.todo += [("whole", b) for b in order[halvings:]]
-        back = order[:halvings][::-1]
-        self.todo += [("gather", back[0])] + list(zip(back[:-1], back[1:]))
+    def __init__(self, devices, orders, send, keep):
+        self.devices, self.orders, self.count = devices, orders, len(orders)
+        self.rest = list(range(4, devices.bit_length() - 1))
+        self.level, self.state = 0, "halve"
+        self.own = self.parted(keep)
+        self.got = self.parted(exchange(send, 0, devices))
+        self.token = send
+
+    def parted(self, block):
+        size = block.shape[0] // self.count
+        return [block[n * size : (n + 1) * size] for n in range(self.count)]
+
+    def send(self, blocks):
+        self.token = blocks[0]
+        if self.level in (1, 2):
+            bits = [order[self.level - 1] for order in self.orders]
+            self.got = [exchange(b, bit, self.devices) for b, bit in zip(blocks, bits)]
+        else:
+            bit = {0: 0, 3: 3}.get(self.level, self.level)
+            whole_block = jnp.concatenate(blocks) if len(blocks) > 1 else blocks[0]
+            self.token = whole_block
+            self.got = self.parted(exchange(whole_block, bit, self.devices))
 
     def advance(self, deps=()):
-        if not self.todo:
-            return
-        kind, bit = self.todo.pop(0)
-        own, got = after((self.own, self.got), deps)
-        if kind == "split":
-            send, self.own = split_sum(self.bits[bit], own, got)
-        elif kind in ("whole", "gather"):
-            send = self.own = added(own, got)
+        both = after((*self.own, *self.got), deps)
+        own, got = both[: self.count], both[self.count :]
+        if self.state == "halve":
+            half = own[0].shape[0] // 2
+            self.own = [added(a[half:], b[half:]) for a, b in zip(own, got)]
+            self.level += 1
+            self.send([added(a[:half], b[:half]) for a, b in zip(own, got)])
+            if self.level == 3:
+                self.state = "whole"
+        elif self.state == "whole":
+            self.own = [added(a, b) for a, b in zip(own, got)]
+            if self.rest:
+                self.level = self.rest.pop(0)
+            else:
+                self.level, self.state = 3, "join"
+            self.send(self.own)
         else:
-            send = self.own = join(self.bits[kind], own, got)
-        self.token = send
-        self.got = exchange(send, bit, self.devices)
+            self.own = [jnp.concatenate([b, a]) for a, b in zip(own, got)]
+            self.level -= 1
+            self.send(self.own)
+            if self.level == 0:
+                self.state = "done"
+
+    def result(self):
+        return [blocks[0] if self.count == 1 else jnp.concatenate(blocks) for blocks in (self.own, self.got)]
 
 
 def ffn_final(bits, own, got, w_expand, gain, deps=(), chunk=512):
@@ -767,7 +820,7 @@
     return call(
         ffn_final_kernel, (steps,), bits,
         [
-            (own, source(True), HBM), (got, source(False), HBM),
+            (own, source(True)), (got, source(False)),
             (w_expand, pl.BlockSpec((width, chunk), lambda i, bits: (0, i))),
             (gain, whole(1, width)),
         ],
@@ -776,6 +829,7 @@
             ((width, hidden), f32, pl.BlockSpec((width, chunk), lambda i, bits: (0, i))),
             ((1, width), f32, whole(1, width)),
         ],
+        [pltpu.VMEM((2 * chunk, width), bf16)],
         deps=deps,
     )
 
@@ -788,13 +842,14 @@
     return call(
         cross_final_kernel, (2,), bits,
         [
-            (own, whole(*own.shape), HBM), (got, whole(*own.shape), HBM), (w_query, part), (gain, column),
+            (own, whole(*own.shape)), (got, whole(*own.shape)), (w_query, part), (gain, column),
         ],
         [
             ((width, width), f32, part), ((width, width), f32, part),
             ((width, 2 * width), f32, by_step(half, 2 * width)), ((width, width), f32, part),
             ((1, width), f32, column),
         ],
+        [pltpu.VMEM(own.shape, bf16)],
         deps=deps,
     )
 
@@ -806,10 +861,11 @@
     return call(
         self_final_kernel, (2,), bits,
         [
-            (own, whole(*own.shape), HBM), (got, whole(*own.shape), HBM),
+            (own, whole(*own.shape)), (got, whole(*own.shape)),
             (w_qkv, by_step(half, 3 * width)), (gain, column),
         ],
         [((width, 3 * width), f32, by_step(half, 3 * width)), ((1, width), f32, column)],
+        [pltpu.VMEM(own.shape, bf16)],
         deps=deps,
     )
 
@@ -823,11 +879,8 @@
     rows = seq_count * length
     gain_self, gain_cross, gain_ffn = gain_self[None], gain_cross[None], gain_ffn[None]
     flat_tokens = tokens.reshape(rows, width)
-    order = tuple(range(devices.bit_length() - 1))
-    turned = order[:1] + order[2:3] + order[1:2] + order[3:]
     me = lax.axis_index("dp")
-    mine = [(me >> b) & 1 for b in order]
-    bits = jnp.stack(mine).astype(jnp.int32)
+    bits = jnp.stack([(me >> b) & 1 for b in range(devices.bit_length() - 1)]).astype(jnp.int32)
     raw = lax.all_to_all(
         memory.reshape(devices, -1, width), "dp", split_axis=0, concat_axis=0, tiled=True
     ).reshape(-1, width)
@@ -842,41 +895,65 @@
     output, grad_normed, send, keep = feed_forward(
         bits, act, grad_low_near, late_near, w_expand, w_contract
     )
-    ffn = Lane(mine, devices, order, send, keep, MOST)
-    ffn.advance()
-    gradient, grad_arrived, send, keep = cross_backward(
-        bits, grad_normed, late, grad_low, cross, cross_weights, pairs, queries, mid, arrived,
-        attended, w_cross_out, w_cross_query, w_cross_kv, gain_ffn, gain_cross, length, mem_total,
-        deps=[ffn.token],
-    )
-    ffn.advance([send])
-    crossed = Lane(mine, devices, order, after((send,), [ffn.token])[0], keep, MOST)
-    crossed.advance()
-    grad_triple, send, keep = self_backward(
-        bits, gradient, triple, self_weights, act_one, w_self_out, length, deps=[ffn.token, crossed.token]
-    )
-    ffn.advance([send])
-    crossed.advance([ffn.token])
-    selfs = Lane(mine, devices, turned, after((send,), [crossed.token])[0], keep, MOST)
-    selfs.advance()
-    grad_memory = lax.all_to_all(
-        after((grad_arrived,), [selfs.token])[0].reshape(devices, -1, width),
-        "dp", split_axis=0, concat_axis=0, tiled=True,
-    ).reshape(memory.shape)
-    grad_tokens = token_gradient(
-        bits, gradient, grad_triple, flat_tokens, w_qkv, gain_self,
-        deps=[ffn.token, crossed.token, selfs.token],
-    )
-    deps = [grad_tokens, grad_memory]
-    while selfs.todo or crossed.todo or ffn.todo:
-        for lane in (ffn, crossed, selfs):
-            lane.advance(deps)
-            deps = [lane.token]
-    grad_contract, grad_expand, grad_gain_ffn = ffn_final(bits, ffn.own, ffn.got, w_expand, gain_ffn)
-    grad_cross_out, grad_cross_query, grad_cross_kv, grad_self_out, grad_gain_cross = cross_final(
-        bits, crossed.own, crossed.got, w_cross_query, gain_cross
-    )
-    grad_qkv, grad_gain_self = self_final(bits, selfs.own, selfs.got, w_qkv, gain_self)
+    straight, turned = (1, 2), (2, 1)
+    lanes = {"ffn": Lane(devices, (straight, turned), send, keep)}
+    token, fresh, kept, found = send, {}, {}, {}
+    for n, name in enumerate(PLAN):
+        deps = [token]
+        if PLAN[n - 1] == "self":
+            deps.append(grad_memory)
+        if name.startswith("end"):
+            lane = lanes[name[4:]]
+            while lane.state != "done":
+                lane.advance(deps)
+                deps = [lane.token]
+        if name == "cross":
+            gradient, grad_arrived, send, keep = cross_backward(
+                bits, grad_normed, late, grad_low, cross, cross_weights, pairs, queries, mid, arrived,
+                attended, w_cross_out, w_cross_query, w_cross_kv, gain_ffn, gain_cross, length, mem_total,
+                deps=deps,
+            )
+            token = fresh["cross"] = send
+            kept["cross"] = keep
+        elif name == "self":
+            grad_triple, send, keep = self_backward(
+                bits, gradient, triple, self_weights, act_one, w_self_out, length, deps=deps
+            )
+            token = fresh["self"] = send
+            kept["self"] = keep
+        elif name == "tokens":
+            token = grad_tokens = token_gradient(
+                bits, gradient, grad_triple, flat_tokens, w_qkv, gain_self, deps=deps
+            )
+        elif name == "memory":
+            grad_memory = lax.all_to_all(
+                after((grad_arrived,), deps)[0].reshape(devices, -1, width),
+                "dp", split_axis=0, concat_axis=0, tiled=True,
+            ).reshape(memory.shape)
+        elif name in ("start cross", "start self"):
+            name = name[6:]
+            order = turned if TURNED[name == "self"] else straight
+            lanes[name] = Lane(devices, (order,), after((fresh[name],), deps)[0], kept[name])
+        elif name == "end ffn":
+            own, got = lanes["ffn"].result()
+            found["ffn"] = ffn_final(bits, own, got, w_expand, gain_ffn, deps=deps)
+            token = found["ffn"][2]
+        elif name == "end cross":
+            own, got = lanes["cross"].result()
+            found["cross"] = cross_final(bits, own, got, w_cross_query, gain_cross, deps=deps)
+            token = found["cross"][4]
+        elif name == "end self":
+            own, got = lanes["self"].result()
+            found["self"] = self_final(bits, own, got, w_qkv, gain_self, deps=deps)
+            token = found["self"][1]
+        else:
+            lane = lanes[name[3:]]
+            if lane.state != "done":
+                lane.advance(deps)
+                token = lane.token
+    grad_contract, grad_expand, grad_gain_ffn = found["ffn"]
+    grad_cross_out, grad_cross_query, grad_cross_kv, grad_self_out, grad_gain_cross = found["cross"]
+    grad_qkv, grad_gain_self = found["self"]
     return (
         output.reshape(tokens.shape),
         grad_tokens.reshape(tokens.shape),

time: 283 us -> 243 us (0.86)
  waiting for transfers between devices: 79.7 us -> 56.2 us
  other arithmetic: 23.9 us -> 8.22 us
  starting transfers between devices: 39.1 us -> 45.8 us
  Pallas kernels: 129 us -> 123 us
    ppermute x27 -> x31, waiting for transfers between devices: 79.7 us -> 56.2 us  [exchange(): lax.ppermute(block, 'dp', [(i, i ^ 1 << bit) for i in range(devices)])]
    convert_element_type x15 -> x19, other arithmetic: 16.7 us -> 8.16 us  [added(): return (left.astype(f32) + right.astype(f32)).astype(bf16)]
    ppermute x27 -> x31, starting transfers between devices: 25.9 us -> 34.4 us  [exchange(): lax.ppermute(block, 'dp', [(i, i ^ 1 << bit) for i in range(devices)])]
    select_n x9 -> x0, other arithmetic: 7.14 us -> none  [join(): jnp.where(mine == 0, jnp.concatenate([own, got]), jnp.concatenate([got, o...]
    pallas_call x9, Pallas kernels: 129 us -> 123 us  [call(): pl.pallas_call(body, grid_spec=pltpu.PrefetchScalarGridSpec(num_scalar_pr...]
    unnamed x45 -> x50, local copies, waits for them, and re-layouts: 9.31 us -> 6.17 us
  transfers between devices with their start and end apart: 29 -> 33, of which waited for: 16 -> 15; matrix products, arithmetic and copies ran while one was open for 4% -> 3% of each run, Pallas kernels for 27% -> 31%
where the time goes in v2:
time: 243 us; the launch traced here: 242 us
  Pallas kernels  123 us (51%)
  waiting for transfers between devices  56.2 us (23%)
  starting transfers between devices  45.8 us (19%)
  local copies, waits for them, and re-layouts  8.35 us (3%)
  other arithmetic  8.22 us (3%)
    pallas_call x9, Pallas kernels, call(): pl.pallas_call(body, grid_spec=pltpu.PrefetchScalarGridSpec(num_scalar_pr...  123 us
    ppermute x31, waiting for transfers between devices, exchange(): lax.ppermute(block, 'dp', [(i, i ^ 1 << bit) for i in range(devices)])  56.2 us
    ppermute x31, starting transfers between devices, exchange(): lax.ppermute(block, 'dp', [(i, i ^ 1 << bit) for i in range(devices)])  34.4 us
    convert_element_type x19, other arithmetic, added(): return (left.astype(f32) + right.astype(f32)).astype(bf16)  8.16 us
    all_to_all x1, starting transfers between devices, local(): lax.all_to_all(memory.reshape(devices, -1, width), 'dp', split_axis=0, co...  7.3 us
    unnamed x50, local copies, waits for them, and re-layouts  6.17 us
  transfers between devices with their start and end apart: 33, of which 15 were waited for; matrix products, arithmetic and copies ran while one was open for 3% of the time, Pallas kernels for 31%

profile of v2, /device:TPU:0, one launch (start us, length us, event | category | flops | bytes accessed | tf_op | source)
XLA Modules:
  0.0 242.5 jit_solution(17035701965976240664)
XLA Ops:
  0.6 7.3 %all-to-all-start = ((bf16[32,16,512]{2,1,0:T(8,128)(2,1)}), bf16[32,16,512]{2,1,0:T(8,128)(2,1)S(1)}, u32[]{:S(2)}, u32[]{:S(2)}) async-start(bf16[32,16,512]{2,1,0:T(8,128)(2,1)} %bitcast.33), calls=%async_computation | async-start | bytes 1048576 | tf_op jit(solution)/shard_map/all_to_all | solution.py:884
  10.1 15.7 %shard_map.246 = (bf16[2048,512]{1,0:T(8,128)(2,1)}, bf16[2048,1536]{1,0:T(8,128)(2,1)}, bf16[16,4,128,256]{3,2,1,0:T(8,128)(2,1)}, bf16[2048,512]{1,0:T(8,128)(...) custom-call(s32[5]{0:T(128)S(1)} %stack.23.bits_ref, s32[16]{0:T(128)S(1)} %copy-done.12, ...), custom_call_target="tpu_custom_call" | custom-call | flops 6442450944 | bytes 23597120 | tf_op jit(solution)/shard_map/pallas_call | solution.py:504
  27.0 10.7 %shard_map.247 = (bf16[512,512]{1,0:T(8,128)(2,1)}, bf16[512,1024]{1,0:T(8,128)(2,1)}, bf16[16,256,128]{2,1,0:T(8,128)(2,1)}, bf16[2048,512]{1,0:T(8,128)(2,1)},...) custom-call(s32[5]{0:T(128)S(1)} %stack.23.bits_ref, ...), custom_call_target="tpu_custom_call" | custom-call | flops 3221225472 | bytes 23595136 | tf_op jit(solution)/shard_map/pallas_call | solution.py:504
  37.7 34.7 %shard_map.248 = (bf16[2048,512]{1,0:T(8,128)(2,1)}, bf16[2048,512]{1,0:T(8,128)(2,1)}, bf16[2048,512]{1,0:T(8,128)(2,1)}, bf16[2048,512]{1,0:T(8,128)(2,1)}) custom-call(s32[5]{0:T(128)S(1)} %stack.23.bits_ref, bf16[2048,512]{1,0:T(8,128)(2,1)S(1)} %get-tuple-element.118.refs_0_, bf16[2048,512]{1,0:T(8,128)(2,1)S(1)} %get-tuple-element.119.refs_1_, ...), custom_call_target="tpu_custom_call" | custom-call | flops 25769803776 | bytes 18874368 | tf_op jit(solution)/shard_map/pallas_call | solution.py:504
  81.6 24.7 %shard_map.249 = (bf16[2048,512]{1,0:T(8,128)(2,1)}, bf16[512,512]{1,0:T(8,128)(2,1)}, bf16[1280,512]{1,0:T(8,128)(2,1)}, bf16[1280,512]{1,0:T(8,128)(2,1)}) custom-call(s32[5]{0:T(128)S(1)} %stack.23.bits_ref, bf16[2048,512]{1,0:T(8,128)(2,1)} %get-tuple-element.122.refs_0_, bf16[2048,512]{1,0:T(8,128)(2,1)} %get-tuple-element.123.refs_1_, ...), custom_call_target="tpu_custom_call" | custom-call | flops 7516192768 | bytes 24645632 | tf_op jit(solution)/shard_map/pallas_call | solution.py:504
  107.3 3.2 %collective-permute-done.3 = bf16[1280,512]{1,0:T(8,128)(2,1)S(1)} collective-permute-done((bf16[1280,512]{1,0:T(8,128)(2,1)}, bf16[1280,512]{1,0:T(8,128)(2,1)S(1)}, u32[]{:S(2)}, u32[]{:S(2)}) %collective-permute-start.3) | collective-permute-done | bytes 1310752 | tf_op jit(solution)/shard_map/ppermute | solution.py:754
  111.0 4.1 %all-to-all-start.1 = ((bf16[32,16,512]{2,1,0:T(8,128)(2,1)}), bf16[32,16,512]{2,1,0:T(8,128)(2,1)}, u32[]{:S(2)}, u32[]{:S(2)}) async-start(bf16[32,16,512]{2,1,0:T(8,128)(2,1)} %bitcast.34), calls=%async_computation.1 | async-start | bytes 1048576 | tf_op jit(solution)/shard_map/all_to_all | solution.py:929
  120.6 16.6 %shard_map.250 = (bf16[2048,1536]{1,0:T(8,128)(2,1)}, bf16[768,512]{1,0:T(8,128)(2,1)}, bf16[768,512]{1,0:T(8,128)(2,1)}) custom-call(s32[5]{0:T(128)S(1)} %stack.23.bits_ref, bf16[2048,512]{1,0:T(8,128)(2,1)} %get-tuple-element.134.refs_0_, bf16[2048,1536]{1,0:T(8,128)(2,1)} %get-tuple-element.135.refs_1_, ...), custom_call_target="tpu_custom_call" | custom-call | flops 7516192768 | bytes 23068672 | tf_op jit(solution)/shard_map/pallas_call | solution.py:504
  138.9 4.0 %collective-permute-done.4 = bf16[640,512]{1,0:T(8,128)(2,1)} collective-permute-done((bf16[640,512]{1,0:T(8,128)(2,1)S(1)}, bf16[640,512]{1,0:T(8,128)(2,1)}, u32[]{:S(2)}, u32[]{:S(2)}) %collective-permute-start.4) | collective-permute-done | bytes 655392 | tf_op jit(solution)/shard_map/ppermute | solution.py:754
  147.3 5.7 %collective-permute-done.8 = bf16[256,512]{1,0:T(8,128)(2,1)S(1)} collective-permute-done((bf16[256,512]{1,0:T(8,128)(2,1)S(1)}, bf16[256,512]{1,0:T(8,128)(2,1)S(1)}, u32[]{:S(2)}, u32[]{:S(2)}) %collective-permute-start.8) | collective-permute-done | bytes 262176 | tf_op jit(solution)/shard_map/ppermute | solution.py:754
  159.0 10.0 %shard_map.251 = bf16[2048,512]{1,0:T(8,128)(2,1)} custom-call(s32[5]{0:T(128)S(1)} %stack.23.bits_ref, bf16[2048,512]{1,0:T(8,128)(2,1)} %get-tuple-element.134.refs_0_, bf16[2048,1536]{1,0:T(8,128)(2,1)} %get-tuple-element.147.refs_1_, bf16[2048,512]{1,0:T(8,128)(2,1)} %bitcast.31, bf16[512,1536]{1,0:T(8,128)(2,1)} %refs_2_.4, f32[1,512]{1,0:T(1,128)S(1)} %bitcast.21, ...), custom_call_target="tpu_custom_call" | custom-call | flops 3221225472 | bytes 14157824 | tf_op jit(solution)/shard_map/pallas_call | solution.py:504
  170.6 3.2 %collective-permute-start.18 = (bf16[160,512]{1,0:T(8,128)(2,1)S(1)}, bf16[160,512]{1,0:T(8,128)(2,1)S(1)}, u32[]{:S(2)}, u32[]{:S(2)}) collective-permute-start(bf16[160,512]{1,0:T(8,128)(2,1)S(1)} %add_convert_fusion.17), channel_id=1, source_target_pairs={{0,16},{1,17},{2,18},{3,19},{4,20},{5,21},{6,22},{7,23},{8,24},{9,... | collective-permute-start | bytes 491528 | tf_op jit(solution)/shard_map/ppermute | solution.py:754
  173.8 6.3 %collective-permute-done.13 = bf16[256,512]{1,0:T(8,128)(2,1)S(1)} collective-permute-done((bf16[256,512]{1,0:T(8,128)(2,1)S(1)}, bf16[256,512]{1,0:T(8,128)(2,1)S(1)}, u32[]{:S(2)}, u32[]{:S(2)}) %collective-permute-start.13) | collective-permute-done | bytes 262176 | tf_op jit(solution)/shard_map/ppermute | solution.py:754
  188.8 3.0 %collective-permute-start.19 = (bf16[96,512]{1,0:T(8,128)(2,1)S(1)}, bf16[96,512]{1,0:T(8,128)(2,1)S(1)}, u32[]{:S(2)}, u32[]{:S(2)}) collective-permute-start(bf16[96,512]{1,0:T(8,128)(2,1)S(1)} %add_convert_fusion.29), channel_id=1, source_target_pairs={{0,16},{1,17},{2,18},{3,19},{4,20},{5,21},{6,22},{7,23},{8,24},{9,... | collective-permute-start | bytes 294920 | tf_op jit(solution)/shard_map/ppermute | solution.py:754
  194.5 2.5 %collective-permute-start.21 = (bf16[96,512]{1,0:T(8,128)(2,1)S(1)}, bf16[96,512]{1,0:T(8,128)(2,1)S(1)}, u32[]{:S(2)}, u32[]{:S(2)}) collective-permute-start(bf16[96,512]{1,0:T(8,128)(2,1)S(1)} %add_convert_fusion.28), channel_id=1, source_target_pairs={{0,8},{1,9},{2,10},{3,11},{4,12},{5,13},{6,14},{7,15},{8,0},{9,1},... | collective-permute-start | bytes 294920 | tf_op jit(solution)/shard_map/ppermute | solution.py:754
  197.0 2.6 %collective-permute-done.21 = bf16[96,512]{1,0:T(8,128)(2,1)S(1)} collective-permute-done((bf16[96,512]{1,0:T(8,128)(2,1)S(1)}, bf16[96,512]{1,0:T(8,128)(2,1)S(1)}, u32[]{:S(2)}, u32[]{:S(2)}) %collective-permute-start.21) | collective-permute-done | bytes 98336 | tf_op jit(solution)/shard_map/ppermute | solution.py:754
  199.6 3.5 %collective-permute-done.25 = bf16[512,512]{1,0:T(8,128)(2,1)S(1)} collective-permute-done((bf16[512,512]{1,0:T(8,128)(2,1)S(1)}, bf16[512,512]{1,0:T(8,128)(2,1)S(1)}, u32[]{:S(2)}, u32[]{:S(2)}) %collective-permute-start.25) | collective-permute-done | bytes 524320 | tf_op jit(solution)/shard_map/ppermute | solution.py:754
  204.5 9.0 %collective-permute-done.23 = bf16[320,512]{1,0:T(8,128)(2,1)S(1)} collective-permute-done((bf16[320,512]{1,0:T(8,128)(2,1)S(1)}, bf16[320,512]{1,0:T(8,128)(2,1)S(1)}, u32[]{:S(2)}, u32[]{:S(2)}) %collective-permute-start.23) | collective-permute-done | bytes 327712 | tf_op jit(solution)/shard_map/ppermute | solution.py:754
  214.8 4.6 %shard_map.252 = (f32[2048,512]{1,0:T(8,128)}, f32[512,2048]{1,0:T(8,128)}, f32[1,512]{1,0:T(1,128)}) custom-call(s32[5]{0:T(128)S(1)} %stack.23.bits_ref, bf16[2048,512]{1,0:T(8,128)(2,1)S(1)} %constant_dynamic-update-slice_fusion.12.refs_0_, bf16[2048,512]{1,0:T(8,128)(2,1)S(1)} %collective-permute-done.27.refs_1_, bf16[512,2048]{1,0:T(8,128)(2,1)S(1)} %copy-done.1, ...), custom_call_target="tpu_custom_call" | custom-call | bytes 14684160 | tf_op jit(solution)/shard_map/pallas_call | solution.py:504
  219.3 5.4 %collective-permute-done.26 = bf16[384,512]{1,0:T(8,128)(2,1)S(1)} collective-permute-done((bf16[384,512]{1,0:T(8,128)(2,1)S(1)}, bf16[384,512]{1,0:T(8,128)(2,1)S(1)}, u32[]{:S(2)}, u32[]{:S(2)}) %collective-permute-start.26) | collective-permute-done | bytes 393248 | tf_op jit(solution)/shard_map/ppermute | solution.py:754
  224.8 5.2 %collective-permute-done.29 = bf16[640,512]{1,0:T(8,128)(2,1)S(1)} collective-permute-done((bf16[640,512]{1,0:T(8,128)(2,1)S(1)}, bf16[640,512]{1,0:T(8,128)(2,1)S(1)}, u32[]{:S(2)}, u32[]{:S(2)}) %collective-permute-start.29) | collective-permute-done | bytes 655392 | tf_op jit(solution)/shard_map/ppermute | solution.py:754
  230.6 3.6 %collective-permute-done.28.refs_1_ = bf16[768,512]{1,0:T(8,128)(2,1)S(1)} collective-permute-done((bf16[768,512]{1,0:T(8,128)(2,1)S(1)}, bf16[768,512]{1,0:T(8,128)(2,1)S(1)}, u32[]{:S(2)}, u32[]{:S(2)}) %collective-permute-start.28) | collective-permute-done | bytes 786464 | tf_op jit(solution)/shard_map/ppermute | solution.py:754
  234.3 2.5 %shard_map.253 = (f32[512,1536]{1,0:T(8,128)}, f32[1,512]{1,0:T(1,128)}) custom-call(s32[5]{0:T(128)S(1)} %stack.23.bits_ref, bf16[768,512]{1,0:T(8,128)(2,1)S(1)} %constant_dynamic-update-slice_fusion.20.refs_0_, bf16[768,512]{1,0:T(8,128)(2,1)S(1)} %collective-permute-done.28.refs_1_, bf16[512,1536]{1,0:T(8,128)(2,1)S(1)} %copy-done, ...), custom_call_target="tpu_custom_call" | custom-call | bytes 6295552 | tf_op jit(solution)/shard_map/pallas_call | solution.py:504
  237.5 3.1 %shard_map.254 = (f32[512,512]{1,0:T(8,128)}, f32[512,512]{1,0:T(8,128)}, f32[512,1024]{1,0:T(8,128)}, f32[512,512]{1,0:T(8,128)}, f32[1,512]{1,0:T(1,128)}) custom-call(s32[5]{0:T(128)S(1)} %stack.23.bits_ref, bf16[1280,512]{1,0:T(8,128)(2,1)S(1)} %constant_dynamic-update-slice_fusion.22.refs_4_.refs_0_, ...), custom_call_target="tpu_custom_call" | custom-call | bytes 8392704 | tf_op jit(solution)/shard_map/pallas_call | solution.py:504
  (140 shorter events, 49.9 us)
Async XLA Ops:
  0.6 25.1 %all-to-all-start = ((bf16[32,16,512]{2,1,0:T(8,128)(2,1)}), bf16[32,16,512]{2,1,0:T(8,128)(2,1)S(1)}, u32[]{:S(2)}, u32[]{:S(2)}) async-start(bf16[32,16,512]{2,1,0:T(8,128)(2,1)} %bitcast.33), calls=%async_computation | async-start | bytes 1048576 | tf_op jit(solution)/shard_map/all_to_all | solution.py:884
  77.2 29.1 %collective-permute-start.1 = (bf16[512,512]{1,0:T(8,128)(2,1)S(1)}, bf16[512,512]{1,0:T(8,128)(2,1)S(1)}, u32[]{:S(2)}, u32[]{:S(2)}) collective-permute-start(bf16[512,512]{1,0:T(8,128)(2,1)S(1)} %get-tuple-element.224.refs_15_), channel_id=1, source_target_pairs={{0,2},{1,3},{2,0},{3,1},{4,6},{5,7},{6,4},{7,5},{8,10},{9,11},{10,... | collective-permute-start | bytes 1572872 | tf_op jit(solution)/shard_map/ppermute | solution.py:754
  80.2 26.2 %collective-permute-start.2 = (bf16[512,512]{1,0:T(8,128)(2,1)S(1)}, bf16[512,512]{1,0:T(8,128)(2,1)S(1)}, u32[]{:S(2)}, u32[]{:S(2)}) collective-permute-start(bf16[512,512]{1,0:T(8,128)(2,1)S(1)} %get-tuple-element.221), channel_id=1, source_target_pairs={{0,4},{1,5},{2,6},{3,7},{4,0},{5,1},{6,2},{7,3},{8,12},{9,13},{10,... | collective-permute-start | bytes 1572872 | tf_op jit(solution)/shard_map/ppermute | solution.py:754
  111.0 26.3 %all-to-all-start.1 = ((bf16[32,16,512]{2,1,0:T(8,128)(2,1)}), bf16[32,16,512]{2,1,0:T(8,128)(2,1)}, u32[]{:S(2)}, u32[]{:S(2)}) async-start(bf16[32,16,512]{2,1,0:T(8,128)(2,1)} %bitcast.34), calls=%async_computation.1 | async-start | bytes 1048576 | tf_op jit(solution)/shard_map/all_to_all | solution.py:929
  115.1 22.2 %collective-permute-start.5 = (bf16[256,512]{1,0:T(8,128)(2,1)}, bf16[256,512]{1,0:T(8,128)(2,1)}, u32[]{:S(2)}, u32[]{:S(2)}) collective-permute-start(bf16[256,512]{1,0:T(8,128)(2,1)} %get-tuple-element.236), channel_id=1, source_target_pairs={{0,4},{1,5},{2,6},{3,7},{4,0},{5,1},{6,2},{7,3},{8,12},{9,13},{10,... | collective-permute-start | bytes 786440 | tf_op jit(solution)/shard_map/ppermute | solution.py:754
  118.6 18.7 %collective-permute-start.6 = (bf16[256,512]{1,0:T(8,128)(2,1)S(1)}, bf16[256,512]{1,0:T(8,128)(2,1)}, u32[]{:S(2)}, u32[]{:S(2)}) collective-permute-start(bf16[256,512]{1,0:T(8,128)(2,1)S(1)} %get-tuple-element.233), channel_id=1, source_target_pairs={{0,2},{1,3},{2,0},{3,1},{4,6},{5,7},{6,4},{7,5},{8,10},{9,11},{10,... | collective-permute-start | bytes 786440 | tf_op jit(solution)/shard_map/ppermute | solution.py:754
  120.1 22.9 %collective-permute-start.4 = (bf16[640,512]{1,0:T(8,128)(2,1)S(1)}, bf16[640,512]{1,0:T(8,128)(2,1)}, u32[]{:S(2)}, u32[]{:S(2)}) collective-permute-start(bf16[640,512]{1,0:T(8,128)(2,1)S(1)} %get-tuple-element.220.refs_5_), channel_id=1, source_target_pairs={{0,4},{1,5},{2,6},{3,7},{4,0},{5,1},{6,2},{7,3},{8,12},{9,13},{10,... | collective-permute-start | bytes 1966088 | tf_op jit(solution)/shard_map/ppermute | solution.py:754
  144.2 8.8 %collective-permute-start.9 = (bf16[768,512]{1,0:T(8,128)(2,1)S(1)}, bf16[768,512]{1,0:T(8,128)(2,1)S(1)}, u32[]{:S(2)}, u32[]{:S(2)}) collective-permute-start(bf16[768,512]{1,0:T(8,128)(2,1)S(1)} %copy-done.17), channel_id=1, source_target_pairs={{0,1},{1,0},{2,3},{3,2},{4,5},{5,4},{6,7},{7,6},{8,9},{9,8},{10,11... | collective-permute-start | bytes 2359304 | tf_op jit(solution)/shard_map/ppermute | solution.py:754
  144.3 8.7 %collective-permute-start.8 = (bf16[256,512]{1,0:T(8,128)(2,1)S(1)}, bf16[256,512]{1,0:T(8,128)(2,1)S(1)}, u32[]{:S(2)}, u32[]{:S(2)}) collective-permute-start(bf16[256,512]{1,0:T(8,128)(2,1)S(1)} %pad_maximum_fusion), channel_id=1, source_target_pairs={{0,8},{1,9},{2,10},{3,11},{4,12},{5,13},{6,14},{7,15},{8,0},{9,1},... | collective-permute-start | bytes 786440 | tf_op jit(solution)/shard_map/ppermute | solution.py:754
  146.0 11.4 %collective-permute-start.7 = (bf16[320,512]{1,0:T(8,128)(2,1)S(1)}, bf16[320,512]{1,0:T(8,128)(2,1)S(1)}, u32[]{:S(2)}, u32[]{:S(2)}) collective-permute-start(bf16[320,512]{1,0:T(8,128)(2,1)S(1)} %get-tuple-element.231), channel_id=1, source_target_pairs={{0,2},{1,3},{2,0},{3,1},{4,6},{5,7},{6,4},{7,5},{8,10},{9,11},{10,... | collective-permute-start | bytes 983048 | tf_op jit(solution)/shard_map/ppermute | solution.py:754
  153.3 16.5 %collective-permute-start.10 = (bf16[384,512]{1,0:T(8,128)(2,1)S(1)}, bf16[384,512]{1,0:T(8,128)(2,1)S(1)}, u32[]{:S(2)}, u32[]{:S(2)}) collective-permute-start(bf16[384,512]{1,0:T(8,128)(2,1)S(1)} %get-tuple-element.230), channel_id=1, source_target_pairs={{0,2},{1,3},{2,0},{3,1},{4,6},{5,7},{6,4},{7,5},{8,10},{9,11},{10,... | collective-permute-start | bytes 1179656 | tf_op jit(solution)/shard_map/ppermute | solution.py:754
  154.9 14.2 %collective-permute-start.11 = (bf16[256,512]{1,0:T(8,128)(2,1)S(1)}, bf16[256,512]{1,0:T(8,128)(2,1)S(1)}, u32[]{:S(2)}, u32[]{:S(2)}) collective-permute-start(bf16[256,512]{1,0:T(8,128)(2,1)S(1)} %pad_maximum_fusion.1), channel_id=1, source_target_pairs={{0,16},{1,17},{2,18},{3,19},{4,20},{5,21},{6,22},{7,23},{8,24},{9,... | collective-permute-start | bytes 786440 | tf_op jit(solution)/shard_map/ppermute | solution.py:754
  157.4 13.1 %collective-permute-start.14 = (bf16[160,512]{1,0:T(8,128)(2,1)S(1)}, bf16[160,512]{1,0:T(8,128)(2,1)S(1)}, u32[]{:S(2)}, u32[]{:S(2)}) collective-permute-start(bf16[160,512]{1,0:T(8,128)(2,1)S(1)} %get-tuple-element.240.refs_5_), channel_id=1, source_target_pairs={{0,8},{1,9},{2,10},{3,11},{4,12},{5,13},{6,14},{7,15},{8,0},{9,1},... | collective-permute-start | bytes 491528 | tf_op jit(solution)/shard_map/ppermute | solution.py:754
  169.2 10.8 %collective-permute-start.13 = (bf16[256,512]{1,0:T(8,128)(2,1)S(1)}, bf16[256,512]{1,0:T(8,128)(2,1)S(1)}, u32[]{:S(2)}, u32[]{:S(2)}) collective-permute-start(bf16[256,512]{1,0:T(8,128)(2,1)S(1)} %pad_maximum_fusion.2), channel_id=1, source_target_pairs={{0,8},{1,9},{2,10},{3,11},{4,12},{5,13},{6,14},{7,15},{8,0},{9,1},... | collective-permute-start | bytes 786440 | tf_op jit(solution)/shard_map/ppermute | solution.py:754
  169.9 11.9 %collective-permute-start.12 = (bf16[192,512]{1,0:T(8,128)(2,1)S(1)}, bf16[192,512]{1,0:T(8,128)(2,1)S(1)}, u32[]{:S(2)}, u32[]{:S(2)}) collective-permute-start(bf16[192,512]{1,0:T(8,128)(2,1)S(1)} %get-tuple-element.237), channel_id=1, source_target_pairs={{0,4},{1,5},{2,6},{3,7},{4,0},{5,1},{6,2},{7,3},{8,12},{9,13},{10,... | collective-permute-start | bytes 589832 | tf_op jit(solution)/shard_map/ppermute | solution.py:754
  170.6 11.3 %collective-permute-start.18 = (bf16[160,512]{1,0:T(8,128)(2,1)S(1)}, bf16[160,512]{1,0:T(8,128)(2,1)S(1)}, u32[]{:S(2)}, u32[]{:S(2)}) collective-permute-start(bf16[160,512]{1,0:T(8,128)(2,1)S(1)} %add_convert_fusion.17), channel_id=1, source_target_pairs={{0,16},{1,17},{2,18},{3,19},{4,20},{5,21},{6,22},{7,23},{8,24},{9,... | collective-permute-start | bytes 491528 | tf_op jit(solution)/shard_map/ppermute | solution.py:754
  182.0 9.9 %collective-permute-start.20 = (bf16[160,512]{1,0:T(8,128)(2,1)S(1)}, bf16[160,512]{1,0:T(8,128)(2,1)S(1)}, u32[]{:S(2)}, u32[]{:S(2)}) collective-permute-start(bf16[160,512]{1,0:T(8,128)(2,1)S(1)} %add_convert_fusion.16), channel_id=1, source_target_pairs={{0,8},{1,9},{2,10},{3,11},{4,12},{5,13},{6,14},{7,15},{8,0},{9,1},... | collective-permute-start | bytes 491528 | tf_op jit(solution)/shard_map/ppermute | solution.py:754
  187.1 16.0 %collective-permute-start.24 = (bf16[512,512]{1,0:T(8,128)(2,1)S(1)}, bf16[512,512]{1,0:T(8,128)(2,1)S(1)}, u32[]{:S(2)}, u32[]{:S(2)}) collective-permute-start(bf16[512,512]{1,0:T(8,128)(2,1)S(1)} %constant_dynamic-update-slice_fusion.4), channel_id=1, source_target_pairs={{0,2},{1,3},{2,0},{3,1},{4,6},{5,7},{6,4},{7,5},{8,10},{9,11},{10,... | collective-permute-start | bytes 1572872 | tf_op jit(solution)/shard_map/ppermute | solution.py:754
  191.9 11.2 %collective-permute-start.25 = (bf16[512,512]{1,0:T(8,128)(2,1)S(1)}, bf16[512,512]{1,0:T(8,128)(2,1)S(1)}, u32[]{:S(2)}, u32[]{:S(2)}) collective-permute-start(bf16[512,512]{1,0:T(8,128)(2,1)S(1)} %constant_dynamic-update-slice_fusion.10), channel_id=1, source_target_pairs={{0,4},{1,5},{2,6},{3,7},{4,0},{5,1},{6,2},{7,3},{8,12},{9,13},{10,... | collective-permute-start | bytes 1572872 | tf_op jit(solution)/shard_map/ppermute | solution.py:754
  203.3 11.5 %collective-permute-start.27 = (bf16[2048,512]{1,0:T(8,128)(2,1)S(1)}, bf16[2048,512]{1,0:T(8,128)(2,1)S(1)}, u32[]{:S(2)}, u32[]{:S(2)}) collective-permute-start(bf16[2048,512]{1,0:T(8,128)(2,1)S(1)} %constant_dynamic-update-slice_fusion.12.refs_0_), channel_id=1, source_target_pairs={{0,1},{1,0},{2,3},{3,2},{4,5},{5,4},{6,7},{7,6},{8,9},{9,8},{10,11... | collective-permute-start | bytes 6291464 | tf_op jit(solution)/shard_map/ppermute | solution.py:754
  203.4 10.1 %collective-permute-start.23 = (bf16[320,512]{1,0:T(8,128)(2,1)S(1)}, bf16[320,512]{1,0:T(8,128)(2,1)S(1)}, u32[]{:S(2)}, u32[]{:S(2)}) collective-permute-start(bf16[320,512]{1,0:T(8,128)(2,1)S(1)} %constant_dynamic-update-slice_fusion.6), channel_id=1, source_target_pairs={{0,2},{1,3},{2,0},{3,1},{4,6},{5,7},{6,4},{7,5},{8,10},{9,11},{10,... | collective-permute-start | bytes 983048 | tf_op jit(solution)/shard_map/ppermute | solution.py:754
  203.9 10.3 %collective-permute-start.22 = (bf16[192,512]{1,0:T(8,128)(2,1)S(1)}, bf16[192,512]{1,0:T(8,128)(2,1)S(1)}, u32[]{:S(2)}, u32[]{:S(2)}) collective-permute-start(bf16[192,512]{1,0:T(8,128)(2,1)S(1)} %constant_dynamic-update-slice_fusion.8), channel_id=1, source_target_pairs={{0,4},{1,5},{2,6},{3,7},{4,0},{5,1},{6,2},{7,3},{8,12},{9,13},{10,... | collective-permute-start | bytes 589832 | tf_op jit(solution)/shard_map/ppermute | solution.py:754
  213.6 16.4 %collective-permute-start.29 = (bf16[640,512]{1,0:T(8,128)(2,1)S(1)}, bf16[640,512]{1,0:T(8,128)(2,1)S(1)}, u32[]{:S(2)}, u32[]{:S(2)}) collective-permute-start(bf16[640,512]{1,0:T(8,128)(2,1)S(1)} %constant_dynamic-update-slice_fusion.16), channel_id=1, source_target_pairs={{0,4},{1,5},{2,6},{3,7},{4,0},{5,1},{6,2},{7,3},{8,12},{9,13},{10,... | collective-permute-start | bytes 1966088 | tf_op jit(solution)/shard_map/ppermute | solution.py:754
  214.2 10.5 %collective-permute-start.26 = (bf16[384,512]{1,0:T(8,128)(2,1)S(1)}, bf16[384,512]{1,0:T(8,128)(2,1)S(1)}, u32[]{:S(2)}, u32[]{:S(2)}) collective-permute-start(bf16[384,512]{1,0:T(8,128)(2,1)S(1)} %constant_dynamic-update-slice_fusion.18.refs_4_), channel_id=1, source_target_pairs={{0,2},{1,3},{2,0},{3,1},{4,6},{5,7},{6,4},{7,5},{8,10},{9,11},{10,... | collective-permute-start | bytes 1179656 | tf_op jit(solution)/shard_map/ppermute | solution.py:754
  (27 other events, 178.4 us)

commit v3 on v2

--- a/solution.py
+++ b/solution.py
@@ -62,6 +62,11 @@
 
 
 PARTS = 1
+CROSS_GROUP = 4
+FF_CHUNK = 512
+FF_ROWS = 512
+TOKEN_ROWS = 512
+FF_LIMIT = 36
 LAG = 1
 
 
@@ -240,12 +245,17 @@
         change[r, :] += dot(slope, w_expand[...], 1, 1)
 
     def fill(grads):
-        found = [dot(activated[...], grad_low[...], 0, 0), dot(act[...], grad_expanded[...], 0, 0)]
-        size = chunk // 4
-        turned = lax.rem(step, pl.num_programs(0) // 2) == 1
-        for n in range(8):
-            at = pl.ds(pl.multiple_of(place(bits, n, turned) * size, size), size)
-            grads[at, :] = found[n // 4][n % 4 * size : (n % 4 + 1) * size, :].astype(bf16)
+        unit = grad_low.shape[1]
+        size = unit // 4
+        contract = dot(activated[...], grad_low[...], 0, 0)
+        expand = dot(act[...], grad_expanded[...], 0, 0)
+        for k in range(chunk // unit):
+            found = [contract[k * unit : (k + 1) * unit, :], expand[:, k * unit : (k + 1) * unit]]
+            turned = lax.rem(step * (chunk // unit) + k, 2) == 1
+            for n in range(8):
+                at = k * 2 * unit + place(bits, n, turned) * size
+                at = pl.ds(pl.multiple_of(at, size), size)
+                grads[at, :] = found[n // 4][n % 4 * size : (n % 4 + 1) * size, :].astype(bf16)
 
     @pl.when(step < pl.num_programs(0) // 2)
     def _():
@@ -261,48 +271,76 @@
         grad_normed[...] = change[...].astype(bf16)
 
 
-def add_halves(total, n, value):
-    half = value.shape[0] // 2
-    rows = total.shape[0] // 2
-    total[n * half : (n + 1) * half, :] += value[:half]
-    total[rows + n * half : rows + (n + 1) * half, :] += value[half:]
-
-
-def give_halves(bits, total, send, keep, turned):
-    rows = send.shape[0]
-    size = rows // 8
-    for n in range(8):
-        to = pl.ds(pl.multiple_of(place(bits, n, turned) * size, size), size)
-        at = pl.ds(pl.multiple_of((1 - bits[0]) * rows + n * size, size), size)
-        send[to, :] = total[at, :].astype(bf16)
-        at = pl.ds(pl.multiple_of(bits[0] * rows + n * size, size), size)
-        keep[to, :] = total[at, :].astype(bf16)
+def give_rows(bits, start, low, high, send, keep, size, turned):
+    first = bits[0] == 0
+    for side, one, other in ((keep, low, high), (send, high, low)):
+        rows = jnp.where(first, one, other)
+        at, end = start, start + low.shape[0]
+        while at < end:
+            part = at // size
+            stop = min(end, (part + 1) * size)
+            to = place(bits, part, turned) * size + (at - part * size)
+            to = pl.ds(pl.multiple_of(to, 32), stop - at)
+            side[to, :] = rows[at - start : stop - start, :]
+            at = stop
 
 
 def cross_backward_kernel(
-    seqs, length, width, mem_total,
-    bits, grad_normed, late, grad_low, cross, weights, pairs, queries, mid, arrived, attended,
-    w_out, w_query, w_kv, gain_ffn, gain_cross,
+    length, mem_total,
+    bits, grad_normed_far, late_far, grad_low_far, cross_far, weights_far, pairs_far, queries_far, mid_far,
+    arrived_far, attended_far, w_out_far, w_query_far, w_kv_far, gain_ffn, gain_cross,
     gradient, grad_arrived, send, keep,
-    total, grad_rows,
+    grad_normed, late, grad_low, cross, weights, pairs, queries, mid,
+    arrived, attended, w_out, w_query, w_kv,
+    running, low_queries, out, low_pairs, arrival,
 ):
-    step = pl.program_id(0)
-
-    @pl.when(step == 0)
-    def _():
-        total[...] = jnp.zeros_like(total)
-
-    normal, spread = normalize(late[...].astype(f32))
-    change = norm_backward(
-        grad_normed[...].astype(f32), gain_ffn[...], normal, spread
-    )
-    running = grad_low[...].astype(f32) + change
-    low = running.astype(bf16)
-    add_halves(total, 0, dot(cross[...], low, 0, 0))
-    grad_cross = dot(low, w_out[...], 1, 1).astype(bf16)
+    rows, width = grad_normed.shape
+    seqs = rows // length
+    heads = width // HEAD
+    blocks = [slice(n * rows // 4, (n + 1) * rows // 4) for n in range(4)]
+    copies = []
+
+    def fetch(far, near):
+        copy = pltpu.make_async_copy(far, near, arrival.at[len(copies)])
+        copies.append(copy)
+        copy.start()
+        return copy
+
+    def fetch_rows(n):
+        return [
+            fetch(far.at[blocks[n], :], near.at[blocks[n], :])
+            for far, near in ((grad_normed_far, grad_normed), (late_far, late), (grad_low_far, grad_low))
+        ]
+
+    waiting = [fetch_rows(0), fetch_rows(1)]
+    copy_out = fetch(w_out_far, w_out)
     masks = wide_mask(mem_total, width)
     mask = jnp.concatenate(masks, axis=0).astype(bf16)
-    heads = width // HEAD
+    grad_cross = []
+    for n in range(4):
+        for copy in waiting[n]:
+            copy.wait()
+        if n < 2:
+            waiting.append(fetch_rows(n + 2))
+        if n == 1:
+            early = [fetch(weights_far, weights), fetch(pairs_far, pairs), fetch(queries_far, queries)]
+        if n == 2:
+            later = [fetch(w_query_far, w_query), fetch(mid_far, mid)]
+        if n == 3:
+            last = [
+                fetch(cross_far, cross), fetch(arrived_far, arrived), fetch(w_kv_far, w_kv),
+                fetch(attended_far, attended),
+            ]
+        normal, spread = normalize(late[blocks[n], :].astype(f32))
+        change = norm_backward(grad_normed[blocks[n], :].astype(f32), gain_ffn[...], normal, spread)
+        change = grad_low[blocks[n], :].astype(f32) + change
+        running[blocks[n], :] = change
+        low = change.astype(bf16)
+        grad_normed[blocks[n], :] = low
+        if n == 0:
+            copy_out.wait()
+        grad_cross.append(dot(low, w_out[...], 1, 1).astype(bf16))
+    grad_cross = jnp.concatenate(grad_cross, axis=0)
 
     def widen(s, at):
         return jnp.concatenate([pairs[s * mem_total : (s + 1) * mem_total, at]] * heads, axis=0) * mask
@@ -310,85 +348,124 @@
     def narrow(block):
         return sum(block[h * mem_total : (h + 1) * mem_total, :] * masks[h] for h in range(heads))
 
-    softs = [weights[s] for s in range(seqs)]
-    grads = [grad_cross[s * length : (s + 1) * length, :] for s in range(seqs)]
-    values = [dot(softs[s], grads[s]) for s in range(seqs)]
-    changes = [
-        dot(widen(s, slice(width, 2 * width)), grads[s], 1, 1).reshape(heads, mem_total, length)
-        for s in range(seqs)
-    ]
-    scores = []
-    for s in range(seqs):
-        soft = softs[s].astype(f32).reshape(heads, mem_total, length)
-        product = soft * changes[s]
-        score = product - soft * jnp.sum(product, axis=1, keepdims=True)
-        scores.append(score.reshape(heads * mem_total, length).astype(bf16))
-    low_q = [
-        (dot(scores[s], widen(s, slice(0, width)), 0, 0) * 0.125).astype(bf16) for s in range(seqs)
-    ]
-    keys = [dot(scores[s], queries[s * length : (s + 1) * length, :]) for s in range(seqs)]
-    low_q = jnp.concatenate(low_q, axis=0)
-    low_pairs = jnp.concatenate(
-        [
-            jnp.concatenate(
-                [(narrow(keys[s]) * 0.125).astype(bf16), narrow(values[s]).astype(bf16)], axis=1
-            )
-            for s in range(seqs)
-        ],
-        axis=0,
-    )
-    at = pl.ds(pl.multiple_of(step * seqs * mem_total, seqs * mem_total), seqs * mem_total)
-    grad_rows[at, :] = dot(low_pairs, w_kv[...], 1, 1).astype(bf16)
-    normal, spread = normalize(mid[...].astype(f32))
-    act = (normal * gain_cross[...]).astype(bf16)
-    add_halves(total, 1, dot(act, low_q, 0, 0))
-    add_halves(total, 2, dot(arrived[...], low_pairs[:, :width], 0, 0))
-    add_halves(total, 3, dot(arrived[...], low_pairs[:, width:], 0, 0))
-    change = norm_backward(
-        dot(low_q, w_query[...], 1, 1), gain_cross[...], normal, spread
-    )
-    running = running + change
-    gradient[...] = running.astype(bf16)
-    add_halves(total, 4, dot(attended[...], running.astype(bf16), 0, 0))
-
-    @pl.when(step == pl.num_programs(0) - 1)
-    def _():
-        give_halves(bits, total, send, keep, TURNED[0])
-        rows = grad_rows.shape[0]
-        block = min(rows, 512)
-        count = rows // mem_total
-        for start in range(0, rows, block):
-            row = lax.broadcasted_iota(jnp.int32, (block, rows), 0) + start
-            column = lax.broadcasted_iota(jnp.int32, (block, rows), 1)
-            shift = count.bit_length() - 1
-            source = (row & (count - 1)) * mem_total + (row >> shift)
-            order = jnp.where(column == source, 1.0, 0.0).astype(bf16)
-            grad_arrived[start : start + block, :] = dot(order, grad_rows[...]).astype(bf16)
+    for copy in early:
+        copy.wait()
+    for start in range(0, seqs, CROSS_GROUP):
+        group = range(start, start + CROSS_GROUP)
+        softs = [weights[s] for s in group]
+        grads = [grad_cross[s * length : (s + 1) * length, :] for s in group]
+        changes = [
+            dot(widen(s, slice(width, 2 * width)), grad, 1, 1).reshape(heads, mem_total, length)
+            for s, grad in zip(group, grads)
+        ]
+        values = [dot(soft, grad) for soft, grad in zip(softs, grads)]
+        scores = []
+        for soft, change in zip(softs, changes):
+            soft = soft.astype(f32).reshape(heads, mem_total, length)
+            product = soft * change
+            score = product - soft * jnp.sum(product, axis=1, keepdims=True)
+            scores.append(score.reshape(heads * mem_total, length).astype(bf16))
+        for s, score in zip(group, scores):
+            low_queries[s * length : (s + 1) * length, :] = (
+                dot(score, widen(s, slice(0, width)), 0, 0) * 0.125
+            ).astype(bf16)
+        keys = [
+            dot(score, queries[s * length : (s + 1) * length, :]) for s, score in zip(group, scores)
+        ]
+        for s, key, value in zip(group, keys, values):
+            at = slice(s * mem_total, (s + 1) * mem_total)
+            low_pairs[at, :width] = (narrow(key) * 0.125).astype(bf16)
+            low_pairs[at, width:] = narrow(value).astype(bf16)
+    for copy in later + last:
+        copy.wait()
+    half = width // 2
+
+    def give(n, left, right):
+        found = dot(left[...], right, 0, 0).astype(bf16)
+        size = send.shape[0] // 8
+        give_rows(bits, n * half, found[:half], found[half:], send, keep, size, TURNED[0])
+
+    give(0, cross, grad_normed[...])
+    sent = []
+    for n in range(4):
+        back = dot(low_queries[blocks[n], :], w_query[...], 1, 1)
+        normal, spread = normalize(mid[blocks[n], :].astype(f32))
+        mid[blocks[n], :] = (normal * gain_cross[...]).astype(bf16)
+        low = (running[blocks[n], :] + norm_backward(back, gain_cross[...], normal, spread)).astype(bf16)
+        out[blocks[n], :] = low
+        copy = pltpu.make_async_copy(
+            out.at[blocks[n], :], gradient.at[blocks[n], :], arrival.at[len(copies) + n]
+        )
+        copy.start()
+        sent.append(copy)
+    give(1, mid, low_queries[...])
+    give(2, arrived, low_pairs[:, :width])
+    give(3, arrived, low_pairs[:, width:])
+    give(4, attended, out[...])
+    grad_rows = dot(low_pairs[...], w_kv[...], 1, 1).astype(bf16)
+    count = seqs
+    total = grad_rows.shape[0]
+    block = min(total, 512)
+    for start in range(0, total, block):
+        row = lax.broadcasted_iota(jnp.int32, (block, total), 0) + start
+        column = lax.broadcasted_iota(jnp.int32, (block, total), 1)
+        shift = count.bit_length() - 1
+        source = (row & (count - 1)) * mem_total + (row >> shift)
+        order = jnp.where(column == source, 1.0, 0.0).astype(bf16)
+        grad_arrived[start : start + block, :] = dot(order, grad_rows).astype(bf16)
+    for copy in sent:
+        copy.wait()
 
 
 def self_backward_kernel(
-    seqs, length, width,
-    bits, gradient, triple, weights, act, w_out,
-    grad_triple, send, keep,
-    total,
+    length,
+    bits, gradient_far, triple_far, weights_far, act_far, w_out_far,
+    grad_triple_far, send, keep,
+    gradient, triple, weights, act, w_out, grad_triple, arrival,
 ):
-    step = pl.program_id(0)
-
-    @pl.when(step == 0)
-    def _():
-        total[...] = jnp.zeros_like(total)
-
-    low = dot(gradient[...], w_out[...], 1, 1).astype(bf16)
+    rows, width = gradient.shape
+    seqs = rows // length // 4
+    blocks = [slice(n * rows // 4, (n + 1) * rows // 4) for n in range(4)]
+    copies = []
+
+    def move(source, target):
+        copy = pltpu.make_async_copy(source, target, arrival.at[len(copies)])
+        copies.append(copy)
+        copy.start()
+        return copy
+
+    def fetch(n):
+        own = slice(n * seqs, (n + 1) * seqs)
+        return [
+            move(gradient_far.at[blocks[n], :], gradient.at[blocks[n], :]),
+            move(triple_far.at[blocks[n], :], triple.at[blocks[n], :]),
+            move(weights_far.at[own], weights.at[own]),
+        ]
+
+    ready = [move(w_out_far, w_out)]
+    waiting = [fetch(0), fetch(1)]
     first, second = head_masks(length)
-    heads = [(s, p) for s in range(seqs) for p in range(width // PAIR)]
-    for start in range(0, len(heads), GROUP):
+    sent = []
+    for n in range(4):
+        for copy in waiting[n] + ready:
+            copy.wait()
+        ready = []
+        if n < 2:
+            waiting.append(fetch(n + 2))
+        if n == 2:
+            late = move(act_far, act)
+        low = dot(gradient[blocks[n], :], w_out[...], 1, 1).astype(bf16)
         group = []
-        for s, p in heads[start : start + GROUP]:
-            rows = slice(s * length, (s + 1) * length)
-            group.append((s, p, rows, [slice(j * width + p * PAIR, j * width + (p + 1) * PAIR) for j in range(3)]))
-        grads = [spread_pair(low[rows, at[0]], first, second) for s, p, rows, at in group]
-        softs = [weights[s, p] for s, p, rows, at in group]
-        changes = [dot(triple[rows, at[2]], grad, 1, 1) for (s, p, rows, at), grad in zip(group, grads)]
+        for s in range(n * seqs, (n + 1) * seqs):
+            for p in range(width // PAIR):
+                at = [slice(j * width + p * PAIR, j * width + (p + 1) * PAIR) for j in range(3)]
+                group.append((s, p, slice(s * length, (s + 1) * length), at))
+        grads = [
+            spread_pair(low[(s - n * seqs) * length : (s + 1 - n * seqs) * length, at[0]], first, second)
+            for s, p, span, at in group
+        ]
+        softs = [weights[s, p] for s, p, span, at in group]
+        changes = [dot(triple[span, at[2]], grad, 1, 1) for (s, p, span, at), grad in zip(group, grads)]
         values = [dot(soft, grad).astype(bf16) for soft, grad in zip(softs, grads)]
         scores = []
         for soft, change in zip(softs, changes):
@@ -396,23 +473,25 @@
             product = soft * change
             scores.append((product - soft * jnp.sum(product, axis=0, keepdims=True)).astype(bf16))
         keys = [
-            dot(score, spread_pair(triple[rows, at[0]] * 0.125, first, second)).astype(bf16)
-            for (s, p, rows, at), score in zip(group, scores)
+            dot(score, spread_pair(triple[span, at[0]] * 0.125, first, second)).astype(bf16)
+            for (s, p, span, at), score in zip(group, scores)
         ]
         queries = [
-            (dot(stack_pair(score), spread_pair(triple[rows, at[1]], first, second), 0, 0) * 0.125).astype(bf16)
-            for (s, p, rows, at), score in zip(group, scores)
+            (dot(stack_pair(score), spread_pair(triple[span, at[1]], first, second), 0, 0) * 0.125).astype(bf16)
+            for (s, p, span, at), score in zip(group, scores)
         ]
-        for n, (s, p, rows, at) in enumerate(group):
-            grad_triple[rows, at[0]] = queries[n]
-            grad_triple[rows, at[1]] = keys[n]
-            grad_triple[rows, at[2]] = values[n]
+        for k, (s, p, span, at) in enumerate(group):
+            grad_triple[span, at[0]] = queries[k]
+            grad_triple[span, at[1]] = keys[k]
+            grad_triple[span, at[2]] = values[k]
+        sent.append(move(grad_triple.at[blocks[n], :], grad_triple_far.at[blocks[n], :]))
+    late.wait()
+    half = width // 2
     for j in range(3):
-        add_halves(total, j, dot(act[...], grad_triple[:, j * width : (j + 1) * width], 0, 0))
-
-    @pl.when(step == pl.num_programs(0) - 1)
-    def _():
-        give_halves(bits, total, send, keep, TURNED[1])
+        found = dot(act[...], grad_triple[:, j * width : (j + 1) * width], 0, 0).astype(bf16)
+        give_rows(bits, j * half, found[:half], found[half:], send, keep, send.shape[0] // 8, TURNED[1])
+    for copy in sent:
+        copy.wait()
 
 
 def grad_tokens_kernel(bits, gradient, grad_triple, tokens, w_qkv, gain_self, grad_tokens):
@@ -537,18 +616,17 @@
     "do ffn",
     "start cross",
     "do cross",
+    "do ffn",
     "memory",
     "self",
     "do ffn",
     "do cross",
     "start self",
     "do self",
+    "do cross",
     "do ffn",
     "do cross",
-    "tokens",
-    "do ffn",
     "do self",
-    "do cross",
     "do ffn",
     "do self",
     "do cross",
@@ -560,9 +638,10 @@
     "do ffn",
     "do cross",
     "do self",
-    "end ffn",
+    "tokens",
     "do self",
     "do cross",
+    "end ffn",
     "end self",
     "end cross",
 )
@@ -628,7 +707,7 @@
     )
 
 
-def feed_forward(bits, act, grad_low, start, w_expand, w_contract, chunk=512):
+def feed_forward(bits, act, grad_low, start, w_expand, w_contract, chunk=FF_CHUNK):
     rows, width = act.shape
     hidden = w_expand.shape[1]
     steps = hidden // chunk
@@ -641,7 +720,7 @@
         return pl.BlockSpec((2 * chunk, width), lambda i, bits: (place(i), 0))
 
     return call(
-        functools.partial(ffn_kernel, min(rows, 512)),
+        functools.partial(ffn_kernel, min(rows, FF_ROWS)),
         (steps,), bits,
         [
             (act, whole(rows, width)), (grad_low, whole(rows, width)), (start, whole(rows, width)),
@@ -661,72 +740,66 @@
             pltpu.VMEM((rows, width), f32),
         ],
         flops=12 * rows * width * hidden,
-        limit=32,
+        limit=FF_LIMIT,
     )
 
 
 def cross_backward(bits, grad_normed, late, grad_low, cross, weights, pairs, queries, mid, arrived, attended, w_out, w_query, w_kv, gain_ffn, gain_cross, length, mem_total, deps=()):
     rows, width = queries.shape
-    n = rows // length
-    block = SEQS * length
-    mem = SEQS * mem_total
-    heads = width // HEAD
-    row = by_step(block, width)
+    far = [
+        grad_normed, late, grad_low, cross, weights, pairs, queries, mid, arrived, attended,
+        w_out, w_query, w_kv,
+    ]
+    anywhere = pl.BlockSpec(memory_space=pl.ANY)
     return call(
-        functools.partial(cross_backward_kernel, SEQS, length, width, mem_total),
-        (n // SEQS,), bits,
-        [
-            (grad_normed, row, HBM), (late, row, HBM), (grad_low, row, HBM), (cross, row, HBM),
-            (weights, by_step(SEQS, heads * mem_total, length), HBM),
-            (pairs, by_step(mem, 2 * width), HBM), (queries, row, HBM), (mid, row, HBM),
-            (arrived, by_step(mem, width), HBM), (attended, row, HBM),
-            (w_out, whole(width, width), HBM), (w_query, whole(width, width), HBM),
-            (w_kv, whole(width, 2 * width), HBM),
-            (gain_ffn, whole(1, width)), (gain_cross, whole(1, width)),
-        ],
-        [
-            ((rows, width), bf16, row, HBM),
-            ((n * mem_total, width), bf16, whole(n * mem_total, width), HBM),
+        functools.partial(cross_backward_kernel, length, mem_total),
+        (1,), bits,
+        [(a, anywhere, HBM) for a in far]
+        + [(gain_ffn, whole(1, width)), (gain_cross, whole(1, width))],
+        [
+            ((rows, width), bf16, anywhere, HBM),
+            (arrived.shape, bf16, whole(*arrived.shape), HBM),
             ((5 * width // 2, width), bf16, whole(5 * width // 2, width), HBM),
             ((5 * width // 2, width), bf16, whole(5 * width // 2, width), HBM),
         ],
-        [
-            pltpu.VMEM((5 * width, width), f32),
-            pltpu.VMEM((n * mem_total, width), bf16),
+        [pltpu.VMEM(a.shape, bf16) for a in far]
+        + [
+            pltpu.VMEM((rows, width), f32),
+            pltpu.VMEM((rows, width), bf16),
+            pltpu.VMEM((rows, width), bf16),
+            pltpu.VMEM(pairs.shape, bf16),
+            pltpu.SemaphoreType.DMA((32,)),
         ],
         flops=14 * rows * width * width,
         deps=deps,
-        limit=40 if mem_total <= 32 else 56,
+        limit=48 if mem_total <= 32 else 62,
     )
 
 
 def self_backward(bits, gradient, triple, weights, act, w_out, length, deps=()):
     rows, width = gradient.shape
-    n = rows // length
-    block = SEQS * length
+    far = [gradient, triple, weights, act, w_out]
+    anywhere = pl.BlockSpec(memory_space=pl.ANY)
     return call(
-        functools.partial(self_backward_kernel, SEQS, length, width),
-        (n // SEQS,), bits,
-        [
-            (gradient, by_step(block, width), HBM), (triple, by_step(block, 3 * width), HBM),
-            (weights, by_step(SEQS, width // PAIR, length, 2 * length), HBM),
-            (act, by_step(block, width), HBM), (w_out, whole(width, width), HBM),
-        ],
-        [
-            ((rows, 3 * width), bf16, by_step(block, 3 * width), HBM),
+        functools.partial(self_backward_kernel, length),
+        (1,), bits,
+        [(a, anywhere, HBM) for a in far],
+        [
+            (triple.shape, bf16, anywhere, HBM),
             ((3 * width // 2, width), bf16, whole(3 * width // 2, width), HBM),
             ((3 * width // 2, width), bf16, whole(3 * width // 2, width), HBM),
         ],
-        [pltpu.VMEM((3 * width, width), f32)],
+        [pltpu.VMEM(a.shape, bf16) for a in far]
+        + [pltpu.VMEM(triple.shape, bf16), pltpu.SemaphoreType.DMA((24,))],
         flops=14 * rows * width * width,
-        limit=40,
         deps=deps,
+        limit=44,
     )
 
 
 def token_gradient(bits, gradient, grad_triple, tokens, w_qkv, gain_self, deps=()):
     rows, width = tokens.shape
-    block = 512
+    block = TOKEN_ROWS
     row = by_step(block, width)
     return call(
         grad_tokens_kernel, (rows // block,), bits,

time: 243 us -> 234 us (0.963); the launches traced: 242 us -> 229 us
  Pallas kernels: 123 us -> 117 us
  other arithmetic: 8.22 us -> 4.4 us
  starting transfers between devices: 45.8 us -> 43.1 us
    pallas_call x9, Pallas kernels: 123 us -> 117 us  [call(): pl.pallas_call(body, grid_spec=pltpu.PrefetchScalarGridSpec(num_scalar_pr...]
    convert_element_type x19, other arithmetic: 8.16 us -> 4.34 us  [added(): return (left.astype(f32) + right.astype(f32)).astype(bf16)]
    ppermute x31, starting transfers between devices: 34.4 us -> 31 us  [exchange(): lax.ppermute(block, 'dp', [(i, i ^ 1 << bit) for i in range(devices)])]
    unnamed x50 -> x52, local copies, waits for them, and re-layouts: 6.17 us -> 6.87 us
  transfers between devices with their start and end apart: 33 -> 33, of which waited for: 15 -> 16; matrix products, arithmetic and copies ran while one was open for 3% -> 2% of each run, Pallas kernels for 31% -> 29%
where the time goes in v3:
time: 234 us; the launch traced here: 229 us
  Pallas kernels  117 us (50%)
  waiting for transfers between devices  53.9 us (23%)
  starting transfers between devices  43.1 us (18%)
  local copies, waits for them, and re-layouts  9.05 us (4%)
  other arithmetic  4.4 us (2%)
    pallas_call x9, Pallas kernels, call(): pl.pallas_call(body, grid_spec=pltpu.PrefetchScalarGridSpec(num_scalar_pr...  117 us
    ppermute x31, waiting for transfers between devices, exchange(): lax.ppermute(block, 'dp', [(i, i ^ 1 << bit) for i in range(devices)])  53.9 us
    ppermute x31, starting transfers between devices, exchange(): lax.ppermute(block, 'dp', [(i, i ^ 1 << bit) for i in range(devices)])  31 us
    all_to_all x1, starting transfers between devices, local(): lax.all_to_all(memory.reshape(devices, -1, width), 'dp', split_axis=0, co...  7.3 us
    unnamed x52, local copies, waits for them, and re-layouts  6.87 us
    all_to_all x1, starting transfers between devices, local(): lax.all_to_all(after((grad_arrived,), deps)[0].reshape(devices, -1, width...  4.76 us
  transfers between devices with their start and end apart: 33, of which 16 were waited for; matrix products, arithmetic and copies ran while one was open for 2% of the time, Pallas kernels for 29%

profile of v3, /device:TPU:0, one launch (start us, length us, event | category | flops | bytes accessed | tf_op | source)
XLA Modules:
  0.0 229.1 jit_solution(14112721397927238724)
XLA Ops:
  0.6 7.3 %all-to-all-start = ((bf16[32,16,512]{2,1,0:T(8,128)(2,1)}), bf16[32,16,512]{2,1,0:T(8,128)(2,1)S(1)}, u32[]{:S(2)}, u32[]{:S(2)}) async-start(bf16[32,16,512]{2,1,0:T(8,128)(2,1)} %bitcast.34), calls=%async_computation | async-start | bytes 1048576 | tf_op jit(solution)/shard_map/all_to_all | solution.py:957
  10.1 15.7 %shard_map.246 = (bf16[2048,512]{1,0:T(8,128)(2,1)}, bf16[2048,1536]{1,0:T(8,128)(2,1)}, bf16[16,4,128,256]{3,2,1,0:T(8,128)(2,1)}, bf16[2048,512]{1,0:T(8,128)(...) custom-call(s32[5]{0:T(128)S(1)} %stack.23.bits_ref, s32[16]{0:T(128)S(1)} %copy-done.13, ...), custom_call_target="tpu_custom_call" | custom-call | flops 6442450944 | bytes 23597120 | tf_op jit(solution)/shard_map/pallas_call | solution.py:583
  27.1 10.7 %shard_map.247 = (bf16[512,512]{1,0:T(8,128)(2,1)}, bf16[512,1024]{1,0:T(8,128)(2,1)}, bf16[16,256,128]{2,1,0:T(8,128)(2,1)}, bf16[2048,512]{1,0:T(8,128)(2,1)},...) custom-call(s32[5]{0:T(128)S(1)} %stack.23.bits_ref, ...), custom_call_target="tpu_custom_call" | custom-call | flops 3221225472 | bytes 23595136 | tf_op jit(solution)/shard_map/pallas_call | solution.py:583
  37.7 36.2 %shard_map.248 = (bf16[2048,512]{1,0:T(8,128)(2,1)}, bf16[2048,512]{1,0:T(8,128)(2,1)}, bf16[2048,512]{1,0:T(8,128)(2,1)}, bf16[2048,512]{1,0:T(8,128)(2,1)}) custom-call(s32[5]{0:T(128)S(1)} %stack.23.bits_ref, bf16[2048,512]{1,0:T(8,128)(2,1)S(1)} %get-tuple-element.118.refs_0_, bf16[2048,512]{1,0:T(8,128)(2,1)S(1)} %get-tuple-element.119.refs_1_, ...), custom_call_target="tpu_custom_call" | custom-call | flops 25769803776 | bytes 18874368 | tf_op jit(solution)/shard_map/pallas_call | solution.py:583
  75.9 2.4 %collective-permute-done = bf16[2048,512]{1,0:T(8,128)(2,1)S(1)} collective-permute-done((bf16[2048,512]{1,0:T(8,128)(2,1)}, bf16[2048,512]{1,0:T(8,128)(2,1)S(1)}, u32[]{:S(2)}, u32[]{:S(2)}) %collective-permute-start) | collective-permute-done | bytes 2097184 | tf_op jit(solution)/shard_map/ppermute | solution.py:827
  82.5 19.2 %shard_map.249 = (bf16[2048,512]{1,0:T(8,128)(2,1)}, bf16[512,512]{1,0:T(8,128)(2,1)}, bf16[1280,512]{1,0:T(8,128)(2,1)}, bf16[1280,512]{1,0:T(8,128)(2,1)}) custom-call(s32[5]{0:T(128)S(1)} %stack.23.bits_ref, bf16[2048,512]{1,0:T(8,128)(2,1)} %get-tuple-element.122.refs_0_, bf16[2048,512]{1,0:T(8,128)(2,1)} %get-tuple-element.123.refs_1_, ...), custom_call_target="tpu_custom_call" | custom-call | flops 7516192768 | bytes 24645632 | tf_op jit(solution)/shard_map/pallas_call | solution.py:583
  103.1 2.1 collective-permute-done.5
  106.5 4.2 %collective-permute-done.3 = bf16[256,512]{1,0:T(8,128)(2,1)S(1)} collective-permute-done((bf16[256,512]{1,0:T(8,128)(2,1)S(1)}, bf16[256,512]{1,0:T(8,128)(2,1)S(1)}, u32[]{:S(2)}, u32[]{:S(2)}) %collective-permute-start.3) | collective-permute-done | bytes 262176 | tf_op jit(solution)/shard_map/ppermute | solution.py:827
  111.4 4.8 %all-to-all-start.1 = ((bf16[32,16,512]{2,1,0:T(8,128)(2,1)}), bf16[32,16,512]{2,1,0:T(8,128)(2,1)}, u32[]{:S(2)}, u32[]{:S(2)}) async-start(bf16[32,16,512]{2,1,0:T(8,128)(2,1)} %bitcast.35), calls=%async_computation.1 | async-start | bytes 1048576 | tf_op jit(solution)/shard_map/all_to_all | solution.py:1002
  119.4 15.2 %shard_map.250 = (bf16[2048,1536]{1,0:T(8,128)(2,1)}, bf16[768,512]{1,0:T(8,128)(2,1)}, bf16[768,512]{1,0:T(8,128)(2,1)}) custom-call(s32[5]{0:T(128)S(1)} %stack.23.bits_ref, bf16[2048,512]{1,0:T(8,128)(2,1)} %get-tuple-element.134.refs_0_, bf16[2048,1536]{1,0:T(8,128)(2,1)} %get-tuple-element.135.refs_1_, ...), custom_call_target="tpu_custom_call" | custom-call | flops 7516192768 | bytes 23068672 | tf_op jit(solution)/shard_map/pallas_call | solution.py:583
  134.7 4.3 %collective-permute-done.6 = bf16[640,512]{1,0:T(8,128)(2,1)} collective-permute-done((bf16[640,512]{1,0:T(8,128)(2,1)}, bf16[640,512]{1,0:T(8,128)(2,1)}, u32[]{:S(2)}, u32[]{:S(2)}) %collective-permute-start.6) | collective-permute-done | bytes 655392 | tf_op jit(solution)/shard_map/ppermute | solution.py:827
  140.4 2.5 %collective-permute-start.12 = (bf16[256,512]{1,0:T(8,128)(2,1)S(1)}, bf16[256,512]{1,0:T(8,128)(2,1)S(1)}, u32[]{:S(2)}, u32[]{:S(2)}) collective-permute-start(bf16[256,512]{1,0:T(8,128)(2,1)S(1)} %pad_maximum_fusion.1), channel_id=1, source_target_pairs={{0,16},{1,17},{2,18},{3,19},{4,20},{5,21},{6,22},{7,23},{8,24},{9,... | collective-permute-start | bytes 786440 | tf_op jit(solution)/shard_map/ppermute | solution.py:827
  143.9 11.7 %collective-permute-done.12 = bf16[256,512]{1,0:T(8,128)(2,1)S(1)} collective-permute-done((bf16[256,512]{1,0:T(8,128)(2,1)S(1)}, bf16[256,512]{1,0:T(8,128)(2,1)S(1)}, u32[]{:S(2)}, u32[]{:S(2)}) %collective-permute-start.12) | collective-permute-done | bytes 262176 | tf_op jit(solution)/shard_map/ppermute | solution.py:827
  159.3 3.8 %collective-permute-done.11 = bf16[160,512]{1,0:T(8,128)(2,1)S(1)} collective-permute-done((bf16[160,512]{1,0:T(8,128)(2,1)S(1)}, bf16[160,512]{1,0:T(8,128)(2,1)S(1)}, u32[]{:S(2)}, u32[]{:S(2)}) %collective-permute-start.11) | collective-permute-done | bytes 163872 | tf_op jit(solution)/shard_map/ppermute | solution.py:827
  164.8 5.6 %collective-permute-done.14 = bf16[256,512]{1,0:T(8,128)(2,1)S(1)} collective-permute-done((bf16[256,512]{1,0:T(8,128)(2,1)S(1)}, bf16[256,512]{1,0:T(8,128)(2,1)S(1)}, u32[]{:S(2)}, u32[]{:S(2)}) %collective-permute-start.14) | collective-permute-done | bytes 262176 | tf_op jit(solution)/shard_map/ppermute | solution.py:827
  174.4 3.6 %collective-permute-done.13 = bf16[192,512]{1,0:T(8,128)(2,1)S(1)} collective-permute-done((bf16[192,512]{1,0:T(8,128)(2,1)S(1)}, bf16[192,512]{1,0:T(8,128)(2,1)S(1)}, u32[]{:S(2)}, u32[]{:S(2)}) %collective-permute-start.13) | collective-permute-done | bytes 196640 | tf_op jit(solution)/shard_map/ppermute | solution.py:827
  178.2 2.1 collective-permute-start.20
  185.6 4.5 %collective-permute-done.19 = bf16[96,512]{1,0:T(8,128)(2,1)S(1)} collective-permute-done((bf16[96,512]{1,0:T(8,128)(2,1)S(1)}, bf16[96,512]{1,0:T(8,128)(2,1)S(1)}, u32[]{:S(2)}, u32[]{:S(2)}) %collective-permute-start.19) | collective-permute-done | bytes 98336 | tf_op jit(solution)/shard_map/ppermute | solution.py:827
  191.0 3.8 %collective-permute-done.21 = bf16[96,512]{1,0:T(8,128)(2,1)S(1)} collective-permute-done((bf16[96,512]{1,0:T(8,128)(2,1)S(1)}, bf16[96,512]{1,0:T(8,128)(2,1)S(1)}, u32[]{:S(2)}, u32[]{:S(2)}) %collective-permute-start.21) | collective-permute-done | bytes 98336 | tf_op jit(solution)/shard_map/ppermute | solution.py:827
  197.7 3.8 %collective-permute-done.23 = bf16[320,512]{1,0:T(8,128)(2,1)S(1)} collective-permute-done((bf16[320,512]{1,0:T(8,128)(2,1)S(1)}, bf16[320,512]{1,0:T(8,128)(2,1)S(1)}, u32[]{:S(2)}, u32[]{:S(2)}) %collective-permute-start.23) | collective-permute-done | bytes 327712 | tf_op jit(solution)/shard_map/ppermute | solution.py:827
  203.4 10.0 %shard_map.251 = bf16[2048,512]{1,0:T(8,128)(2,1)} custom-call(s32[5]{0:T(128)S(1)} %stack.23.bits_ref, bf16[2048,512]{1,0:T(8,128)(2,1)} %get-tuple-element.134.refs_0_, bf16[2048,1536]{1,0:T(8,128)(2,1)} %get-tuple-element.153.refs_1_, bf16[2048,512]{1,0:T(8,128)(2,1)} %bitcast.32, bf16[512,1536]{1,0:T(8,128)(2,1)} %refs_2_.4, f32[1,512]{1,0:T(1,128)S(1)} %bitcast.21, ...), custom_call_target="tpu_custom_call" | custom-call | flops 3221225472 | bytes 14157824 | tf_op jit(solution)/shard_map/pallas_call | solution.py:583
  215.3 4.6 %shard_map.252 = (f32[2048,512]{1,0:T(8,128)}, f32[512,2048]{1,0:T(8,128)}, f32[1,512]{1,0:T(1,128)}) custom-call(s32[5]{0:T(128)S(1)} %stack.23.bits_ref, bf16[2048,512]{1,0:T(8,128)(2,1)S(1)} %constant_dynamic-update-slice_fusion.12.refs_0_, bf16[2048,512]{1,0:T(8,128)(2,1)S(1)} %collective-permute-done.28.refs_1_, bf16[512,2048]{1,0:T(8,128)(2,1)S(1)} %copy-done.1, ...), custom_call_target="tpu_custom_call" | custom-call | bytes 14684160 | tf_op jit(solution)/shard_map/pallas_call | solution.py:583
  220.6 2.5 %shard_map.253 = (f32[512,1536]{1,0:T(8,128)}, f32[1,512]{1,0:T(1,128)}) custom-call(s32[5]{0:T(128)S(1)} %stack.23.bits_ref, bf16[768,512]{1,0:T(8,128)(2,1)S(1)} %constant_dynamic-update-slice_fusion.20.refs_0_, bf16[768,512]{1,0:T(8,128)(2,1)S(1)} %collective-permute-done.27.refs_1_, bf16[512,1536]{1,0:T(8,128)(2,1)S(1)} %copy-done, ...), custom_call_target="tpu_custom_call" | custom-call | bytes 6295552 | tf_op jit(solution)/shard_map/pallas_call | solution.py:583
  223.8 3.1 %shard_map.254 = (f32[512,512]{1,0:T(8,128)}, f32[512,512]{1,0:T(8,128)}, f32[512,1024]{1,0:T(8,128)}, f32[512,512]{1,0:T(8,128)}, f32[1,512]{1,0:T(1,128)}) custom-call(s32[5]{0:T(128)S(1)} %stack.23.bits_ref, bf16[1280,512]{1,0:T(8,128)(2,1)S(1)} %constant_dynamic-update-slice_fusion.22.refs_4_.refs_0_, ...), custom_call_target="tpu_custom_call" | custom-call | bytes 8392704 | tf_op jit(solution)/shard_map/pallas_call | solution.py:583
  (142 shorter events, 43.9 us)
Async XLA Ops:
  0.6 25.1 %all-to-all-start = ((bf16[32,16,512]{2,1,0:T(8,128)(2,1)}), bf16[32,16,512]{2,1,0:T(8,128)(2,1)S(1)}, u32[]{:S(2)}, u32[]{:S(2)}) async-start(bf16[32,16,512]{2,1,0:T(8,128)(2,1)} %bitcast.34), calls=%async_computation | async-start | bytes 1048576 | tf_op jit(solution)/shard_map/all_to_all | solution.py:957
  78.8 22.9 %collective-permute-start.1 = (bf16[512,512]{1,0:T(8,128)(2,1)S(1)}, bf16[512,512]{1,0:T(8,128)(2,1)S(1)}, u32[]{:S(2)}, u32[]{:S(2)}) collective-permute-start(bf16[512,512]{1,0:T(8,128)(2,1)S(1)} %get-tuple-element.224.refs_15_), channel_id=1, source_target_pairs={{0,2},{1,3},{2,0},{3,1},{4,6},{5,7},{6,4},{7,5},{8,10},{9,11},{10,... | collective-permute-start | bytes 1572872 | tf_op jit(solution)/shard_map/ppermute | solution.py:827
  81.0 20.8 %collective-permute-start.2 = (bf16[512,512]{1,0:T(8,128)(2,1)S(1)}, bf16[512,512]{1,0:T(8,128)(2,1)S(1)}, u32[]{:S(2)}, u32[]{:S(2)}) collective-permute-start(bf16[512,512]{1,0:T(8,128)(2,1)S(1)} %get-tuple-element.221), channel_id=1, source_target_pairs={{0,4},{1,5},{2,6},{3,7},{4,0},{5,1},{6,2},{7,3},{8,12},{9,13},{10,... | collective-permute-start | bytes 1572872 | tf_op jit(solution)/shard_map/ppermute | solution.py:827
  102.0 8.7 %collective-permute-start.3 = (bf16[256,512]{1,0:T(8,128)(2,1)S(1)}, bf16[256,512]{1,0:T(8,128)(2,1)S(1)}, u32[]{:S(2)}, u32[]{:S(2)}) collective-permute-start(bf16[256,512]{1,0:T(8,128)(2,1)S(1)} %get-tuple-element.235), channel_id=1, source_target_pairs={{0,4},{1,5},{2,6},{3,7},{4,0},{5,1},{6,2},{7,3},{8,12},{9,13},{10,... | collective-permute-start | bytes 786440 | tf_op jit(solution)/shard_map/ppermute | solution.py:827
  102.7 8.4 %collective-permute-start.4 = (bf16[256,512]{1,0:T(8,128)(2,1)S(1)}, bf16[256,512]{1,0:T(8,128)(2,1)S(1)}, u32[]{:S(2)}, u32[]{:S(2)}) collective-permute-start(bf16[256,512]{1,0:T(8,128)(2,1)S(1)} %get-tuple-element.233), channel_id=1, source_target_pairs={{0,2},{1,3},{2,0},{3,1},{4,6},{5,7},{6,4},{7,5},{8,10},{9,11},{10,... | collective-permute-start | bytes 786440 | tf_op jit(solution)/shard_map/ppermute | solution.py:827
  111.4 23.2 %all-to-all-start.1 = ((bf16[32,16,512]{2,1,0:T(8,128)(2,1)}), bf16[32,16,512]{2,1,0:T(8,128)(2,1)}, u32[]{:S(2)}, u32[]{:S(2)}) async-start(bf16[32,16,512]{2,1,0:T(8,128)(2,1)} %bitcast.35), calls=%async_computation.1 | async-start | bytes 1048576 | tf_op jit(solution)/shard_map/all_to_all | solution.py:1002
  116.1 18.4 %collective-permute-start.7 = (bf16[256,512]{1,0:T(8,128)(2,1)S(1)}, bf16[256,512]{1,0:T(8,128)(2,1)S(1)}, u32[]{:S(2)}, u32[]{:S(2)}) collective-permute-start(bf16[256,512]{1,0:T(8,128)(2,1)S(1)} %pad_maximum_fusion.refs_5_), channel_id=1, source_target_pairs={{0,8},{1,9},{2,10},{3,11},{4,12},{5,13},{6,14},{7,15},{8,0},{9,1},... | collective-permute-start | bytes 786440 | tf_op jit(solution)/shard_map/ppermute | solution.py:827
  117.9 21.1 %collective-permute-start.6 = (bf16[640,512]{1,0:T(8,128)(2,1)}, bf16[640,512]{1,0:T(8,128)(2,1)}, u32[]{:S(2)}, u32[]{:S(2)}) collective-permute-start(bf16[640,512]{1,0:T(8,128)(2,1)} %get-tuple-element.220), channel_id=1, source_target_pairs={{0,4},{1,5},{2,6},{3,7},{4,0},{5,1},{6,2},{7,3},{8,12},{9,13},{10,... | collective-permute-start | bytes 1966088 | tf_op jit(solution)/shard_map/ppermute | solution.py:827
  140.3 15.3 %collective-permute-start.8 = (bf16[768,512]{1,0:T(8,128)(2,1)S(1)}, bf16[768,512]{1,0:T(8,128)(2,1)S(1)}, u32[]{:S(2)}, u32[]{:S(2)}) collective-permute-start(bf16[768,512]{1,0:T(8,128)(2,1)S(1)} %copy-done.18), channel_id=1, source_target_pairs={{0,1},{1,0},{2,3},{3,2},{4,5},{5,4},{6,7},{7,6},{8,9},{9,8},{10,11... | collective-permute-start | bytes 2359304 | tf_op jit(solution)/shard_map/ppermute | solution.py:827
  140.4 15.2 %collective-permute-start.12 = (bf16[256,512]{1,0:T(8,128)(2,1)S(1)}, bf16[256,512]{1,0:T(8,128)(2,1)S(1)}, u32[]{:S(2)}, u32[]{:S(2)}) collective-permute-start(bf16[256,512]{1,0:T(8,128)(2,1)S(1)} %pad_maximum_fusion.1), channel_id=1, source_target_pairs={{0,16},{1,17},{2,18},{3,19},{4,20},{5,21},{6,22},{7,23},{8,24},{9,... | collective-permute-start | bytes 786440 | tf_op jit(solution)/shard_map/ppermute | solution.py:827
  142.8 13.1 %collective-permute-start.10 = (bf16[320,512]{1,0:T(8,128)(2,1)S(1)}, bf16[320,512]{1,0:T(8,128)(2,1)S(1)}, u32[]{:S(2)}, u32[]{:S(2)}) collective-permute-start(bf16[320,512]{1,0:T(8,128)(2,1)S(1)} %get-tuple-element.232), channel_id=1, source_target_pairs={{0,2},{1,3},{2,0},{3,1},{4,6},{5,7},{6,4},{7,5},{8,10},{9,11},{10,... | collective-permute-start | bytes 983048 | tf_op jit(solution)/shard_map/ppermute | solution.py:827
  156.3 14.0 %collective-permute-start.14 = (bf16[256,512]{1,0:T(8,128)(2,1)S(1)}, bf16[256,512]{1,0:T(8,128)(2,1)S(1)}, u32[]{:S(2)}, u32[]{:S(2)}) collective-permute-start(bf16[256,512]{1,0:T(8,128)(2,1)S(1)} %pad_maximum_fusion.2), channel_id=1, source_target_pairs={{0,8},{1,9},{2,10},{3,11},{4,12},{5,13},{6,14},{7,15},{8,0},{9,1},... | collective-permute-start | bytes 786440 | tf_op jit(solution)/shard_map/ppermute | solution.py:827
  158.3 12.1 %collective-permute-start.9 = (bf16[384,512]{1,0:T(8,128)(2,1)S(1)}, bf16[384,512]{1,0:T(8,128)(2,1)S(1)}, u32[]{:S(2)}, u32[]{:S(2)}) collective-permute-start(bf16[384,512]{1,0:T(8,128)(2,1)S(1)} %get-tuple-element.229), channel_id=1, source_target_pairs={{0,2},{1,3},{2,0},{3,1},{4,6},{5,7},{6,4},{7,5},{8,10},{9,11},{10,... | collective-permute-start | bytes 1179656 | tf_op jit(solution)/shard_map/ppermute | solution.py:827
  163.2 14.9 %collective-permute-start.18 = (bf16[160,512]{1,0:T(8,128)(2,1)S(1)}, bf16[160,512]{1,0:T(8,128)(2,1)S(1)}, u32[]{:S(2)}, u32[]{:S(2)}) collective-permute-start(bf16[160,512]{1,0:T(8,128)(2,1)S(1)} %add_convert_fusion.17), channel_id=1, source_target_pairs={{0,16},{1,17},{2,18},{3,19},{4,20},{5,21},{6,22},{7,23},{8,24},{9,... | collective-permute-start | bytes 491528 | tf_op jit(solution)/shard_map/ppermute | solution.py:827
  170.5 7.5 %collective-permute-start.13 = (bf16[192,512]{1,0:T(8,128)(2,1)S(1)}, bf16[192,512]{1,0:T(8,128)(2,1)S(1)}, u32[]{:S(2)}, u32[]{:S(2)}) collective-permute-start(bf16[192,512]{1,0:T(8,128)(2,1)S(1)} %get-tuple-element.237), channel_id=1, source_target_pairs={{0,4},{1,5},{2,6},{3,7},{4,0},{5,1},{6,2},{7,3},{8,12},{9,13},{10,... | collective-permute-start | bytes 589832 | tf_op jit(solution)/shard_map/ppermute | solution.py:827
  171.1 9.1 %collective-permute-start.17 = (bf16[256,512]{1,0:T(8,128)(2,1)S(1)}, bf16[256,512]{1,0:T(8,128)(2,1)S(1)}, u32[]{:S(2)}, u32[]{:S(2)}) collective-permute-start(bf16[256,512]{1,0:T(8,128)(2,1)S(1)} %constant_dynamic-update-slice_fusion.2), channel_id=1, source_target_pairs={{0,2},{1,3},{2,0},{3,1},{4,6},{5,7},{6,4},{7,5},{8,10},{9,11},{10,... | collective-permute-start | bytes 786440 | tf_op jit(solution)/shard_map/ppermute | solution.py:827
  172.5 8.3 %collective-permute-start.16 = (bf16[256,512]{1,0:T(8,128)(2,1)S(1)}, bf16[256,512]{1,0:T(8,128)(2,1)S(1)}, u32[]{:S(2)}, u32[]{:S(2)}) collective-permute-start(bf16[256,512]{1,0:T(8,128)(2,1)S(1)} %constant_dynamic-update-slice_fusion), channel_id=1, source_target_pairs={{0,4},{1,5},{2,6},{3,7},{4,0},{5,1},{6,2},{7,3},{8,12},{9,13},{10,... | collective-permute-start | bytes 786440 | tf_op jit(solution)/shard_map/ppermute | solution.py:827
  180.9 15.7 %collective-permute-start.25 = (bf16[512,512]{1,0:T(8,128)(2,1)S(1)}, bf16[512,512]{1,0:T(8,128)(2,1)S(1)}, u32[]{:S(2)}, u32[]{:S(2)}) collective-permute-start(bf16[512,512]{1,0:T(8,128)(2,1)S(1)} %constant_dynamic-update-slice_fusion.10), channel_id=1, source_target_pairs={{0,4},{1,5},{2,6},{3,7},{4,0},{5,1},{6,2},{7,3},{8,12},{9,13},{10,... | collective-permute-start | bytes 1572872 | tf_op jit(solution)/shard_map/ppermute | solution.py:827
  182.6 14.9 %collective-permute-start.24 = (bf16[512,512]{1,0:T(8,128)(2,1)S(1)}, bf16[512,512]{1,0:T(8,128)(2,1)S(1)}, u32[]{:S(2)}, u32[]{:S(2)}) collective-permute-start(bf16[512,512]{1,0:T(8,128)(2,1)S(1)} %constant_dynamic-update-slice_fusion.4), channel_id=1, source_target_pairs={{0,2},{1,3},{2,0},{3,1},{4,6},{5,7},{6,4},{7,5},{8,10},{9,11},{10,... | collective-permute-start | bytes 1572872 | tf_op jit(solution)/shard_map/ppermute | solution.py:827
  190.2 11.3 %collective-permute-start.23 = (bf16[320,512]{1,0:T(8,128)(2,1)S(1)}, bf16[320,512]{1,0:T(8,128)(2,1)S(1)}, u32[]{:S(2)}, u32[]{:S(2)}) collective-permute-start(bf16[320,512]{1,0:T(8,128)(2,1)S(1)} %constant_dynamic-update-slice_fusion.6), channel_id=1, source_target_pairs={{0,2},{1,3},{2,0},{3,1},{4,6},{5,7},{6,4},{7,5},{8,10},{9,11},{10,... | collective-permute-start | bytes 983048 | tf_op jit(solution)/shard_map/ppermute | solution.py:827
  201.6 13.1 %collective-permute-start.29 = (bf16[640,512]{1,0:T(8,128)(2,1)S(1)}, bf16[640,512]{1,0:T(8,128)(2,1)S(1)}, u32[]{:S(2)}, u32[]{:S(2)}) collective-permute-start(bf16[640,512]{1,0:T(8,128)(2,1)S(1)} %constant_dynamic-update-slice_fusion.16), channel_id=1, source_target_pairs={{0,4},{1,5},{2,6},{3,7},{4,0},{5,1},{6,2},{7,3},{8,12},{9,13},{10,... | collective-permute-start | bytes 1966088 | tf_op jit(solution)/shard_map/ppermute | solution.py:827
  201.7 11.7 %collective-permute-start.26 = (bf16[384,512]{1,0:T(8,128)(2,1)S(1)}, bf16[384,512]{1,0:T(8,128)(2,1)S(1)}, u32[]{:S(2)}, u32[]{:S(2)}) collective-permute-start(bf16[384,512]{1,0:T(8,128)(2,1)S(1)} %constant_dynamic-update-slice_fusion.18.refs_5_), channel_id=1, source_target_pairs={{0,2},{1,3},{2,0},{3,1},{4,6},{5,7},{6,4},{7,5},{8,10},{9,11},{10,... | collective-permute-start | bytes 1179656 | tf_op jit(solution)/shard_map/ppermute | solution.py:827
  203.3 12.0 %collective-permute-start.28 = (bf16[2048,512]{1,0:T(8,128)(2,1)S(1)}, bf16[2048,512]{1,0:T(8,128)(2,1)S(1)}, u32[]{:S(2)}, u32[]{:S(2)}) collective-permute-start(bf16[2048,512]{1,0:T(8,128)(2,1)S(1)} %constant_dynamic-update-slice_fusion.12.refs_0_), channel_id=1, source_target_pairs={{0,1},{1,0},{2,3},{3,2},{4,5},{5,4},{6,7},{7,6},{8,9},{9,8},{10,11... | collective-permute-start | bytes 6291464 | tf_op jit(solution)/shard_map/ppermute | solution.py:827
  214.7 8.4 %collective-permute-start.30 = (bf16[1280,512]{1,0:T(8,128)(2,1)S(1)}, bf16[1280,512]{1,0:T(8,128)(2,1)S(1)}, u32[]{:S(2)}, u32[]{:S(2)}) collective-permute-start(bf16[1280,512]{1,0:T(8,128)(2,1)S(1)} %constant_dynamic-update-slice_fusion.22.refs_4_.refs_0_), channel_id=1, source_target_pairs={{0,1},{1,0},{2,3},{3,2},{4,5},{5,4},{6,7},{7,6},{8,9},{9,8},{10,11... | collective-permute-start | bytes 3932168 | tf_op jit(solution)/shard_map/ppermute | solution.py:827
  (28 other events, 187.9 us)
